TPU v7x, 32 devices: a whole 2x2x4 slice. The times are simulated.
32 devices in a mesh: slab: 16 (over z, y, x), col: 2 (over core).
Axes of the slice: x: 2, y: 2, z: 4, core: 2. Of those that a mesh axis runs over, the one named last changes fastest.
Arguments:
- coupling: float32 [16, 512, 512], P('slab', None, 'col'), as said below
- tile_pattern: int32 [16, 4, 4], P('slab', None, 'col'), may hold values from 0 to 1, as said below
- orbital_mass: float32 [16, 512], P('slab', 'col'), may hold values from 0.0001 to 0.05
- sources: float32 [16, 512, 256], P('slab', None, 'col'), may hold values from -0.3 to 0.3
Outputs:
- solution: float32 [16, 512, 256], P('slab', None, 'col')
Inputs may be any that keep to these rules, and one draw needn't show every extreme that they name: Each coupling block is symmetric and positive semidefinite. `tile_pattern`: in each slab every tile belongs to one group, and two tiles are linked exactly when they share a group, so each pattern is symmetric with ones on its diagonal.
All inputs are finite; a program needn't handle non-finite values.
Results may differ from a plain program's by a relative error of at most 0.0003.
Values sent between devices are 32-bit elements; how exact they have to be, the bound alone decides.
No kernel may reach another device: no remote copies, remote signals or barrier semaphores. Data moves between devices by JAX's collectives and lax.ppermute only.
A program may use at most 128 MiB of HBM per device.

v0:
```python
import functools
import math

import jax
import jax.numpy as jnp
from jax import lax
from jax.experimental import pallas as pl
from jax.experimental.pallas import tpu as pltpu
from jax.sharding import Mesh
from jax.sharding import PartitionSpec as P

MEMBERS = 4
SPARE_BYTES = 16 * 1024 * 1024

LEAF = 128
PANEL = 32
GROUP = 8


def split(x):
    high = x.astype(jnp.bfloat16)
    low = (x - high.astype(jnp.float32)).astype(jnp.bfloat16)
    return high, low


def dot_split(a, b):
    (ah, al), (bh, bl) = a, b
    mul = functools.partial(jnp.dot, preferred_element_type=jnp.float32)
    return mul(ah, bh) + (mul(ah, bl) + mul(al, bh))


def dot3(a, b):
    return dot_split(split(a), split(b))


def leaf_inverse(blocks, background=()):
    shape = (GROUP, LEAF)
    lane = lax.broadcasted_iota(jnp.int32, shape, 1)
    sub = lax.broadcasted_iota(jnp.int32, shape, 0)
    count = LEAF // GROUP
    sets = [[b[GROUP * i : GROUP * (i + 1), :] for i in range(count)] for b in blocks]
    background = list(background)

    def row_of(v, p):
        return jnp.broadcast_to(v[p : p + 1, :], shape)

    def col_of(v, c):
        return jnp.broadcast_to(v[:, c : c + 1], shape)

    def eliminate(k, order):
        base = GROUP * k
        vs = [rows[k] for rows in sets]
        cols = [[col_of(v, base + p) for p in range(GROUP)] for v in vs]
        for p in range(0, GROUP, 2):
            first, second = sub == p, sub == p + 1
            both = first | second
            for at, c in enumerate(cols):
                a, b = row_of(c[p], p), row_of(c[p + 1], p)
                b_low, d = row_of(c[p], p + 1), row_of(c[p + 1], p + 1)
                det = a * d - b * b_low
                guess = pl.reciprocal(det, approx=True)
                refine = 2.0 - det * guess
                m0 = jnp.where(first, -1.0, jnp.where(second, 0.0, c[p]))
                m1 = jnp.where(first, 0.0, jnp.where(second, -1.0, c[p + 1]))

                def solved(x):
                    e0, e1 = row_of(x, p), row_of(x, p + 1)
                    t0 = d * e0 - b * e1
                    t1 = a * e1 - b_low * e0
                    return jnp.where(both, 0.0, x) - ((m0 * t0 + m1 * t1) * guess) * refine

                for q in range(p + 2, GROUP):
                    c[q] = solved(c[q])
                unit0 = jnp.where(first, 1.0, 0.0)
                unit1 = jnp.where(second, 1.0, 0.0)
                v = jnp.where(lane == base + p, unit0, jnp.where(lane == base + p + 1, unit1, vs[at]))
                vs[at] = solved(v)
        inside = (lane >= base) & (lane < base + GROUP)
        pivots = [[row_of(v, p) for p in range(GROUP)] for v in vs]
        for rows, v in zip(sets, vs):
            rows[k] = v
        for i in order:
            for rows, pivot in zip(sets, pivots):
                w = rows[i]
                terms = [col_of(w, base + p) * pivot[p] for p in range(GROUP)]
                while len(terms) > 1:
                    terms = [x + y for x, y in zip(terms[::2], terms[1::2])]
                rows[i] = jnp.where(inside, 0.0, w) - terms[0]

    per = PANEL // GROUP
    panels = count // per
    for j in range(panels):
        panel = list(range(per * j, per * (j + 1)))
        if j + 1 < panels:
            eager = list(range(per * (j + 1), per * (j + 2)))
        else:
            eager = list(range(per * j))
        others = [i for i in range(count) if i not in panel and i not in eager]
        for k in panel:
            eliminate(k, [i for i in panel if i > k] + [i for i in panel if i < k] + eager)
        inside = (lane >= PANEL * j) & (lane < PANEL * (j + 1))
        zeros = jnp.zeros(shape, jnp.float32)
        if others:
            for rows in sets:
                left = jnp.concatenate([jnp.where(inside, rows[i], 0.0) for i in others], axis=0)
                pivot = jnp.concatenate(
                    [rows[i] if i in panel else zeros for i in range(count)], axis=0
                )
                product = dot3(left, pivot)
                for at, i in enumerate(others):
                    kept = jnp.where(inside, 0.0, rows[i])
                    rows[i] = kept - product[GROUP * at : GROUP * (at + 1), :]
        share = -(-len(background) // (panels - j))
        for part in background[:share]:
            part()
        background = background[share:]
    return [jnp.concatenate(rows, axis=0) for rows in sets]


def inverse_in(work_refs, background=()):
    n = work_refs[0].shape[-1]
    steps = n // LEAF
    rest = n - LEAF
    scales = []
    for ref in work_refs:
        largest = jnp.max(jnp.max(jnp.abs(ref[0]), axis=0, keepdims=True), axis=1, keepdims=True)
        scales.append(1.0 / largest)
        ref[0] = ref[0] * scales[-1]

    def update(ref, src, dst, leaf):
        ls = split(leaf)
        cs = [split(ref[src, LEAF * r : LEAF * (r + 1), :LEAF]) for r in range(1, steps)]
        q = dot_split(ls, split(ref[src, :LEAF, LEAF : 2 * LEAF]))
        qs = [split(q)]
        pivot = ref[src, LEAF : 2 * LEAF, LEAF : 2 * LEAF] - dot_split(cs[0], qs[0])

        def prepare():
            wide = dot_split(ls, split(ref[src, :LEAF, 2 * LEAF :]))
            ref[dst, rest:, :LEAF] = q
            ref[dst, rest:, LEAF:rest] = wide
            ref[dst, rest:, rest:] = leaf
            ref[dst, :LEAF, :LEAF] = pivot
            whole_q = jnp.concatenate([q, wide], axis=1)
            qs[0] = split(whole_q)

        def strip(r):
            def run():
                rows = slice(LEAF * r, LEAF * (r + 1))
                out = slice(LEAF * (r - 1), LEAF * r)
                new = ref[src, rows, LEAF:] - dot_split(cs[r - 1], qs[0])
                if r == 1:
                    ref[dst, out, LEAF:rest] = new[:, LEAF:]
                else:
                    ref[dst, out, :rest] = new
                ref[dst, out, rest:] = -dot_split(cs[r - 1], ls)

            return run

        return pivot, [prepare] + [strip(r) for r in range(1, steps)]

    def body(step, leaves):
        src = lax.rem(step, 2)
        pivots, parts = [], []
        for ref, leaf in zip(work_refs, leaves):
            pivot, own = update(ref, src, 1 - src, leaf)
            pivots.append(pivot)
            parts.append(own)
        return tuple(leaf_inverse(pivots, [part for group in zip(*parts) for part in group]))

    leaves = tuple(leaf_inverse([ref[0, :LEAF, :LEAF] for ref in work_refs], background))
    leaves = lax.fori_loop(0, steps - 1, body, leaves)
    for ref, leaf in zip(work_refs, leaves):
        for part in update(ref, (steps - 1) % 2, steps % 2, leaf)[1]:
            part()
    for ref, scale in zip(work_refs, scales):
        ref[0] = ref[0] * scale


def plus_diagonal(matrix, row):
    shape = matrix.shape
    here = lax.broadcasted_iota(jnp.int32, shape, 0) == lax.broadcasted_iota(jnp.int32, shape, 1)
    return matrix + jnp.where(here, jnp.broadcast_to(row, shape), 0.0)


def dot_down(a, b):
    (ah, al), (bh, bl) = split(a), split(b)
    mul = functools.partial(
        lax.dot_general,
        dimension_numbers=(((0,), (0,)), ((), ())),
        preferred_element_type=jnp.float32,
    )
    return mul(ah, bh) + (mul(ah, bl) + mul(al, bh))


RIGHT, LAST, COL, MEMBER, SETTLED, PLANE = range(6)


def panel_kernel(pattern, coupling, mass, panel):
    width, half = coupling.shape
    tile_w = width // (width // LEAF)
    first = lax.axis_index("col") * half
    rows = lax.broadcasted_iota(jnp.int32, (LEAF, LEAF), 0)
    columns = lax.broadcasted_iota(jnp.int32, (LEAF, LEAF), 1)
    across = half // tile_w
    for r in range(width // tile_w):
        for c in range(across):
            at = (slice(tile_w * r, tile_w * (r + 1)), slice(tile_w * c, tile_w * (c + 1)))
            unit = (rows + tile_w * r == columns + (first + tile_w * c)).astype(jnp.float32)
            panel[at] = unit + pattern[across * r + c].astype(jnp.float32) * coupling[at]
    panel[width:, :] = jnp.broadcast_to(mass[...], (GROUP, half))


def place_bonds(flags, pieces, bonds):
    half = bonds.shape[-1] // 2
    me = flags[MEMBER]
    for source in range(2):
        core = flags[COL] if source == 0 else 1 - flags[COL]
        columns = pl.ds(pl.multiple_of(core * half, half), half)
        own, by_x, by_y, top, bottom = pieces[5 * source : 5 * source + 5]
        for rel, piece in enumerate((own, by_x, by_y)):
            bonds[me ^ rel, :, columns] = piece[...]
        bonds[me ^ 3, :half, columns] = top[...]
        bonds[me ^ 3, half:, columns] = bottom[...]


def first_kernel(flags, *refs):
    pieces = refs[:10]
    bonds, inverse, placed, work = refs[10:]
    width = inverse.shape[0]
    right = flags[RIGHT]
    place_bonds(flags, pieces, placed)
    for k in range(MEMBERS):
        at = jnp.where(right == 1, MEMBERS - 1 - k, k)
        bonds[k, :width, :] = placed[at, :width, :]
        at = jnp.where((right == 1) & (k > 0), MEMBERS - k, k)
        bonds[k, width:, :] = placed[at, width:, :]
    side = 2 * flags[COL]
    work[0] = plus_diagonal(
        bonds[side, :width, :] + bonds[side + 1, :width, :], bonds[side + 1, width : width + 1, :]
    )
    inverse_in([work])
    inverse[...] = work[0]


def sides(flags, mine, other):
    first = flags[COL] == 0
    a, b = mine[...], other[...]
    return jnp.where(first, a, b), jnp.where(first, b, a)


def reduce_kernel(
    flags, bonds, mine, other, i2, y10, y12, y32, y3i, yo, yi, goi, gio, mo, mi, mi_half, work_a, work_b
):
    width = i2.shape[0]

    def bond(k):
        return bonds[k, :width, :]

    def mass(k):
        return bonds[k, width : width + 1, :]

    right = flags[RIGHT]
    m1, m2, m3 = mass(1), mass(2), mass(3)
    c0, c1, c2, c3 = (split(bond(k)) for k in range(MEMBERS))
    p1, p3 = sides(flags, mine, other)
    q1, q3 = split(p1), split(p3)
    y12[...] = dot_split(c1, q1)
    y32[...] = dot_split(c2, q3)
    to_o = dot_split(split(y12[...]), c0)
    to_i = dot_split(split(y32[...]), c3)
    mass2 = plus_diagonal(y12[...] * m1 + y32[...] * m3, m2)
    work_a[0] = to_o + to_i + mass2

    def ends_i():
        y3i[...] = dot_split(c3, q3)

    def ends_o():
        y10[...] = dot_split(c0, q1)

    def from_i():
        work_b[0] = dot_split(split(y3i[...]), c2)

    def from_o():
        work_b[1] = dot_split(split(y10[...]), c1)

    inverse_in([work_a], [ends_i, ends_o, from_i, from_o])
    i2[...] = work_a[0]
    q2 = split(i2[...])
    sm = split(mass2)
    m0 = mass(0)
    left_on = jnp.where(right == 1, 0.0, 1.0)
    yi[...] = dot_split(split(work_b[0]), q2)
    si = split(yi[...])
    back = dot_split(si, split(to_o))
    gio[...] = back
    mi[...] = plus_diagonal(
        y3i[...] * m3 + dot_split(si, sm) + back * jnp.where(flags[LAST] == 1, 1.0, 0.0),
        m0 * (1.0 - left_on),
    )
    keep_half(flags, mi, mi_half)

    @pl.when(flags[LAST] == 0)
    def _():
        yo[...] = dot_split(split(work_b[1]), q2)
        so = split(yo[...])
        goi[...] = dot_split(so, split(to_i))
        mo[...] = plus_diagonal(y10[...] * m1 + dot_split(so, sm), m0 * left_on)

    @pl.when(flags[LAST] == 1)
    def _():
        yo[...] = jnp.zeros_like(yo)


def keep_half(flags, full, half_ref):
    half = half_ref.shape[1]
    half_ref[...] = jnp.where(flags[COL] == 0, full[:, :half], full[:, half:])


def whole(flags, mine, other):
    first = flags[COL] == 0
    a, b = mine[...], other[...]
    return jnp.concatenate([jnp.where(first, a, b), jnp.where(first, b, a)], axis=1)


def chain_kernel(planes, flags, goi, gio, mo, mi, mine, other, new_half, si, y, work):
    @pl.when((flags[PLANE] == planes[0]) | (flags[PLANE] == planes[1]))
    def _():
        mass_o = mo[...] + whole(flags, mine, other)
        work[0] = goi[...] + mass_o
        inverse_in([work])
        si[...] = work[0]
        y[...] = dot3(gio[...], si[...])
        work[0] = mi[...] + dot3(y[...], mass_o)
        keep_half(flags, work.at[0], new_half)


def root_first_kernel(
    root, flags, goi, gio, mo, mi, o_mine, o_other, i_mine, i_other, inv_i, y, left, work
):
    @pl.when(flags[PLANE] == root)
    def _():
        mass_i = mi[...] + whole(flags, i_mine, i_other)
        work[0] = gio[...] + mass_i
        inverse_in([work])
        inv_i[...] = work[0]
        y[...] = dot3(goi[...], inv_i[...])
        mass_o = mo[...] + whole(flags, o_mine, o_other)
        left[...] = mass_o + dot3(y[...], mass_i)


def root_last_kernel(
    root, flags, inv_i, y, left, ro, ro_in, ri, ri_in, xo, xi, work, inner, outer
):
    @pl.when(flags[PLANE] == root)
    def _():
        work[0] = left[...]

        def columns():
            s = split(ri[...] + ri_in[...])
            inner[...] = dot_split(split(inv_i[...]), s)
            outer[...] = ro[...] + ro_in[...] + dot_split(split(y[...]), s)

        inverse_in([work], [columns])
        xo[...] = dot3(work[0], outer[...])
        xi[...] = inner[...] + dot_down(y[...], xo[...])


def columns_kernel(
    flags, own, by_x, by_y, by_xy, p_mine, p_other, i2, y10, y12, y32, y3i, yo, yi, w, ao, ai, ro, ri, rhs
):
    right = flags[RIGHT]
    member = flags[MEMBER]
    for rel, piece in enumerate((own, by_x, by_y, by_xy)):
        rhs[member ^ rel] = piece[...]
    r0 = rhs[0]
    r2 = rhs[2]
    r1 = rhs[jnp.where(right == 1, 3, 1)]
    r3 = rhs[jnp.where(right == 1, 1, 3)]
    s1, s3 = split(r1), split(r3)
    p1, p3 = sides(flags, p_mine, p_other)
    v1 = dot_split(split(p1), s1)
    v3 = dot_split(split(p3), s3)
    r2 = r2 + dot_split(split(y12[...]), s1) + dot_split(split(y32[...]), s3)
    s2 = split(r2)
    v2 = dot_split(split(i2[...]), s2)
    left_on = jnp.where(right == 1, 0.0, 1.0)
    yos, yis = split(yo[...]), split(yi[...])
    ro[...] = r0 * left_on + dot_split(split(y10[...]), s1) + dot_split(yos, s2)
    ri[...] = r0 * (1.0 - left_on) + dot_split(split(y3i[...]), s3) + dot_split(yis, s2)
    is_2 = member == 2
    is_1 = member == jnp.where(right == 1, 3, 1)
    z = jnp.where(is_1, y12[...], y32[...])
    zs = split(z)
    w[...] = jnp.where(is_2, v2, jnp.where(is_1, v1, v3) + dot_down(z, v2))
    ao[...] = jnp.where(is_2, yo[...], dot_split(yos, zs) + jnp.where(is_1, y10[...], 0.0))
    ai[...] = jnp.where(is_2, yi[...], dot_split(yis, zs) + jnp.where(is_1, 0.0, y3i[...]))


def chain_columns_kernel(y, si, ro, ro_in, ri, new_ri, vo):
    s = split(ro[...] + ro_in[...])
    new_ri[...] = ri[...] + dot_split(split(y[...]), s)
    vo[...] = dot_split(split(si[...]), s)


def chain_back_kernel(vo, y, xi, xo):
    xo[...] = vo[...] + dot_down(y[...], xi[...])


def final_kernel(flags, w, ao, ai, y, vo, last_y, last_vo, xo, xi, in_a, in_b, in_c, out):
    last = flags[LAST] == 1
    settled = flags[SETTLED] == 1
    came = in_a[...] + in_b[...] + in_c[...]
    end = jnp.where(last, last_vo[...], vo[...]) + dot_down(
        jnp.where(last, last_y[...], y[...]), came
    )
    end_o = jnp.where(settled, xo[...], jnp.where(last, 0.0, end))
    end_i = jnp.where(settled, xi[...], jnp.where(last, end, came))
    mine = w[...] + dot_down(ao[...], end_o) + dot_down(ai[...], end_i)
    here = jnp.where(flags[RIGHT] == 1, end_i, end_o)
    out[...] = jnp.where(flags[MEMBER] == 0, here, mine)


def call(kernel, args, outs, scratch=(), flops=0):
    def spec(a):
        space = pltpu.SMEM if a.dtype == jnp.int32 else pltpu.VMEM
        return pl.BlockSpec(memory_space=space)

    moved = sum(a.size * 4 for a in args) + sum(4 * math.prod(s) for s in outs)
    held = moved + sum(4 * math.prod(s) for s in scratch)
    return pl.pallas_call(
        kernel,
        out_shape=[jax.ShapeDtypeStruct(s, jnp.float32) for s in outs],
        in_specs=[spec(a) for a in args],
        out_specs=[pl.BlockSpec(memory_space=pltpu.VMEM) for _ in outs],
        scratch_shapes=[pltpu.VMEM(s, jnp.float32) for s in scratch],
        cost_estimate=pl.CostEstimate(flops=flops, bytes_accessed=moved, transcendentals=0),
        compiler_params=pltpu.CompilerParams(vmem_limit_bytes=held + SPARE_BYTES),
    )(*args)


def on_device(coupling, tile_pattern, orbital_mass, sources):
    width = coupling.shape[1]
    half = coupling.shape[2]
    modes = sources.shape[2]
    column = lax.axis_index("col")
    member = lax.axis_index("member")
    group = lax.axis_index("group")
    groups = lax.axis_size("group")
    middle = groups // 2

    def send(x, pairs):
        return lax.ppermute(x, "group", pairs)

    def swap(x, bits):
        return lax.ppermute(x, "member", [(m, m ^ bits) for m in range(MEMBERS)])

    def other_core(x):
        return lax.ppermute(x, "col", [(0, 1), (1, 0)])

    def after(x, *others):
        return lax.optimization_barrier((x, *others))[0]

    (own,) = call(
        panel_kernel,
        [tile_pattern[0].reshape(-1), coupling[0], orbital_mass],
        [(width + GROUP, half)],
    )
    by_x, by_y = swap(own, 1), swap(own, 2)
    top, bottom = swap(by_x[:half], 2), swap(by_y[half:], 1)
    mine = [own, by_x, by_y, top, bottom]
    pieces = mine + [other_core(piece) for piece in mine]
    settled = flags[SETTLED] == 1
    came = in_a[...] + in_b[...] + in_c[...]
    end = jnp.where(last, last_vo[...], vo[...]) + dot_down(
        jnp.where(last, last_y[...], y[...]), came
    )
    end_o = jnp.where(settled, xo[...], jnp.where(last, 0.0, end))
    end_i = jnp.where(settled, xi[...], jnp.where(last, end, came))
    mine = w[...] + dot_down(ao[...], end_o) + dot_down(ai[...], end_i)
    here = jnp.where(flags[RIGHT] == 1, end_i, end_o)
    out[...] = jnp.where(flags[MEMBER] == 0, here, mine)


def call(kernel, args, outs, scratch=(), flops=0):
    def spec(a):
        space = pltpu.SMEM if a.dtype == jnp.int32 else pltpu.VMEM
        return pl.BlockSpec(memory_space=space)

    moved = sum(a.size * 4 for a in args) + sum(4 * math.prod(s) for s in outs)
    held = moved + sum(4 * math.prod(s) for s in scratch)
    return pl.pallas_call(
        kernel,
        out_shape=[jax.ShapeDtypeStruct(s, jnp.float32) for s in outs],
        in_specs=[spec(a) for a in args],
        out_specs=[pl.BlockSpec(memory_space=pltpu.VMEM) for _ in outs],
        scratch_shapes=[pltpu.VMEM(s, jnp.float32) for s in scratch],
        cost_estimate=pl.CostEstimate(flops=flops, bytes_accessed=moved, transcendentals=0),
        compiler_params=pltpu.CompilerParams(vmem_limit_bytes=held + SPARE_BYTES),
    )(*args)


def on_device(coupling, tile_pattern, orbital_mass, sources):
    width = coupling.shape[1]
    half = coupling.shape[2]
    modes = sources.shape[2]
    column = lax.axis_index("col")
    member = lax.axis_index("member")
    group = lax.axis_index("group")
    groups = lax.axis_size("group")
    middle = groups // 2

    def send(x, pairs):
        return lax.ppermute(x, "group", pairs)

    def swap(x, bits):
        return lax.ppermute(x, "member", [(m, m ^ bits) for m in range(MEMBERS)])

    def other_core(x):
        return lax.ppermute(x, "col", [(0, 1), (1, 0)])

    def after(x, *others):
        return lax.optimization_barrier((x, *others))[0]

    (own,) = call(
        panel_kernel,
        [tile_pattern[0].reshape(-1), coupling[0], orbital_mass],
        [(width + GROUP, half)],
    )
    by_x, by_y = swap(own, 1), swap(own, 2)
    top, bottom = swap(by_x[:half], 2), swap(by_y[half:], 1)
    mine = [own, by_x, by_y, top, bottom]
    pieces = mine + [other_core(piece) for piece in mine]
    source = after(sources[0], top, bottom)
    rhs = [source, swap(source, 1), swap(source, 2), swap(source, 3)]
    settled = (group != 0) & (group < groups - 2)
    flags = jnp.stack(
        [
            (group >= middle).astype(jnp.int32),
            (group == groups - 1).astype(jnp.int32),
            column.astype(jnp.int32),
            member.astype(jnp.int32),
            settled.astype(jnp.int32),
            group.astype(jnp.int32),
        ]
    )
    square = (width, width)
    block = (width, modes)
    panel = (width, half)
    room = (2, width, width)
    unit_flops = 6 * width**3
    bonds, p_mine = call(
        first_kernel,
        [flags, *pieces],
        [(MEMBERS, width + GROUP, width), square],
        [(MEMBERS, width + GROUP, width), room],
        20 * unit_flops,
    )
    p_other = other_core(p_mine)
    source = after(sources[0], p_mine)
    rhs = [source, swap(source, 1), swap(source, 2), swap(source, 3)]
    i2, y10, y12, y32, y3i, yo, yi, goi, gio, mo, mi, mi_half = call(
        reduce_kernel,
        [flags, bonds, p_mine, p_other],
        [square] * 11 + [panel],
        [room, room],
        30 * unit_flops,
    )
    first = [(groups - 1, groups - 2)]
    into_o = send(mi_half, first)
    w, ao, ai, ro, ri = call(
        columns_kernel,
        [flags, *rhs, p_mine, p_other, i2, y10, y12, y32, y3i, yo, yi],
        [block, square, square, block, block],
        [(MEMBERS, width, modes)],
        flops=6 * unit_flops,
    )
    ro_in = send(ri, first)
    into_o = after(into_o, ro)
    steps = []
    for t in range(middle - 1):
        new_half, si, y = call(
            functools.partial(chain_kernel, (t, groups - 2 - t)),
            [flags, goi, gio, mo, mi, into_o, other_core(into_o)],
            [panel, square, square],
            [room],
            20 * unit_flops,
        )
        upward = [(t, t + 1)]
        downward = [(groups - 2 - t, groups - 3 - t)]
        from_left, from_right = send(new_half, upward), send(new_half, downward)
        new_ri, vo = call(
            chain_columns_kernel, [y, si, ro, ro_in, ri], [block] * 2, flops=unit_flops
        )
        steps.append((y, vo))
        rhs_left, rhs_right = send(new_ri, upward), send(new_ri, downward)
        from_left, from_right = after(from_left, vo), after(from_right, vo)
        if groups - 3 - t >= middle:
            into_o = from_left + from_right
            ro_in = rhs_left + rhs_right
        else:
            into_o, into_i = from_left, from_right
            ro_in, ri_in = rhs_left, rhs_right
    inv_i, y, left = call(
        functools.partial(root_first_kernel, middle - 1),
        [flags, goi, gio, mo, mi, into_o, other_core(into_o), into_i, other_core(into_i)],
        [square] * 3,
        [room],
        20 * unit_flops,
    )
    last_y, last_vo = (send(after(part, inv_i), [(groups - 2, groups - 1)]) for part in steps[0])
    xo, xi = call(
        functools.partial(root_last_kernel, middle - 1),
        [flags, inv_i, y, left, ro, ro_in, ri, ri_in],
        [block] * 2,
        [room, block, block],
        20 * unit_flops,
    )
    for t in reversed(range(1, middle - 1)):
        y, vo = steps[t]
        from_right = send(xo, [(t + 1, t)])
        from_left = send(jnp.where(group == middle - 1, xi, xo), [(groups - 3 - t, groups - 2 - t)])
        on_left = group == t
        on_right = group == groups - 2 - t
        xi = jnp.where(on_left, from_right, jnp.where(on_right, from_left, xi))
        (outer,) = call(chain_back_kernel, [vo, y, xi], [block], flops=unit_flops)
        xo = jnp.where(on_left | on_right, outer, xo)
    outward = xi if middle - 1 == groups - 3 else xo
    in_a = send(xo, [(1, 0)])
    in_b = send(outward, [(groups - 3, groups - 2)])
    in_c = send(outward, [(groups - 3, groups - 1)])
    y, vo = steps[0]
    (out,) = call(
        final_kernel,
        [flags, w, ao, ai, y, vo, last_y, last_vo, xo, xi, in_a, in_b, in_c],
        [block],
        flops=2 * unit_flops,
    )
    return out[None]


def solution(mesh):
    groups = mesh.shape["slab"] // MEMBERS
    fine = Mesh(
        mesh.devices.reshape(groups, MEMBERS, mesh.shape["col"]), ("group", "member", "col")
    )
    slab = ("group", "member")
    placed = (
        P(slab, None, "col"),
        P(slab, None, "col"),
        P(slab, "col"),
        P(slab, None, "col"),
    )
    return jax.shard_map(
        on_device, mesh=fine, in_specs=placed, out_specs=P(slab, None, "col"), check_vma=False
    )
```

profile of v0, /device:TPU:28, one launch (start us, length us, event | category | flops | bytes accessed | tf_op | source)
XLA Modules:
  0.0 216.5 jit_solution(2674395165258852387)
XLA Ops:
  0.0 0.8 copy.6
  0.9 1.0 copy-done
  3.8 1.5 collective-permute-start
  5.3 11.8 %collective-permute-done.1.refs_2_ = f32[520,256]{1,0:T(8,128)S(1)} collective-permute-done((f32[520,256]{1,0:T(8,128)S(1)}, f32[520,256]{1,0:T(8,128)S(1)}, u32[]{:S(2)}, u32[]{:S(2)}) %collective-permute-start.1) | collective-permute-done | bytes 532512 | tf_op jit(solution)/shard_map/ppermute | solution.py:516
  17.1 1.6 collective-permute-start.3
  19.8 4.7 %collective-permute-done.3.refs_4_ = f32[264,256]{1,0:T(8,128)S(1)} collective-permute-done((f32[264,256]{1,0:T(8,128)S(1)}, f32[264,256]{1,0:T(8,128)S(1)}, u32[]{:S(2)}, u32[]{:S(2)}) %collective-permute-start.3) | collective-permute-done | bytes 270368 | tf_op jit(solution)/shard_map/ppermute | solution.py:516
  24.5 3.6 %collective-permute-done.2.refs_3_ = f32[256,256]{1,0:T(8,128)} collective-permute-done((f32[256,256]{1,0:T(8,128)S(1)}, f32[256,256]{1,0:T(8,128)}, u32[]{:S(2)}, u32[]{:S(2)}) %collective-permute-start.2) | collective-permute-done | bytes 262176 | tf_op jit(solution)/shard_map/ppermute | solution.py:516
  28.2 1.8 collective-permute-done.7.refs_8_
  30.0 23.1 %shard_map.47 = (f32[4,520,512]{2,1,0:T(8,128)S(1)}, f32[512,512]{1,0:T(8,128)S(1)}) custom-call(s32[6]{0:T(128)S(1)} %stack.39.flags, f32[520,256]{1,0:T(8,128)S(1)} %shard_map.46.refs_0_, f32[520,256]{1,0:T(8,128)S(1)} %collective-permute-done.refs_1_, f32[520,256]{1,0:T(8,128)S(1)} %collective-permute-done.1.refs_2_, ...), custom_call_target="tpu_custom_call" | custom-call | flops 16106127360 | bytes 9568280 | tf_op jit(solution)/shard_map/pallas_call | solution.py:491
  53.1 2.0 copy-done.3
  55.8 1.5 collective-permute-start.11
  57.3 1.5 collective-permute-start.9
  58.8 30.8 %shard_map.48 = (f32[512,512]{1,0:T(8,128)S(1)}, f32[512,512]{1,0:T(8,128)S(1)}, f32[512,512]{1,0:T(8,128)S(1)}, f32[512,512]{1,0:T(8,128)S(1)}, f32[512,512]{1,...) custom-call(s32[6]{0:T(128)S(1)} %stack.39.flags, ...), custom_call_target="tpu_custom_call" | custom-call | flops 24159191040 | bytes 18415640 | tf_op jit(solution)/shard_map/pallas_call | solution.py:491
  89.5 4.9 %collective-permute-start.13 = (f32[512,256]{1,0:T(8,128)S(1)}, f32[512,256]{1,0:T(8,128)S(1)}, u32[]{:S(2)}, u32[]{:S(2)}) collective-permute-start(f32[512,256]{1,0:T(8,128)S(1)} %get-tuple-element.57), channel_id=1, source_target_pairs={{24,16},{25,17},{26,18},{27,19},{28,20},{29,21},{30,22},{31,23}} | collective-permute-start | bytes 1572872 | tf_op jit(solution)/shard_map/ppermute | solution.py:513
  94.5 8.4 %shard_map.49 = (f32[512,128]{1,0:T(8,128)S(1)}, f32[512,512]{1,0:T(8,128)S(1)}, f32[512,512]{1,0:T(8,128)S(1)}, f32[512,128]{1,0:T(8,128)S(1)}, f32[512,128]{1,0:T(8,128)S(1)}) custom-call(s32[6]{0:T(128)S(1)} %stack.39.flags, f32[512,128]{1,0:T(8,128)S(1)} %bitcast.13, f32[512,128]{1,0:T(8,128)S(1)} %collective-permute-done.9.by_x, ...), custom_call_target="tpu_custom_call" | custom-call | flops 4831838208 | bytes 13369368 | tf_op jit(solution)/shard_map/pallas_call | solution.py:491
  102.9 2.4 %collective-permute-done.13.mine = f32[512,256]{1,0:T(8,128)S(1)} collective-permute-done((f32[512,256]{1,0:T(8,128)S(1)}, f32[512,256]{1,0:T(8,128)S(1)}, u32[]{:S(2)}, u32[]{:S(2)}) %collective-permute-start.13) | collective-permute-done | bytes 524320 | tf_op jit(solution)/shard_map/ppermute | solution.py:513
  105.3 1.9 collective-permute-done.14.other
  107.2 0.7 shard_map.50
  108.0 0.7 collective-permute-start.18
  108.7 0.7 collective-permute-start.16
  109.4 28.0 %collective-permute-start.15 = (f32[512,128]{1,0:T(8,128)S(1)}, f32[512,128]{1,0:T(8,128)S(1)}, u32[]{:S(2)}, u32[]{:S(2)}) collective-permute-start(f32[512,128]{1,0:T(8,128)S(1)} %get-tuple-element.62.ri), channel_id=1, source_target_pairs={{24,16},{25,17},{26,18},{27,19},{28,20},{29,21},{30,22},{31,23}} | collective-permute-start | bytes 786440 | tf_op jit(solution)/shard_map/ppermute | solution.py:513
  137.3 5.8 %collective-permute-done.15.ro_in = f32[512,128]{1,0:T(8,128)S(1)} collective-permute-done((f32[512,128]{1,0:T(8,128)S(1)}, f32[512,128]{1,0:T(8,128)S(1)}, u32[]{:S(2)}, u32[]{:S(2)}) %collective-permute-start.15) | collective-permute-done | bytes 262176 | tf_op jit(solution)/shard_map/ppermute | solution.py:513
  143.2 1.0 shard_map.51
  145.5 0.7 collective-permute-start.23
  146.2 0.7 collective-permute-done.17.o_other
  146.9 0.8 shard_map.52
  147.7 1.3 collective-permute-start.20
  149.0 6.8 %shard_map.53 = (f32[512,128]{1,0:T(8,128)S(1)}, f32[512,128]{1,0:T(8,128)S(1)}) custom-call(s32[6]{0:T(128)S(1)} %stack.39.flags, f32[512,512]{1,0:T(8,128)S(1)} %get-tuple-element.67.inv_i, f32[512,512]{1,0:T(8,128)S(1)} %get-tuple-element.70.y, f32[512,512]{1,0:T(8,128)S(1)} %get-tuple-element.71.left, f32[512,128]{1,0:T(8,128)S(1)} %get-tuple-element.58.ro, ...), custom_call_target="tpu_custom_call" | custom-call | flops 16106127360 | bytes 4718616 | tf_op jit(solution)/shard_map/pallas_call | solution.py:491
  156.5 1.3 collective-permute-start.26
  158.5 1.3 collective-permute-start.21
  159.8 52.6 %collective-permute-done.26.in_c = f32[512,128]{1,0:T(8,128)S(1)} collective-permute-done((f32[512,128]{1,0:T(8,128)S(1)}, f32[512,128]{1,0:T(8,128)S(1)}, u32[]{:S(2)}, u32[]{:S(2)}) %collective-permute-start.26) | collective-permute-done | bytes 262176 | tf_op jit(solution)/shard_map/ppermute | solution.py:513
  212.4 3.7 %shard_map.54 = f32[512,128]{1,0:T(8,128)} custom-call(s32[6]{0:T(128)S(1)} %stack.39.flags, f32[512,128]{1,0:T(8,128)S(1)} %get-tuple-element.50.w, f32[512,512]{1,0:T(8,128)S(1)} %get-tuple-element.51.ao, f32[512,512]{1,0:T(8,128)S(1)} %get-tuple-element.52.ai, f32[512,512]{1,0:T(8,128)S(1)} %get-tuple-element.68.y, f32[512,128]{1,0:T(8,128)S(1)} %get-tuple-element.69.vo, ...), custom_call_target="tpu_custom_call" | custom-call | flops 1610612736 | bytes 6553624 | tf_op jit(solution)/shard_map/pallas_call | solution.py:491
  (44 shorter events, 6.5 us)
Async XLA Ops:
  0.9 1.0 copy-start
  1.9 0.7 copy-start.1
  3.2 13.9 %collective-permute-start.1 = (f32[520,256]{1,0:T(8,128)S(1)}, f32[520,256]{1,0:T(8,128)S(1)}, u32[]{:S(2)}, u32[]{:S(2)}) collective-permute-start(f32[520,256]{1,0:T(8,128)S(1)} %shard_map.46.refs_0_), channel_id=1, source_target_pairs={{0,4},{2,6},{4,0},{6,2},{1,5},{3,7},{5,1},{7,3},{8,12},{10,14},{12... | collective-permute-start | bytes 1597448 | tf_op jit(solution)/shard_map/ppermute | solution.py:516
  3.8 14.9 %collective-permute-start = (f32[520,256]{1,0:T(8,128)S(1)}, f32[520,256]{1,0:T(8,128)S(1)}, u32[]{:S(2)}, u32[]{:S(2)}) collective-permute-start(f32[520,256]{1,0:T(8,128)S(1)} %shard_map.46.refs_0_), channel_id=1, source_target_pairs={{0,2},{2,0},{4,6},{6,4},{1,3},{3,1},{5,7},{7,5},{8,10},{10,8},{12,... | collective-permute-start | bytes 1597448 | tf_op jit(solution)/shard_map/ppermute | solution.py:516
  17.1 7.4 %collective-permute-start.3 = (f32[264,256]{1,0:T(8,128)S(1)}, f32[264,256]{1,0:T(8,128)S(1)}, u32[]{:S(2)}, u32[]{:S(2)}) collective-permute-start(f32[264,256]{1,0:T(8,128)S(1)} %slice.9), channel_id=1, source_target_pairs={{0,2},{2,0},{4,6},{6,4},{1,3},{3,1},{5,7},{7,5},{8,10},{10,8},{12,... | collective-permute-start | bytes 811016 | tf_op jit(solution)/shard_map/ppermute | solution.py:516
  18.7 9.5 %collective-permute-start.4 = (f32[520,256]{1,0:T(8,128)S(1)}, f32[520,256]{1,0:T(8,128)S(1)}, u32[]{:S(2)}, u32[]{:S(2)}) collective-permute-start(f32[520,256]{1,0:T(8,128)S(1)} %shard_map.46.refs_0_), channel_id=1, source_target_pairs={{0,1},{1,0},{2,3},{3,2},{4,5},{5,4},{6,7},{7,6},{8,9},{9,8},{10,11... | collective-permute-start | bytes 1597448 | tf_op jit(solution)/shard_map/ppermute | solution.py:519
  18.7 11.3 %collective-permute-start.5 = (f32[520,256]{1,0:T(8,128)S(1)}, f32[520,256]{1,0:T(8,128)S(1)}, u32[]{:S(2)}, u32[]{:S(2)}) collective-permute-start(f32[520,256]{1,0:T(8,128)S(1)} %collective-permute-done.refs_1_), channel_id=1, source_target_pairs={{0,1},{1,0},{2,3},{3,2},{4,5},{5,4},{6,7},{7,6},{8,9},{9,8},{10,11... | collective-permute-start | bytes 1597448 | tf_op jit(solution)/shard_map/ppermute | solution.py:519
  19.2 10.8 %collective-permute-start.6 = (f32[520,256]{1,0:T(8,128)S(1)}, f32[520,256]{1,0:T(8,128)S(1)}, u32[]{:S(2)}, u32[]{:S(2)}) collective-permute-start(f32[520,256]{1,0:T(8,128)S(1)} %collective-permute-done.1.refs_2_), channel_id=1, source_target_pairs={{0,1},{1,0},{2,3},{3,2},{4,5},{5,4},{6,7},{7,6},{8,9},{9,8},{10,11... | collective-permute-start | bytes 1597448 | tf_op jit(solution)/shard_map/ppermute | solution.py:519
  19.2 8.9 %collective-permute-start.2 = (f32[256,256]{1,0:T(8,128)S(1)}, f32[256,256]{1,0:T(8,128)}, u32[]{:S(2)}, u32[]{:S(2)}) collective-permute-start(f32[256,256]{1,0:T(8,128)S(1)} %slice.8), channel_id=1, source_target_pairs={{0,4},{2,6},{4,0},{6,2},{1,5},{3,7},{5,1},{7,3},{8,12},{10,14},{12... | collective-permute-start | bytes 786440 | tf_op jit(solution)/shard_map/ppermute | solution.py:516
  24.5 5.5 %collective-permute-start.8 = (f32[264,256]{1,0:T(8,128)S(1)}, f32[264,256]{1,0:T(8,128)}, u32[]{:S(2)}, u32[]{:S(2)}) collective-permute-start(f32[264,256]{1,0:T(8,128)S(1)} %collective-permute-done.3.refs_4_), channel_id=1, source_target_pairs={{0,1},{1,0},{2,3},{3,2},{4,5},{5,4},{6,7},{7,6},{8,9},{9,8},{10,11... | collective-permute-start | bytes 811016 | tf_op jit(solution)/shard_map/ppermute | solution.py:519
  28.1 1.9 collective-permute-start.7
  28.2 27.0 %copy-start.2 = (f32[1,512,128]{2,1,0:T(8,128)S(1)}, f32[1,512,128]{2,1,0:T(8,128)}, u32[]{:S(2)}) copy-start(f32[1,512,128]{2,1,0:T(8,128)} %param.7) | copy-start | bytes 786436
  53.1 2.0 copy-start.3
  55.1 3.6 %collective-permute-start.12 = (f32[512,512]{1,0:T(8,128)S(1)}, f32[512,512]{1,0:T(8,128)S(1)}, u32[]{:S(2)}, u32[]{:S(2)}) collective-permute-start(f32[512,512]{1,0:T(8,128)S(1)} %get-tuple-element.40.mine.p_mine), channel_id=1, source_target_pairs={{0,1},{1,0},{2,3},{3,2},{4,5},{5,4},{6,7},{7,6},{8,9},{9,8},{10,11... | collective-permute-start | bytes 3145736 | tf_op jit(solution)/shard_map/ppermute | solution.py:519
  55.2 39.2 %collective-permute-start.10 = (f32[512,128]{1,0:T(8,128)S(1)}, f32[512,128]{1,0:T(8,128)S(1)}, u32[]{:S(2)}, u32[]{:S(2)}) collective-permute-start(f32[512,128]{1,0:T(8,128)S(1)} %bitcast.10), channel_id=1, source_target_pairs={{0,4},{2,6},{4,0},{6,2},{1,5},{3,7},{5,1},{7,3},{8,12},{10,14},{12... | collective-permute-start | bytes 786440 | tf_op jit(solution)/shard_map/ppermute | solution.py:516
  55.8 38.7 %collective-permute-start.11 = (f32[512,128]{1,0:T(8,128)S(1)}, f32[512,128]{1,0:T(8,128)S(1)}, u32[]{:S(2)}, u32[]{:S(2)}) collective-permute-start(f32[512,128]{1,0:T(8,128)S(1)} %bitcast.11), channel_id=1, source_target_pairs={{0,6},{2,4},{4,2},{6,0},{1,7},{3,5},{5,3},{7,1},{8,14},{10,12},{12... | collective-permute-start | bytes 786440 | tf_op jit(solution)/shard_map/ppermute | solution.py:516
  57.3 37.2 %collective-permute-start.9 = (f32[512,128]{1,0:T(8,128)S(1)}, f32[512,128]{1,0:T(8,128)S(1)}, u32[]{:S(2)}, u32[]{:S(2)}) collective-permute-start(f32[512,128]{1,0:T(8,128)S(1)} %bitcast.12), channel_id=1, source_target_pairs={{0,2},{2,0},{4,6},{6,4},{1,3},{3,1},{5,7},{7,5},{8,10},{10,8},{12,... | collective-permute-start | bytes 786440 | tf_op jit(solution)/shard_map/ppermute | solution.py:516
  89.5 15.8 %collective-permute-start.13 = (f32[512,256]{1,0:T(8,128)S(1)}, f32[512,256]{1,0:T(8,128)S(1)}, u32[]{:S(2)}, u32[]{:S(2)}) collective-permute-start(f32[512,256]{1,0:T(8,128)S(1)} %get-tuple-element.57), channel_id=1, source_target_pairs={{24,16},{25,17},{26,18},{27,19},{28,20},{29,21},{30,22},{31,23}} | collective-permute-start | bytes 1572872 | tf_op jit(solution)/shard_map/ppermute | solution.py:513
  105.3 1.9 collective-permute-start.14
  108.0 36.2 %collective-permute-start.18 = (f32[512,256]{1,0:T(8,128)S(1)}, f32[512,256]{1,0:T(8,128)S(1)}, u32[]{:S(2)}, u32[]{:S(2)}) collective-permute-start(f32[512,256]{1,0:T(8,128)S(1)} %get-tuple-element.64), channel_id=1, source_target_pairs={{16,8},{17,9},{18,10},{19,11},{20,12},{21,13},{22,14},{23,15}} | collective-permute-start | bytes 1572872 | tf_op jit(solution)/shard_map/ppermute | solution.py:513
  108.7 35.6 %collective-permute-start.16 = (f32[512,256]{1,0:T(8,128)S(1)}, f32[512,256]{1,0:T(8,128)S(1)}, u32[]{:S(2)}, u32[]{:S(2)}) collective-permute-start(f32[512,256]{1,0:T(8,128)S(1)} %get-tuple-element.64), channel_id=1, source_target_pairs={{0,8},{1,9},{2,10},{3,11},{4,12},{5,13},{6,14},{7,15}} | collective-permute-start | bytes 1572872 | tf_op jit(solution)/shard_map/ppermute | solution.py:513
  109.4 33.8 %collective-permute-start.15 = (f32[512,128]{1,0:T(8,128)S(1)}, f32[512,128]{1,0:T(8,128)S(1)}, u32[]{:S(2)}, u32[]{:S(2)}) collective-permute-start(f32[512,128]{1,0:T(8,128)S(1)} %get-tuple-element.62.ri), channel_id=1, source_target_pairs={{24,16},{25,17},{26,18},{27,19},{28,20},{29,21},{30,22},{31,23}} | collective-permute-start | bytes 786440 | tf_op jit(solution)/shard_map/ppermute | solution.py:513
  144.2 2.0 collective-permute-start.19
  144.3 2.6 %collective-permute-start.17 = (f32[512,256]{1,0:T(8,128)S(1)}, f32[512,256]{1,0:T(8,128)S(1)}, u32[]{:S(2)}, u32[]{:S(2)}) collective-permute-start(f32[512,256]{1,0:T(8,128)S(1)} %collective-permute-done.16.o_mine), channel_id=1, source_target_pairs={{0,1},{1,0},{2,3},{3,2},{4,5},{5,4},{6,7},{7,6},{8,9},{9,8},{10,11... | collective-permute-start | bytes 1572872 | tf_op jit(solution)/shard_map/ppermute | solution.py:519
  144.8 4.2 %collective-permute-start.22 = (f32[512,128]{1,0:T(8,128)S(1)}, f32[512,128]{1,0:T(8,128)S(1)}, u32[]{:S(2)}, u32[]{:S(2)}) collective-permute-start(f32[512,128]{1,0:T(8,128)S(1)} %get-tuple-element.72), channel_id=1, source_target_pairs={{0,8},{1,9},{2,10},{3,11},{4,12},{5,13},{6,14},{7,15}} | collective-permute-start | bytes 786440 | tf_op jit(solution)/shard_map/ppermute | solution.py:513
  145.5 3.6 %collective-permute-start.23 = (f32[512,128]{1,0:T(8,128)S(1)}, f32[512,128]{1,0:T(8,128)S(1)}, u32[]{:S(2)}, u32[]{:S(2)}) collective-permute-start(f32[512,128]{1,0:T(8,128)S(1)} %get-tuple-element.72), channel_id=1, source_target_pairs={{16,8},{17,9},{18,10},{19,11},{20,12},{21,13},{22,14},{23,15}} | collective-permute-start | bytes 786440 | tf_op jit(solution)/shard_map/ppermute | solution.py:513
  147.7 64.7 %collective-permute-start.20 = (f32[512,512]{1,0:T(8,128)S(1)}, f32[512,512]{1,0:T(8,128)S(1)}, u32[]{:S(2)}, u32[]{:S(2)}) collective-permute-start(f32[512,512]{1,0:T(8,128)S(1)} %get-tuple-element.68.y), channel_id=1, source_target_pairs={{16,24},{17,25},{18,26},{19,27},{20,28},{21,29},{22,30},{23,31}} | collective-permute-start | bytes 3145736 | tf_op jit(solution)/shard_map/ppermute | solution.py:513
  155.8 4.0 %collective-permute-start.25 = (f32[512,128]{1,0:T(8,128)S(1)}, f32[512,128]{1,0:T(8,128)S(1)}, u32[]{:S(2)}, u32[]{:S(2)}) collective-permute-start(f32[512,128]{1,0:T(8,128)S(1)} %get-tuple-element.74.xi), channel_id=1, source_target_pairs={{8,16},{9,17},{10,18},{11,19},{12,20},{13,21},{14,22},{15,23}} | collective-permute-start | bytes 786440 | tf_op jit(solution)/shard_map/ppermute | solution.py:513
  156.5 55.9 %collective-permute-start.26 = (f32[512,128]{1,0:T(8,128)S(1)}, f32[512,128]{1,0:T(8,128)S(1)}, u32[]{:S(2)}, u32[]{:S(2)}) collective-permute-start(f32[512,128]{1,0:T(8,128)S(1)} %get-tuple-element.74.xi), channel_id=1, source_target_pairs={{8,24},{9,25},{10,26},{11,27},{12,28},{13,29},{14,30},{15,31}} | collective-permute-start | bytes 786440 | tf_op jit(solution)/shard_map/ppermute | solution.py:513
  157.8 2.0 collective-permute-start.24
  158.5 53.9 %collective-permute-start.21 = (f32[512,128]{1,0:T(8,128)S(1)}, f32[512,128]{1,0:T(8,128)S(1)}, u32[]{:S(2)}, u32[]{:S(2)}) collective-permute-start(f32[512,128]{1,0:T(8,128)S(1)} %get-tuple-element.69.vo), channel_id=1, source_target_pairs={{16,24},{17,25},{18,26},{19,27},{20,28},{21,29},{22,30},{23,31}} | collective-permute-start | bytes 786440 | tf_op jit(solution)/shard_map/ppermute | solution.py:513
where the time goes:
time: 221 us; the launch traced here: 217 us
  waiting for transfers between devices  85.5 us (39%)
  Pallas kernels  75.8 us (34%)
  starting transfers between devices  49.8 us (23%)
  local copies, waits for them, and re-layouts  4.68 us (2%)
    pallas_call x9, Pallas kernels, call(): pl.pallas_call(kernel, out_shape=[jax.ShapeDtypeStruct(s, jnp.float32) fo...  75.8 us
    ppermute x11, waiting for transfers between devices, send(): return lax.ppermute(x, 'group', pairs)  60.8 us
    ppermute x11, starting transfers between devices, send(): return lax.ppermute(x, 'group', pairs)  40.9 us
    ppermute x7, waiting for transfers between devices, swap(): return lax.ppermute(x, 'member', [(m, m ^ bits) for m in range(MEMBERS)])  20.2 us
    ppermute x7, starting transfers between devices, swap(): return lax.ppermute(x, 'member', [(m, m ^ bits) for m in range(MEMBERS)])  7.69 us
    ppermute x9, waiting for transfers between devices, other_core(): return lax.ppermute(x, 'col', [(0, 1), (1, 0)])  4.49 us
    unnamed x9, local copies, waits for them, and re-layouts  4.47 us
  transfers between devices with their start and end apart: 27, of which 9 were waited for; matrix products, arithmetic and copies ran while one was open for 0% of the time, Pallas kernels for 22%

commit v1 on v0

--- a/solution.py
+++ b/solution.py
@@ -33,13 +33,27 @@
     return dot_split(split(a), split(b))
 
 
-def leaf_inverse(blocks, background=()):
+def dot_down(a, b):
+    (ah, al), (bh, bl) = split(a), split(b)
+    mul = functools.partial(
+        lax.dot_general,
+        dimension_numbers=(((0,), (0,)), ((), ())),
+        preferred_element_type=jnp.float32,
+    )
+    return mul(ah, bh) + (mul(ah, bl) + mul(al, bh))
+
+
+def reciprocal(x):
+    guess = pl.reciprocal(x, approx=True)
+    return guess * (2.0 - x * guess)
+
+
+def leaf_reduce(block, room, background=()):
     shape = (GROUP, LEAF)
     lane = lax.broadcasted_iota(jnp.int32, shape, 1)
     sub = lax.broadcasted_iota(jnp.int32, shape, 0)
-    count = LEAF // GROUP
-    sets = [[b[GROUP * i : GROUP * (i + 1), :] for i in range(count)] for b in blocks]
     background = list(background)
+    room[0] = block
 
     def row_of(v, p):
         return jnp.broadcast_to(v[p : p + 1, :], shape)
@@ -47,87 +61,71 @@
     def col_of(v, c):
         return jnp.broadcast_to(v[:, c : c + 1], shape)
 
+    def rows_at(i):
+        return slice(GROUP * i, GROUP * (i + 1))
+
     def eliminate(k, order):
         base = GROUP * k
-        vs = [rows[k] for rows in sets]
-        cols = [[col_of(v, base + p) for p in range(GROUP)] for v in vs]
-        for p in range(0, GROUP, 2):
-            first, second = sub == p, sub == p + 1
-            both = first | second
-            for at, c in enumerate(cols):
-                a, b = row_of(c[p], p), row_of(c[p + 1], p)
-                b_low, d = row_of(c[p], p + 1), row_of(c[p + 1], p + 1)
-                det = a * d - b * b_low
-                guess = pl.reciprocal(det, approx=True)
-                refine = 2.0 - det * guess
-                m0 = jnp.where(first, -1.0, jnp.where(second, 0.0, c[p]))
-                m1 = jnp.where(first, 0.0, jnp.where(second, -1.0, c[p + 1]))
-
-                def solved(x):
-                    e0, e1 = row_of(x, p), row_of(x, p + 1)
-                    t0 = d * e0 - b * e1
-                    t1 = a * e1 - b_low * e0
-                    return jnp.where(both, 0.0, x) - ((m0 * t0 + m1 * t1) * guess) * refine
-
-                for q in range(p + 2, GROUP):
-                    c[q] = solved(c[q])
-                unit0 = jnp.where(first, 1.0, 0.0)
-                unit1 = jnp.where(second, 1.0, 0.0)
-                v = jnp.where(lane == base + p, unit0, jnp.where(lane == base + p + 1, unit1, vs[at]))
-                vs[at] = solved(v)
+        v = room[0, rows_at(k), :]
+        cols = [col_of(v, base + p) for p in range(GROUP)]
+        for p in range(GROUP):
+            here = sub == p
+            inv = reciprocal(row_of(cols[p], p))
+            for q in range(p + 1, GROUP):
+                entry = row_of(cols[q], p) * inv
+                cols[q] = jnp.where(here, entry, cols[q] - cols[p] * entry)
+            v = jnp.where(lane == base + p, jnp.where(here, 1.0, 0.0), v)
+            scaled = row_of(v, p) * inv
+            v = jnp.where(here, scaled, v - cols[p] * scaled)
+        room[0, rows_at(k), :] = v
         inside = (lane >= base) & (lane < base + GROUP)
-        pivots = [[row_of(v, p) for p in range(GROUP)] for v in vs]
-        for rows, v in zip(sets, vs):
-            rows[k] = v
+        pivots = [row_of(v, p) for p in range(GROUP)]
         for i in order:
-            for rows, pivot in zip(sets, pivots):
-                w = rows[i]
-                terms = [col_of(w, base + p) * pivot[p] for p in range(GROUP)]
-                while len(terms) > 1:
-                    terms = [x + y for x, y in zip(terms[::2], terms[1::2])]
-                rows[i] = jnp.where(inside, 0.0, w) - terms[0]
+            w = room[0, rows_at(i), :]
+            terms = [col_of(w, base + p) * pivots[p] for p in range(GROUP)]
+            while len(terms) > 1:
+                terms = [x + y for x, y in zip(terms[::2], terms[1::2])]
+            room[0, rows_at(i), :] = jnp.where(inside, 0.0, w) - terms[0]
 
     per = PANEL // GROUP
-    panels = count // per
+    panels = LEAF // PANEL
+    wide_lane = lax.broadcasted_iota(jnp.int32, (PANEL, LEAF), 1)
+    wide_sub = lax.broadcasted_iota(jnp.int32, (PANEL, LEAF), 0)
     for j in range(panels):
+        top = PANEL * j
+        here = slice(top, top + PANEL)
+        start = jnp.where(wide_lane < top, room[0, here, :], 0.0)
+        room[1, here, :] = start + jnp.where(wide_lane == wide_sub + top, 1.0, 0.0)
         panel = list(range(per * j, per * (j + 1)))
-        if j + 1 < panels:
-            eager = list(range(per * (j + 1), per * (j + 2)))
-        else:
-            eager = list(range(per * j))
-        others = [i for i in range(count) if i not in panel and i not in eager]
+        lazy = 2 * (j + 2) <= panels
+        eager = list(range(per * (j + 1), per * (j + 2 if lazy else panels)))
         for k in panel:
             eliminate(k, [i for i in panel if i > k] + [i for i in panel if i < k] + eager)
-        inside = (lane >= PANEL * j) & (lane < PANEL * (j + 1))
-        zeros = jnp.zeros(shape, jnp.float32)
-        if others:
-            for rows in sets:
-                left = jnp.concatenate([jnp.where(inside, rows[i], 0.0) for i in others], axis=0)
-                pivot = jnp.concatenate(
-                    [rows[i] if i in panel else zeros for i in range(count)], axis=0
-                )
-                product = dot3(left, pivot)
-                for at, i in enumerate(others):
-                    kept = jnp.where(inside, 0.0, rows[i])
-                    rows[i] = kept - product[GROUP * at : GROUP * (at + 1), :]
+        room[2, here, :] = jnp.where(wide_lane < top + PANEL, room[0, here, :], 0.0)
+        if lazy:
+            below = slice(top + 2 * PANEL, LEAF)
+            depth = LEAF - top - 2 * PANEL
+            lanes = lax.broadcasted_iota(jnp.int32, (depth, LEAF), 1)
+            inside = (lanes >= top) & (lanes < top + PANEL)
+            w = room[0, below, :]
+            parts = [room[0, here, :]]
+            if top:
+                parts = [jnp.zeros((top, LEAF), jnp.float32)] + parts
+            parts.append(jnp.zeros((LEAF - top - PANEL, LEAF), jnp.float32))
+            product = dot3(jnp.where(inside, w, 0.0), jnp.concatenate(parts, axis=0))
+            room[0, below, :] = jnp.where(inside, 0.0, w) - product
         share = -(-len(background) // (panels - j))
         for part in background[:share]:
             part()
         background = background[share:]
-    return [jnp.concatenate(rows, axis=0) for rows in sets]
-
-
-def inverse_in(work_refs, background=()):
-    n = work_refs[0].shape[-1]
+
+
+def inverse_in(ref, room, background=()):
+    n = ref.shape[-1]
     steps = n // LEAF
     rest = n - LEAF
-    scales = []
-    for ref in work_refs:
-        largest = jnp.max(jnp.max(jnp.abs(ref[0]), axis=0, keepdims=True), axis=1, keepdims=True)
-        scales.append(1.0 / largest)
-        ref[0] = ref[0] * scales[-1]
-
-    def update(ref, src, dst, leaf):
+
+    def update(src, dst, leaf):
         ls = split(leaf)
         cs = [split(ref[src, LEAF * r : LEAF * (r + 1), :LEAF]) for r in range(1, steps)]
         q = dot_split(ls, split(ref[src, :LEAF, LEAF : 2 * LEAF]))
@@ -158,38 +156,25 @@
 
         return pivot, [prepare] + [strip(r) for r in range(1, steps)]
 
-    def body(step, leaves):
+    def leaf():
+        return dot3(room[1].T, room[2])
+
+    def body(step, carry):
         src = lax.rem(step, 2)
-        pivots, parts = [], []
-        for ref, leaf in zip(work_refs, leaves):
-            pivot, own = update(ref, src, 1 - src, leaf)
-            pivots.append(pivot)
-            parts.append(own)
-        return tuple(leaf_inverse(pivots, [part for group in zip(*parts) for part in group]))
-
-    leaves = tuple(leaf_inverse([ref[0, :LEAF, :LEAF] for ref in work_refs], background))
-    leaves = lax.fori_loop(0, steps - 1, body, leaves)
-    for ref, leaf in zip(work_refs, leaves):
-        for part in update(ref, (steps - 1) % 2, steps % 2, leaf)[1]:
-            part()
-    for ref, scale in zip(work_refs, scales):
-        ref[0] = ref[0] * scale
+        pivot, parts = update(src, 1 - src, leaf())
+        leaf_reduce(pivot, room, parts)
+        return carry
+
+    leaf_reduce(ref[0, :LEAF, :LEAF], room, background)
+    lax.fori_loop(0, steps - 1, body, 0)
+    for part in update((steps - 1) % 2, steps % 2, leaf())[1]:
+        part()
 
 
 def plus_diagonal(matrix, row):
     shape = matrix.shape
     here = lax.broadcasted_iota(jnp.int32, shape, 0) == lax.broadcasted_iota(jnp.int32, shape, 1)
     return matrix + jnp.where(here, jnp.broadcast_to(row, shape), 0.0)
-
-
-def dot_down(a, b):
-    (ah, al), (bh, bl) = split(a), split(b)
-    mul = functools.partial(
-        lax.dot_general,
-        dimension_numbers=(((0,), (0,)), ((), ())),
-        preferred_element_type=jnp.float32,
-    )
-    return mul(ah, bh) + (mul(ah, bl) + mul(al, bh))
 
 
 RIGHT, LAST, COL, MEMBER, SETTLED, PLANE = range(6)
@@ -225,7 +210,7 @@
 
 def first_kernel(flags, *refs):
     pieces = refs[:10]
-    bonds, inverse, placed, work = refs[10:]
+    bonds, inverse, placed, work, room = refs[10:]
     width = inverse.shape[0]
     right = flags[RIGHT]
     place_bonds(flags, pieces, placed)
@@ -238,7 +223,7 @@
     work[0] = plus_diagonal(
         bonds[side, :width, :] + bonds[side + 1, :width, :], bonds[side + 1, width : width + 1, :]
     )
-    inverse_in([work])
+    inverse_in(work, room)
     inverse[...] = work[0]
 
 
@@ -249,7 +234,7 @@
 
 
 def reduce_kernel(
-    flags, bonds, mine, other, i2, y10, y12, y32, y3i, yo, yi, goi, gio, mo, mi, mi_half, work_a, work_b
+    flags, bonds, mine, other, i2, y10, y12, y32, y3i, yo, yi, goi, gio, mo, mi, mi_half, work_a, work_b, room
 ):
     width = i2.shape[0]
 
@@ -283,7 +268,7 @@
     def from_o():
         work_b[1] = dot_split(split(y10[...]), c1)
 
-    inverse_in([work_a], [ends_i, ends_o, from_i, from_o])
+    inverse_in(work_a, room, [ends_i, ends_o, from_i, from_o])
     i2[...] = work_a[0]
     q2 = split(i2[...])
     sm = split(mass2)
@@ -322,12 +307,12 @@
     return jnp.concatenate([jnp.where(first, a, b), jnp.where(first, b, a)], axis=1)
 
 
-def chain_kernel(planes, flags, goi, gio, mo, mi, mine, other, new_half, si, y, work):
+def chain_kernel(planes, flags, goi, gio, mo, mi, mine, other, new_half, si, y, work, room):
     @pl.when((flags[PLANE] == planes[0]) | (flags[PLANE] == planes[1]))
     def _():
         mass_o = mo[...] + whole(flags, mine, other)
         work[0] = goi[...] + mass_o
-        inverse_in([work])
+        inverse_in(work, room)
         si[...] = work[0]
         y[...] = dot3(gio[...], si[...])
         work[0] = mi[...] + dot3(y[...], mass_o)
@@ -335,13 +320,13 @@
 
 
 def root_first_kernel(
-    root, flags, goi, gio, mo, mi, o_mine, o_other, i_mine, i_other, inv_i, y, left, work
+    root, flags, goi, gio, mo, mi, o_mine, o_other, i_mine, i_other, inv_i, y, left, work, room
 ):
     @pl.when(flags[PLANE] == root)
     def _():
         mass_i = mi[...] + whole(flags, i_mine, i_other)
         work[0] = gio[...] + mass_i
-        inverse_in([work])
+        inverse_in(work, room)
         inv_i[...] = work[0]
         y[...] = dot3(goi[...], inv_i[...])
         mass_o = mo[...] + whole(flags, o_mine, o_other)
@@ -349,7 +334,7 @@
 
 
 def root_last_kernel(
-    root, flags, inv_i, y, left, ro, ro_in, ri, ri_in, xo, xi, work, inner, outer
+    root, flags, inv_i, y, left, ro, ro_in, ri, ri_in, xo, xi, work, room, inner, outer
 ):
     @pl.when(flags[PLANE] == root)
     def _():
@@ -360,7 +345,7 @@
             inner[...] = dot_split(split(inv_i[...]), s)
             outer[...] = ro[...] + ro_in[...] + dot_split(split(y[...]), s)
 
-        inverse_in([work], [columns])
+        inverse_in(work, room, [columns])
         xo[...] = dot3(work[0], outer[...])
         xi[...] = inner[...] + dot_down(y[...], xo[...])
 
@@ -546,13 +531,14 @@
     square = (width, width)
     block = (width, modes)
     panel = (width, half)
-    room = (2, width, width)
+    work = (2, width, width)
+    room = (3, LEAF, LEAF)
     unit_flops = 6 * width**3
     bonds, p_mine = call(
         first_kernel,
         [flags, *pieces],
         [(MEMBERS, width + GROUP, width), square],
-        [(MEMBERS, width + GROUP, width), room],
+        [(MEMBERS, width + GROUP, width), work, room],
         20 * unit_flops,
     )
     p_other = other_core(p_mine)
@@ -562,7 +548,7 @@
         reduce_kernel,
         [flags, bonds, p_mine, p_other],
         [square] * 11 + [panel],
-        [room, room],
+        [work, work, room],
         30 * unit_flops,
     )
     first = [(groups - 1, groups - 2)]
@@ -582,7 +568,7 @@
             functools.partial(chain_kernel, (t, groups - 2 - t)),
             [flags, goi, gio, mo, mi, into_o, other_core(into_o)],
             [panel, square, square],
-            [room],
+            [work, room],
             20 * unit_flops,
         )
         upward = [(t, t + 1)]
@@ -604,7 +590,7 @@
         functools.partial(root_first_kernel, middle - 1),
         [flags, goi, gio, mo, mi, into_o, other_core(into_o), into_i, other_core(into_i)],
         [square] * 3,
-        [room],
+        [work, room],
         20 * unit_flops,
     )
     last_y, last_vo = (send(after(part, inv_i), [(groups - 2, groups - 1)]) for part in steps[0])
@@ -612,7 +598,7 @@
         functools.partial(root_last_kernel, middle - 1),
         [flags, inv_i, y, left, ro, ro_in, ri, ri_in],
         [block] * 2,
-        [room, block, block],
+        [work, room, block, block],
         20 * unit_flops,
     )
     for t in reversed(range(1, middle - 1)):

time: 221 us -> 246 us (1.11)
  the two profiles are of different devices: /device:TPU:28 before, /device:TPU:24 now
where the time goes in v1:
time: 246 us; the launch traced here: 242 us
  waiting for transfers between devices  94.4 us (38%)
  Pallas kernels  85.5 us (35%)
  starting transfers between devices  56.9 us (23%)
  local copies, waits for them, and re-layouts  4.68 us (2%)
    pallas_call x9, Pallas kernels, call(): pl.pallas_call(kernel, out_shape=[jax.ShapeDtypeStruct(s, jnp.float32) fo...  85.5 us
    ppermute x11, waiting for transfers between devices, send(): return lax.ppermute(x, 'group', pairs)  71.8 us
    ppermute x11, starting transfers between devices, send(): return lax.ppermute(x, 'group', pairs)  46 us
    ppermute x7, waiting for transfers between devices, swap(): return lax.ppermute(x, 'member', [(m, m ^ bits) for m in range(MEMBERS)])  18.1 us
    ppermute x7, starting transfers between devices, swap(): return lax.ppermute(x, 'member', [(m, m ^ bits) for m in range(MEMBERS)])  9.73 us
  transfers between devices with their start and end apart: 27, of which 9 were waited for; matrix products, arithmetic and copies ran while one was open for 0% of the time, Pallas kernels for 21%

profile of v1, /device:TPU:24, one launch (start us, length us, event | category | flops | bytes accessed | tf_op | source)
XLA Modules:
  0.0 242.0 jit_solution(6621344700487110638)
XLA Ops:
  0.0 0.8 copy.6
  0.9 1.0 copy-done
  3.2 1.6 collective-permute-start.1
  4.8 1.5 collective-permute-start
  6.3 10.8 %collective-permute-done.1.refs_2_ = f32[520,256]{1,0:T(8,128)S(1)} collective-permute-done((f32[520,256]{1,0:T(8,128)S(1)}, f32[520,256]{1,0:T(8,128)S(1)}, u32[]{:S(2)}, u32[]{:S(2)}) %collective-permute-start.1) | collective-permute-done | bytes 532512 | tf_op jit(solution)/shard_map/ppermute | solution.py:501
  17.1 1.6 collective-permute-start.3
  19.2 1.6 collective-permute-start.2
  20.8 3.7 %collective-permute-done.3.refs_4_ = f32[264,256]{1,0:T(8,128)S(1)} collective-permute-done((f32[264,256]{1,0:T(8,128)S(1)}, f32[264,256]{1,0:T(8,128)S(1)}, u32[]{:S(2)}, u32[]{:S(2)}) %collective-permute-start.3) | collective-permute-done | bytes 270368 | tf_op jit(solution)/shard_map/ppermute | solution.py:501
  24.5 3.6 %collective-permute-done.2.refs_3_ = f32[256,256]{1,0:T(8,128)} collective-permute-done((f32[256,256]{1,0:T(8,128)S(1)}, f32[256,256]{1,0:T(8,128)}, u32[]{:S(2)}, u32[]{:S(2)}) %collective-permute-start.2) | collective-permute-done | bytes 262176 | tf_op jit(solution)/shard_map/ppermute | solution.py:501
  28.2 1.8 collective-permute-done.7.refs_8_
  30.0 28.5 %shard_map.47 = (f32[4,520,512]{2,1,0:T(8,128)S(1)}, f32[512,512]{1,0:T(8,128)S(1)}) custom-call(s32[6]{0:T(128)S(1)} %stack.39.flags, f32[520,256]{1,0:T(8,128)S(1)} %shard_map.46.refs_0_, f32[520,256]{1,0:T(8,128)S(1)} %collective-permute-done.refs_1_, f32[520,256]{1,0:T(8,128)S(1)} %collective-permute-done.1.refs_2_, ...), custom_call_target="tpu_custom_call" | custom-call | flops 16106127360 | bytes 9568280 | tf_op jit(solution)/shard_map/pallas_call | solution.py:476
  58.5 2.0 copy-done.3
  60.6 1.5 collective-permute-start.10
  62.7 1.4 collective-permute-start.9
  64.1 35.1 %shard_map.48 = (f32[512,512]{1,0:T(8,128)S(1)}, f32[512,512]{1,0:T(8,128)S(1)}, f32[512,512]{1,0:T(8,128)S(1)}, f32[512,512]{1,0:T(8,128)S(1)}, f32[512,512]{1,...) custom-call(s32[6]{0:T(128)S(1)} %stack.39.flags, ...), custom_call_target="tpu_custom_call" | custom-call | flops 24159191040 | bytes 18415640 | tf_op jit(solution)/shard_map/pallas_call | solution.py:476
  99.2 4.9 %collective-permute-start.13 = (f32[512,256]{1,0:T(8,128)S(1)}, f32[512,256]{1,0:T(8,128)S(1)}, u32[]{:S(2)}, u32[]{:S(2)}) collective-permute-start(f32[512,256]{1,0:T(8,128)S(1)} %get-tuple-element.57), channel_id=1, source_target_pairs={{24,16},{25,17},{26,18},{27,19},{28,20},{29,21},{30,22},{31,23}} | collective-permute-start | bytes 1572872 | tf_op jit(solution)/shard_map/ppermute | solution.py:498
  104.2 8.4 %shard_map.49 = (f32[512,128]{1,0:T(8,128)S(1)}, f32[512,512]{1,0:T(8,128)S(1)}, f32[512,512]{1,0:T(8,128)S(1)}, f32[512,128]{1,0:T(8,128)S(1)}, f32[512,128]{1,0:T(8,128)S(1)}) custom-call(s32[6]{0:T(128)S(1)} %stack.39.flags, f32[512,128]{1,0:T(8,128)S(1)} %bitcast.13, f32[512,128]{1,0:T(8,128)S(1)} %collective-permute-done.9.by_x, ...), custom_call_target="tpu_custom_call" | custom-call | flops 4831838208 | bytes 13369368 | tf_op jit(solution)/shard_map/pallas_call | solution.py:476
  112.6 2.4 collective-permute-done.13.mine
  115.0 1.9 collective-permute-done.14.other
  116.9 0.8 shard_map.50
  117.7 0.7 collective-permute-start.18
  119.1 33.1 %collective-permute-start.15 = (f32[512,128]{1,0:T(8,128)S(1)}, f32[512,128]{1,0:T(8,128)S(1)}, u32[]{:S(2)}, u32[]{:S(2)}) collective-permute-start(f32[512,128]{1,0:T(8,128)S(1)} %get-tuple-element.62.ri), channel_id=1, source_target_pairs={{24,16},{25,17},{26,18},{27,19},{28,20},{29,21},{30,22},{31,23}} | collective-permute-start | bytes 786440 | tf_op jit(solution)/shard_map/ppermute | solution.py:498
  152.2 5.8 %collective-permute-done.15.ro_in = f32[512,128]{1,0:T(8,128)S(1)} collective-permute-done((f32[512,128]{1,0:T(8,128)S(1)}, f32[512,128]{1,0:T(8,128)S(1)}, u32[]{:S(2)}, u32[]{:S(2)}) %collective-permute-start.15) | collective-permute-done | bytes 262176 | tf_op jit(solution)/shard_map/ppermute | solution.py:498
  158.0 1.0 shard_map.51
  161.0 0.7 collective-permute-done.17.o_other
  161.7 1.0 shard_map.52
  162.7 1.3 collective-permute-start.20
  164.0 6.5 %shard_map.53 = (f32[512,128]{1,0:T(8,128)S(1)}, f32[512,128]{1,0:T(8,128)S(1)}) custom-call(s32[6]{0:T(128)S(1)} %stack.39.flags, f32[512,512]{1,0:T(8,128)S(1)} %get-tuple-element.67.inv_i, f32[512,512]{1,0:T(8,128)S(1)} %get-tuple-element.70.y, f32[512,512]{1,0:T(8,128)S(1)} %get-tuple-element.71.left, f32[512,128]{1,0:T(8,128)S(1)} %get-tuple-element.58.ro, ...), custom_call_target="tpu_custom_call" | custom-call | flops 16106127360 | bytes 4718616 | tf_op jit(solution)/shard_map/pallas_call | solution.py:476
  171.2 1.3 collective-permute-start.26
  173.2 1.3 collective-permute-start.21
  174.5 63.5 %collective-permute-done.26.in_c = f32[512,128]{1,0:T(8,128)S(1)} collective-permute-done((f32[512,128]{1,0:T(8,128)S(1)}, f32[512,128]{1,0:T(8,128)S(1)}, u32[]{:S(2)}, u32[]{:S(2)}) %collective-permute-start.26) | collective-permute-done | bytes 262176 | tf_op jit(solution)/shard_map/ppermute | solution.py:498
  238.1 3.7 %shard_map.54 = f32[512,128]{1,0:T(8,128)} custom-call(s32[6]{0:T(128)S(1)} %stack.39.flags, f32[512,128]{1,0:T(8,128)S(1)} %get-tuple-element.50.w, f32[512,512]{1,0:T(8,128)S(1)} %get-tuple-element.51.ao, f32[512,512]{1,0:T(8,128)S(1)} %get-tuple-element.52.ai, f32[512,512]{1,0:T(8,128)S(1)} %get-tuple-element.68.y, f32[512,128]{1,0:T(8,128)S(1)} %get-tuple-element.69.vo, ...), custom_call_target="tpu_custom_call" | custom-call | flops 1610612736 | bytes 6553624 | tf_op jit(solution)/shard_map/pallas_call | solution.py:476
  (44 shorter events, 6.8 us)
Async XLA Ops:
  0.9 1.0 copy-start
  1.9 0.7 copy-start.1
  3.2 13.9 %collective-permute-start.1 = (f32[520,256]{1,0:T(8,128)S(1)}, f32[520,256]{1,0:T(8,128)S(1)}, u32[]{:S(2)}, u32[]{:S(2)}) collective-permute-start(f32[520,256]{1,0:T(8,128)S(1)} %shard_map.46.refs_0_), channel_id=1, source_target_pairs={{0,4},{2,6},{4,0},{6,2},{1,5},{3,7},{5,1},{7,3},{8,12},{10,14},{12... | collective-permute-start | bytes 1597448 | tf_op jit(solution)/shard_map/ppermute | solution.py:501
  4.8 13.9 %collective-permute-start = (f32[520,256]{1,0:T(8,128)S(1)}, f32[520,256]{1,0:T(8,128)S(1)}, u32[]{:S(2)}, u32[]{:S(2)}) collective-permute-start(f32[520,256]{1,0:T(8,128)S(1)} %shard_map.46.refs_0_), channel_id=1, source_target_pairs={{0,2},{2,0},{4,6},{6,4},{1,3},{3,1},{5,7},{7,5},{8,10},{10,8},{12,... | collective-permute-start | bytes 1597448 | tf_op jit(solution)/shard_map/ppermute | solution.py:501
  17.1 7.4 %collective-permute-start.3 = (f32[264,256]{1,0:T(8,128)S(1)}, f32[264,256]{1,0:T(8,128)S(1)}, u32[]{:S(2)}, u32[]{:S(2)}) collective-permute-start(f32[264,256]{1,0:T(8,128)S(1)} %slice.9), channel_id=1, source_target_pairs={{0,2},{2,0},{4,6},{6,4},{1,3},{3,1},{5,7},{7,5},{8,10},{10,8},{12,... | collective-permute-start | bytes 811016 | tf_op jit(solution)/shard_map/ppermute | solution.py:501
  18.7 9.5 %collective-permute-start.4 = (f32[520,256]{1,0:T(8,128)S(1)}, f32[520,256]{1,0:T(8,128)S(1)}, u32[]{:S(2)}, u32[]{:S(2)}) collective-permute-start(f32[520,256]{1,0:T(8,128)S(1)} %shard_map.46.refs_0_), channel_id=1, source_target_pairs={{0,1},{1,0},{2,3},{3,2},{4,5},{5,4},{6,7},{7,6},{8,9},{9,8},{10,11... | collective-permute-start | bytes 1597448 | tf_op jit(solution)/shard_map/ppermute | solution.py:504
  18.7 11.3 %collective-permute-start.5 = (f32[520,256]{1,0:T(8,128)S(1)}, f32[520,256]{1,0:T(8,128)S(1)}, u32[]{:S(2)}, u32[]{:S(2)}) collective-permute-start(f32[520,256]{1,0:T(8,128)S(1)} %collective-permute-done.refs_1_), channel_id=1, source_target_pairs={{0,1},{1,0},{2,3},{3,2},{4,5},{5,4},{6,7},{7,6},{8,9},{9,8},{10,11... | collective-permute-start | bytes 1597448 | tf_op jit(solution)/shard_map/ppermute | solution.py:504
  19.2 10.8 %collective-permute-start.6 = (f32[520,256]{1,0:T(8,128)S(1)}, f32[520,256]{1,0:T(8,128)S(1)}, u32[]{:S(2)}, u32[]{:S(2)}) collective-permute-start(f32[520,256]{1,0:T(8,128)S(1)} %collective-permute-done.1.refs_2_), channel_id=1, source_target_pairs={{0,1},{1,0},{2,3},{3,2},{4,5},{5,4},{6,7},{7,6},{8,9},{9,8},{10,11... | collective-permute-start | bytes 1597448 | tf_op jit(solution)/shard_map/ppermute | solution.py:504
  19.2 8.9 %collective-permute-start.2 = (f32[256,256]{1,0:T(8,128)S(1)}, f32[256,256]{1,0:T(8,128)}, u32[]{:S(2)}, u32[]{:S(2)}) collective-permute-start(f32[256,256]{1,0:T(8,128)S(1)} %slice.8), channel_id=1, source_target_pairs={{0,4},{2,6},{4,0},{6,2},{1,5},{3,7},{5,1},{7,3},{8,12},{10,14},{12... | collective-permute-start | bytes 786440 | tf_op jit(solution)/shard_map/ppermute | solution.py:501
  24.5 5.5 %collective-permute-start.8 = (f32[264,256]{1,0:T(8,128)S(1)}, f32[264,256]{1,0:T(8,128)}, u32[]{:S(2)}, u32[]{:S(2)}) collective-permute-start(f32[264,256]{1,0:T(8,128)S(1)} %collective-permute-done.3.refs_4_), channel_id=1, source_target_pairs={{0,1},{1,0},{2,3},{3,2},{4,5},{5,4},{6,7},{7,6},{8,9},{9,8},{10,11... | collective-permute-start | bytes 811016 | tf_op jit(solution)/shard_map/ppermute | solution.py:504
  28.1 1.9 collective-permute-start.7
  28.2 32.4 %copy-start.2 = (f32[1,512,128]{2,1,0:T(8,128)S(1)}, f32[1,512,128]{2,1,0:T(8,128)}, u32[]{:S(2)}) copy-start(f32[1,512,128]{2,1,0:T(8,128)} %param.7) | copy-start | bytes 786436
  58.5 2.0 copy-start.3
  60.5 3.6 %collective-permute-start.12 = (f32[512,512]{1,0:T(8,128)S(1)}, f32[512,512]{1,0:T(8,128)S(1)}, u32[]{:S(2)}, u32[]{:S(2)}) collective-permute-start(f32[512,512]{1,0:T(8,128)S(1)} %get-tuple-element.40.mine.p_mine), channel_id=1, source_target_pairs={{0,1},{1,0},{2,3},{3,2},{4,5},{5,4},{6,7},{7,6},{8,9},{9,8},{10,11... | collective-permute-start | bytes 3145736 | tf_op jit(solution)/shard_map/ppermute | solution.py:504
  60.6 43.6 %collective-permute-start.10 = (f32[512,128]{1,0:T(8,128)S(1)}, f32[512,128]{1,0:T(8,128)S(1)}, u32[]{:S(2)}, u32[]{:S(2)}) collective-permute-start(f32[512,128]{1,0:T(8,128)S(1)} %bitcast.10), channel_id=1, source_target_pairs={{0,4},{2,6},{4,0},{6,2},{1,5},{3,7},{5,1},{7,3},{8,12},{10,14},{12... | collective-permute-start | bytes 786440 | tf_op jit(solution)/shard_map/ppermute | solution.py:501
  62.1 42.0 %collective-permute-start.11 = (f32[512,128]{1,0:T(8,128)S(1)}, f32[512,128]{1,0:T(8,128)S(1)}, u32[]{:S(2)}, u32[]{:S(2)}) collective-permute-start(f32[512,128]{1,0:T(8,128)S(1)} %bitcast.11), channel_id=1, source_target_pairs={{0,6},{2,4},{4,2},{6,0},{1,7},{3,5},{5,3},{7,1},{8,14},{10,12},{12... | collective-permute-start | bytes 786440 | tf_op jit(solution)/shard_map/ppermute | solution.py:501
  62.7 41.5 %collective-permute-start.9 = (f32[512,128]{1,0:T(8,128)S(1)}, f32[512,128]{1,0:T(8,128)S(1)}, u32[]{:S(2)}, u32[]{:S(2)}) collective-permute-start(f32[512,128]{1,0:T(8,128)S(1)} %bitcast.12), channel_id=1, source_target_pairs={{0,2},{2,0},{4,6},{6,4},{1,3},{3,1},{5,7},{7,5},{8,10},{10,8},{12,... | collective-permute-start | bytes 786440 | tf_op jit(solution)/shard_map/ppermute | solution.py:501
  99.2 15.8 %collective-permute-start.13 = (f32[512,256]{1,0:T(8,128)S(1)}, f32[512,256]{1,0:T(8,128)S(1)}, u32[]{:S(2)}, u32[]{:S(2)}) collective-permute-start(f32[512,256]{1,0:T(8,128)S(1)} %get-tuple-element.57), channel_id=1, source_target_pairs={{24,16},{25,17},{26,18},{27,19},{28,20},{29,21},{30,22},{31,23}} | collective-permute-start | bytes 1572872 | tf_op jit(solution)/shard_map/ppermute | solution.py:498
  115.0 1.9 collective-permute-start.14
  117.7 41.4 %collective-permute-start.18 = (f32[512,256]{1,0:T(8,128)S(1)}, f32[512,256]{1,0:T(8,128)S(1)}, u32[]{:S(2)}, u32[]{:S(2)}) collective-permute-start(f32[512,256]{1,0:T(8,128)S(1)} %get-tuple-element.64), channel_id=1, source_target_pairs={{16,8},{17,9},{18,10},{19,11},{20,12},{21,13},{22,14},{23,15}} | collective-permute-start | bytes 1572872 | tf_op jit(solution)/shard_map/ppermute | solution.py:498
  118.4 40.7 %collective-permute-start.16 = (f32[512,256]{1,0:T(8,128)S(1)}, f32[512,256]{1,0:T(8,128)S(1)}, u32[]{:S(2)}, u32[]{:S(2)}) collective-permute-start(f32[512,256]{1,0:T(8,128)S(1)} %get-tuple-element.64), channel_id=1, source_target_pairs={{0,8},{1,9},{2,10},{3,11},{4,12},{5,13},{6,14},{7,15}} | collective-permute-start | bytes 1572872 | tf_op jit(solution)/shard_map/ppermute | solution.py:498
  119.1 38.9 %collective-permute-start.15 = (f32[512,128]{1,0:T(8,128)S(1)}, f32[512,128]{1,0:T(8,128)S(1)}, u32[]{:S(2)}, u32[]{:S(2)}) collective-permute-start(f32[512,128]{1,0:T(8,128)S(1)} %get-tuple-element.62.ri), channel_id=1, source_target_pairs={{24,16},{25,17},{26,18},{27,19},{28,20},{29,21},{30,22},{31,23}} | collective-permute-start | bytes 786440 | tf_op jit(solution)/shard_map/ppermute | solution.py:498
  159.0 2.0 collective-permute-start.19
  159.1 2.6 %collective-permute-start.17 = (f32[512,256]{1,0:T(8,128)S(1)}, f32[512,256]{1,0:T(8,128)S(1)}, u32[]{:S(2)}, u32[]{:S(2)}) collective-permute-start(f32[512,256]{1,0:T(8,128)S(1)} %collective-permute-done.16.o_mine), channel_id=1, source_target_pairs={{0,1},{1,0},{2,3},{3,2},{4,5},{5,4},{6,7},{7,6},{8,9},{9,8},{10,11... | collective-permute-start | bytes 1572872 | tf_op jit(solution)/shard_map/ppermute | solution.py:504
  159.6 4.4 %collective-permute-start.22 = (f32[512,128]{1,0:T(8,128)S(1)}, f32[512,128]{1,0:T(8,128)S(1)}, u32[]{:S(2)}, u32[]{:S(2)}) collective-permute-start(f32[512,128]{1,0:T(8,128)S(1)} %get-tuple-element.72), channel_id=1, source_target_pairs={{0,8},{1,9},{2,10},{3,11},{4,12},{5,13},{6,14},{7,15}} | collective-permute-start | bytes 786440 | tf_op jit(solution)/shard_map/ppermute | solution.py:498
  160.3 3.7 %collective-permute-start.23 = (f32[512,128]{1,0:T(8,128)S(1)}, f32[512,128]{1,0:T(8,128)S(1)}, u32[]{:S(2)}, u32[]{:S(2)}) collective-permute-start(f32[512,128]{1,0:T(8,128)S(1)} %get-tuple-element.72), channel_id=1, source_target_pairs={{16,8},{17,9},{18,10},{19,11},{20,12},{21,13},{22,14},{23,15}} | collective-permute-start | bytes 786440 | tf_op jit(solution)/shard_map/ppermute | solution.py:498
  162.7 75.4 %collective-permute-start.20 = (f32[512,512]{1,0:T(8,128)S(1)}, f32[512,512]{1,0:T(8,128)S(1)}, u32[]{:S(2)}, u32[]{:S(2)}) collective-permute-start(f32[512,512]{1,0:T(8,128)S(1)} %get-tuple-element.68.y), channel_id=1, source_target_pairs={{16,24},{17,25},{18,26},{19,27},{20,28},{21,29},{22,30},{23,31}} | collective-permute-start | bytes 3145736 | tf_op jit(solution)/shard_map/ppermute | solution.py:498
  170.5 4.0 %collective-permute-start.25 = (f32[512,128]{1,0:T(8,128)S(1)}, f32[512,128]{1,0:T(8,128)S(1)}, u32[]{:S(2)}, u32[]{:S(2)}) collective-permute-start(f32[512,128]{1,0:T(8,128)S(1)} %get-tuple-element.74.xi), channel_id=1, source_target_pairs={{8,16},{9,17},{10,18},{11,19},{12,20},{13,21},{14,22},{15,23}} | collective-permute-start | bytes 786440 | tf_op jit(solution)/shard_map/ppermute | solution.py:498
  171.2 66.8 %collective-permute-start.26 = (f32[512,128]{1,0:T(8,128)S(1)}, f32[512,128]{1,0:T(8,128)S(1)}, u32[]{:S(2)}, u32[]{:S(2)}) collective-permute-start(f32[512,128]{1,0:T(8,128)S(1)} %get-tuple-element.74.xi), channel_id=1, source_target_pairs={{8,24},{9,25},{10,26},{11,27},{12,28},{13,29},{14,30},{15,31}} | collective-permute-start | bytes 786440 | tf_op jit(solution)/shard_map/ppermute | solution.py:498
  172.5 2.0 collective-permute-start.24
  173.2 64.9 %collective-permute-start.21 = (f32[512,128]{1,0:T(8,128)S(1)}, f32[512,128]{1,0:T(8,128)S(1)}, u32[]{:S(2)}, u32[]{:S(2)}) collective-permute-start(f32[512,128]{1,0:T(8,128)S(1)} %get-tuple-element.69.vo), channel_id=1, source_target_pairs={{16,24},{17,25},{18,26},{19,27},{20,28},{21,29},{22,30},{23,31}} | collective-permute-start | bytes 786440 | tf_op jit(solution)/shard_map/ppermute | solution.py:498

commit v2 on v0

--- a/solution.py
+++ b/solution.py
@@ -11,7 +11,6 @@
 
 MEMBERS = 4
 SPARE_BYTES = 16 * 1024 * 1024
-
 LEAF = 128
 PANEL = 32
 GROUP = 8
@@ -31,6 +30,11 @@
 
 def dot3(a, b):
     return dot_split(split(a), split(b))
+
+
+def reciprocal(x):
+    guess = pl.reciprocal(x, approx=True)
+    return guess * (2.0 - x * guess)
 
 
 def leaf_inverse(blocks, background=()):
@@ -51,30 +55,18 @@
         base = GROUP * k
         vs = [rows[k] for rows in sets]
         cols = [[col_of(v, base + p) for p in range(GROUP)] for v in vs]
-        for p in range(0, GROUP, 2):
-            first, second = sub == p, sub == p + 1
-            both = first | second
-            for at, c in enumerate(cols):
-                a, b = row_of(c[p], p), row_of(c[p + 1], p)
-                b_low, d = row_of(c[p], p + 1), row_of(c[p + 1], p + 1)
-                det = a * d - b * b_low
-                guess = pl.reciprocal(det, approx=True)
-                refine = 2.0 - det * guess
-                m0 = jnp.where(first, -1.0, jnp.where(second, 0.0, c[p]))
-                m1 = jnp.where(first, 0.0, jnp.where(second, -1.0, c[p + 1]))
-
-                def solved(x):
-                    e0, e1 = row_of(x, p), row_of(x, p + 1)
-                    t0 = d * e0 - b * e1
-                    t1 = a * e1 - b_low * e0
-                    return jnp.where(both, 0.0, x) - ((m0 * t0 + m1 * t1) * guess) * refine
-
-                for q in range(p + 2, GROUP):
-                    c[q] = solved(c[q])
-                unit0 = jnp.where(first, 1.0, 0.0)
-                unit1 = jnp.where(second, 1.0, 0.0)
-                v = jnp.where(lane == base + p, unit0, jnp.where(lane == base + p + 1, unit1, vs[at]))
-                vs[at] = solved(v)
+        for p in range(GROUP):
+            here = sub == p
+            unit = jnp.where(here, 1.0, 0.0)
+            invs = [reciprocal(row_of(c[p], p)) for c in cols]
+            for q in range(p + 1, GROUP):
+                for c, inv in zip(cols, invs):
+                    entry = row_of(c[q], p) * inv
+                    c[q] = jnp.where(here, entry, c[q] - c[p] * entry)
+            for at, (c, inv) in enumerate(zip(cols, invs)):
+                v = jnp.where(lane == base + p, unit, vs[at])
+                scaled = row_of(v, p) * inv
+                vs[at] = jnp.where(here, scaled, v - c[p] * scaled)
         inside = (lane >= base) & (lane < base + GROUP)
         pivots = [[row_of(v, p) for p in range(GROUP)] for v in vs]
         for rows, v in zip(sets, vs):
@@ -121,11 +113,6 @@
     n = work_refs[0].shape[-1]
     steps = n // LEAF
     rest = n - LEAF
-    scales = []
-    for ref in work_refs:
-        largest = jnp.max(jnp.max(jnp.abs(ref[0]), axis=0, keepdims=True), axis=1, keepdims=True)
-        scales.append(1.0 / largest)
-        ref[0] = ref[0] * scales[-1]
 
     def update(ref, src, dst, leaf):
         ls = split(leaf)
@@ -172,8 +159,6 @@
     for ref, leaf in zip(work_refs, leaves):
         for part in update(ref, (steps - 1) % 2, steps % 2, leaf)[1]:
             part()
-    for ref, scale in zip(work_refs, scales):
-        ref[0] = ref[0] * scale
 
 
 def plus_diagonal(matrix, row):
@@ -297,7 +282,7 @@
         y3i[...] * m3 + dot_split(si, sm) + back * jnp.where(flags[LAST] == 1, 1.0, 0.0),
         m0 * (1.0 - left_on),
     )
-    keep_half(flags, mi, mi_half)
+    pack_half(flags, mi, mi_half)
 
     @pl.when(flags[LAST] == 0)
     def _():
@@ -311,15 +296,27 @@
         yo[...] = jnp.zeros_like(yo)
 
 
-def keep_half(flags, full, half_ref):
-    half = half_ref.shape[1]
-    half_ref[...] = jnp.where(flags[COL] == 0, full[:, :half], full[:, half:])
+def pack_half(flags, full, packed):
+    half = packed.shape[1]
+    middle = half + half // 2
+    first = flags[COL] == 0
+    packed[:half, :] = jnp.where(first, full[:half, :half], full[half:, half:])
+    packed[half:, :] = jnp.where(first, full[half:middle, :half], full[middle:, :half])
 
 
 def whole(flags, mine, other):
+    half = mine.shape[1]
     first = flags[COL] == 0
     a, b = mine[...], other[...]
-    return jnp.concatenate([jnp.where(first, a, b), jnp.where(first, b, a)], axis=1)
+    low, high = jnp.where(first, a, b), jnp.where(first, b, a)
+    corner = jnp.concatenate([low[half:], high[half:]], axis=0)
+    return jnp.concatenate(
+        [
+            jnp.concatenate([low[:half], corner.T], axis=1),
+            jnp.concatenate([corner, high[:half]], axis=1),
+        ],
+        axis=0,
+    )
 
 
 def chain_kernel(planes, flags, goi, gio, mo, mi, mine, other, new_half, si, y, work):
@@ -331,7 +328,7 @@
         si[...] = work[0]
         y[...] = dot3(gio[...], si[...])
         work[0] = mi[...] + dot3(y[...], mass_o)
-        keep_half(flags, work.at[0], new_half)
+        pack_half(flags, work.at[0], new_half)
 
 
 def root_first_kernel(
@@ -545,7 +542,7 @@
     )
     square = (width, width)
     block = (width, modes)
-    panel = (width, half)
+    packed = (half + half // 2, half)
     room = (2, width, width)
     unit_flops = 6 * width**3
     bonds, p_mine = call(
@@ -556,38 +553,41 @@
         20 * unit_flops,
     )
     p_other = other_core(p_mine)
-    source = after(sources[0], p_mine)
-    rhs = [source, swap(source, 1), swap(source, 2), swap(source, 3)]
     i2, y10, y12, y32, y3i, yo, yi, goi, gio, mo, mi, mi_half = call(
         reduce_kernel,
         [flags, bonds, p_mine, p_other],
-        [square] * 11 + [panel],
+        [square] * 11 + [packed],
         [room, room],
         30 * unit_flops,
     )
     first = [(groups - 1, groups - 2)]
     into_o = send(mi_half, first)
-    w, ao, ai, ro, ri = call(
-        columns_kernel,
-        [flags, *rhs, p_mine, p_other, i2, y10, y12, y32, y3i, yo, yi],
-        [block, square, square, block, block],
-        [(MEMBERS, width, modes)],
-        flops=6 * unit_flops,
-    )
-    ro_in = send(ri, first)
-    into_o = after(into_o, ro)
+    source = after(sources[0], mi_half)
+    rhs = [source, swap(source, 1), swap(source, 2), swap(source, 3)]
     steps = []
     for t in range(middle - 1):
         new_half, si, y = call(
             functools.partial(chain_kernel, (t, groups - 2 - t)),
             [flags, goi, gio, mo, mi, into_o, other_core(into_o)],
-            [panel, square, square],
+            [packed, square, square],
             [room],
             20 * unit_flops,
         )
         upward = [(t, t + 1)]
         downward = [(groups - 2 - t, groups - 3 - t)]
         from_left, from_right = send(new_half, upward), send(new_half, downward)
+        if t == 0:
+            w, ao, ai, ro, ri = call(
+                columns_kernel,
+                [
+                    *[flags, after(rhs[0], new_half), *rhs[1:], p_mine, p_other],
+                    *[i2, y10, y12, y32, y3i, yo, yi],
+                ],
+                [block, square, square, block, block],
+                [(MEMBERS, width, modes)],
+                flops=6 * unit_flops,
+            )
+            ro_in = send(ri, first)
         new_ri, vo = call(
             chain_columns_kernel, [y, si, ro, ro_in, ri], [block] * 2, flops=unit_flops
         )

time: 221 us -> 203 us (0.919)
  the two profiles are of different devices: /device:TPU:28 before, /device:TPU:16 now
where the time goes in v2:
time: 203 us; the launch traced here: 199 us
  Pallas kernels  89.3 us (44%)
  waiting for transfers between devices  81.4 us (40%)
  starting transfers between devices  22.8 us (11%)
  local copies, waits for them, and re-layouts  4.68 us (2%)
    pallas_call x9, Pallas kernels, call(): pl.pallas_call(kernel, out_shape=[jax.ShapeDtypeStruct(s, jnp.float32) fo...  89.3 us
    ppermute x11, waiting for transfers between devices, send(): return lax.ppermute(x, 'group', pairs)  58.9 us
    ppermute x7, waiting for transfers between devices, swap(): return lax.ppermute(x, 'member', [(m, m ^ bits) for m in range(MEMBERS)])  18.1 us
    ppermute x11, starting transfers between devices, send(): return lax.ppermute(x, 'group', pairs)  11.9 us
    ppermute x7, starting transfers between devices, swap(): return lax.ppermute(x, 'member', [(m, m ^ bits) for m in range(MEMBERS)])  9.71 us
    unnamed x9, local copies, waits for them, and re-layouts  4.47 us
    ppermute x9, waiting for transfers between devices, other_core(): return lax.ppermute(x, 'col', [(0, 1), (1, 0)])  4.33 us
  transfers between devices with their start and end apart: 27, of which 9 were waited for; matrix products, arithmetic and copies ran while one was open for 0% of the time, Pallas kernels for 17%

profile of v2, /device:TPU:16, one launch (start us, length us, event | category | flops | bytes accessed | tf_op | source)
XLA Modules:
  0.0 198.6 jit_solution(12752594282530220488)
XLA Ops:
  0.9 1.0 copy-done
  3.2 1.6 collective-permute-start.1
  4.8 1.5 collective-permute-start
  6.3 10.8 %collective-permute-done.1.refs_2_ = f32[520,256]{1,0:T(8,128)S(1)} collective-permute-done((f32[520,256]{1,0:T(8,128)S(1)}, f32[520,256]{1,0:T(8,128)S(1)}, u32[]{:S(2)}, u32[]{:S(2)}) %collective-permute-start.1) | collective-permute-done | bytes 532512 | tf_op jit(solution)/shard_map/ppermute | solution.py:513
  17.1 1.6 collective-permute-start.3
  19.2 1.6 collective-permute-start.2
  20.8 3.7 %collective-permute-done.3.refs_4_ = f32[264,256]{1,0:T(8,128)S(1)} collective-permute-done((f32[264,256]{1,0:T(8,128)S(1)}, f32[264,256]{1,0:T(8,128)S(1)}, u32[]{:S(2)}, u32[]{:S(2)}) %collective-permute-start.3) | collective-permute-done | bytes 270368 | tf_op jit(solution)/shard_map/ppermute | solution.py:513
  24.5 3.6 %collective-permute-done.2.refs_3_ = f32[256,256]{1,0:T(8,128)} collective-permute-done((f32[256,256]{1,0:T(8,128)S(1)}, f32[256,256]{1,0:T(8,128)}, u32[]{:S(2)}, u32[]{:S(2)}) %collective-permute-start.2) | collective-permute-done | bytes 262176 | tf_op jit(solution)/shard_map/ppermute | solution.py:513
  28.2 1.8 collective-permute-done.7.refs_8_
  30.0 19.9 %shard_map.47 = (f32[4,520,512]{2,1,0:T(8,128)S(1)}, f32[512,512]{1,0:T(8,128)S(1)}) custom-call(s32[6]{0:T(128)S(1)} %stack.39.flags, f32[520,256]{1,0:T(8,128)S(1)} %shard_map.46.refs_0_, f32[520,256]{1,0:T(8,128)S(1)} %collective-permute-done.refs_1_, f32[520,256]{1,0:T(8,128)S(1)} %collective-permute-done.1.refs_2_, ...), custom_call_target="tpu_custom_call" | custom-call | flops 16106127360 | bytes 9568280 | tf_op jit(solution)/shard_map/pallas_call | solution.py:488
  50.0 2.0 copy-done.3
  52.1 2.5 %collective-permute-done.9.other.p_other = f32[512,512]{1,0:T(8,128)S(1)} collective-permute-done((f32[512,512]{1,0:T(8,128)S(1)}, f32[512,512]{1,0:T(8,128)S(1)}, u32[]{:S(2)}, u32[]{:S(2)}) %collective-permute-start.9) | collective-permute-done | bytes 1048608 | tf_op jit(solution)/shard_map/ppermute | solution.py:516
  54.6 31.2 %shard_map.48 = (f32[512,512]{1,0:T(8,128)S(1)}, f32[512,512]{1,0:T(8,128)S(1)}, f32[512,512]{1,0:T(8,128)S(1)}, f32[512,512]{1,0:T(8,128)S(1)}, f32[512,512]{1,...) custom-call(s32[6]{0:T(128)S(1)} %stack.39.flags, ...), custom_call_target="tpu_custom_call" | custom-call | flops 24159191040 | bytes 18284568 | tf_op jit(solution)/shard_map/pallas_call | solution.py:488
  85.8 1.3 collective-permute-start.10
  87.1 11.8 %collective-permute-done.10.mine = f32[384,256]{1,0:T(8,128)S(1)} collective-permute-done((f32[384,256]{1,0:T(8,128)S(1)}, f32[384,256]{1,0:T(8,128)S(1)}, u32[]{:S(2)}, u32[]{:S(2)}) %collective-permute-start.10) | collective-permute-done | bytes 393248 | tf_op jit(solution)/shard_map/ppermute | solution.py:510
  98.9 1.5 collective-permute-start.14
  101.0 1.4 collective-permute-start.12
  102.4 20.3 %shard_map.49 = (f32[384,256]{1,0:T(8,128)S(1)}, f32[512,512]{1,0:T(8,128)S(1)}, f32[512,512]{1,0:T(8,128)S(1)}) custom-call(s32[6]{0:T(128)S(1)} %stack.39.flags, f32[512,512]{1,0:T(8,128)S(1)} %get-tuple-element.44.goi, f32[512,512]{1,0:T(8,128)S(1)} %get-tuple-element.45.gio, f32[512,512]{1,0:T(8,128)S(1)} %get-tuple-element.46.mo, ...), custom_call_target="tpu_custom_call" | custom-call | flops 16106127360 | bytes 7471128 | tf_op jit(solution)/shard_map/pallas_call | solution.py:488
  122.7 1.3 collective-permute-start.18
  124.7 8.3 %shard_map.50 = (f32[512,128]{1,0:T(8,128)S(1)}, f32[512,512]{1,0:T(8,128)S(1)}, f32[512,512]{1,0:T(8,128)S(1)}, f32[512,128]{1,0:T(8,128)S(1)}, f32[512,128]{1,0:T(8,128)S(1)}) custom-call(s32[6]{0:T(128)S(1)} %stack.39.flags, f32[512,128]{1,0:T(8,128)S(1)} %bitcast.13, f32[512,128]{1,0:T(8,128)S(1)} %collective-permute-done.12.by_x, ...), custom_call_target="tpu_custom_call" | custom-call | flops 4831838208 | bytes 13369368 | tf_op jit(solution)/shard_map/pallas_call | solution.py:488
  133.1 1.3 collective-permute-start.15
  134.4 8.5 %collective-permute-done.15.ro_in = f32[512,128]{1,0:T(8,128)S(1)} collective-permute-done((f32[512,128]{1,0:T(8,128)S(1)}, f32[512,128]{1,0:T(8,128)S(1)}, u32[]{:S(2)}, u32[]{:S(2)}) %collective-permute-start.15) | collective-permute-done | bytes 262176 | tf_op jit(solution)/shard_map/ppermute | solution.py:510
  142.9 1.0 shard_map.51
  144.5 1.3 collective-permute-start.23
  146.5 1.0 shard_map.52
  147.4 1.3 collective-permute-start.21
  148.8 1.4 collective-permute-start.20
  150.1 1.7 collective-permute-done.23.ri_in
  151.8 3.2 %shard_map.53 = (f32[512,128]{1,0:T(8,128)S(1)}, f32[512,128]{1,0:T(8,128)S(1)}) custom-call(s32[6]{0:T(128)S(1)} %stack.39.flags, f32[512,512]{1,0:T(8,128)S(1)} %get-tuple-element.67.inv_i, f32[512,512]{1,0:T(8,128)S(1)} %get-tuple-element.70.y, f32[512,512]{1,0:T(8,128)S(1)} %get-tuple-element.71.left, f32[512,128]{1,0:T(8,128)S(1)} %get-tuple-element.62.ro, ...), custom_call_target="tpu_custom_call" | custom-call | flops 16106127360 | bytes 4718616 | tf_op jit(solution)/shard_map/pallas_call | solution.py:488
  156.4 1.3 collective-permute-start.25
  157.7 37.0 %collective-permute-done.25.in_b = f32[512,128]{1,0:T(8,128)S(1)} collective-permute-done((f32[512,128]{1,0:T(8,128)S(1)}, f32[512,128]{1,0:T(8,128)S(1)}, u32[]{:S(2)}, u32[]{:S(2)}) %collective-permute-start.25) | collective-permute-done | bytes 262176 | tf_op jit(solution)/shard_map/ppermute | solution.py:510
  194.7 3.7 %shard_map.54 = f32[512,128]{1,0:T(8,128)} custom-call(s32[6]{0:T(128)S(1)} %stack.39.flags, f32[512,128]{1,0:T(8,128)S(1)} %get-tuple-element.57.w, f32[512,512]{1,0:T(8,128)S(1)} %get-tuple-element.58.ao, f32[512,512]{1,0:T(8,128)S(1)} %get-tuple-element.59.ai, f32[512,512]{1,0:T(8,128)S(1)} %get-tuple-element.68.y, f32[512,128]{1,0:T(8,128)S(1)} %get-tuple-element.69.vo, ...), custom_call_target="tpu_custom_call" | custom-call | flops 1610612736 | bytes 6553624 | tf_op jit(solution)/shard_map/pallas_call | solution.py:488
  (44 shorter events, 6.9 us)
Async XLA Ops:
  0.9 1.0 copy-start
  1.9 0.7 copy-start.1
  3.2 13.9 %collective-permute-start.1 = (f32[520,256]{1,0:T(8,128)S(1)}, f32[520,256]{1,0:T(8,128)S(1)}, u32[]{:S(2)}, u32[]{:S(2)}) collective-permute-start(f32[520,256]{1,0:T(8,128)S(1)} %shard_map.46.refs_0_), channel_id=1, source_target_pairs={{0,4},{2,6},{4,0},{6,2},{1,5},{3,7},{5,1},{7,3},{8,12},{10,14},{12... | collective-permute-start | bytes 1597448 | tf_op jit(solution)/shard_map/ppermute | solution.py:513
  4.8 14.4 %collective-permute-start = (f32[520,256]{1,0:T(8,128)S(1)}, f32[520,256]{1,0:T(8,128)S(1)}, u32[]{:S(2)}, u32[]{:S(2)}) collective-permute-start(f32[520,256]{1,0:T(8,128)S(1)} %shard_map.46.refs_0_), channel_id=1, source_target_pairs={{0,2},{2,0},{4,6},{6,4},{1,3},{3,1},{5,7},{7,5},{8,10},{10,8},{12,... | collective-permute-start | bytes 1597448 | tf_op jit(solution)/shard_map/ppermute | solution.py:513
  17.1 7.4 %collective-permute-start.3 = (f32[264,256]{1,0:T(8,128)S(1)}, f32[264,256]{1,0:T(8,128)S(1)}, u32[]{:S(2)}, u32[]{:S(2)}) collective-permute-start(f32[264,256]{1,0:T(8,128)S(1)} %slice.9), channel_id=1, source_target_pairs={{0,2},{2,0},{4,6},{6,4},{1,3},{3,1},{5,7},{7,5},{8,10},{10,8},{12,... | collective-permute-start | bytes 811016 | tf_op jit(solution)/shard_map/ppermute | solution.py:513
  18.7 9.5 %collective-permute-start.4 = (f32[520,256]{1,0:T(8,128)S(1)}, f32[520,256]{1,0:T(8,128)S(1)}, u32[]{:S(2)}, u32[]{:S(2)}) collective-permute-start(f32[520,256]{1,0:T(8,128)S(1)} %shard_map.46.refs_0_), channel_id=1, source_target_pairs={{0,1},{1,0},{2,3},{3,2},{4,5},{5,4},{6,7},{7,6},{8,9},{9,8},{10,11... | collective-permute-start | bytes 1597448 | tf_op jit(solution)/shard_map/ppermute | solution.py:516
  18.7 11.3 %collective-permute-start.6 = (f32[520,256]{1,0:T(8,128)S(1)}, f32[520,256]{1,0:T(8,128)S(1)}, u32[]{:S(2)}, u32[]{:S(2)}) collective-permute-start(f32[520,256]{1,0:T(8,128)S(1)} %collective-permute-done.1.refs_2_), channel_id=1, source_target_pairs={{0,1},{1,0},{2,3},{3,2},{4,5},{5,4},{6,7},{7,6},{8,9},{9,8},{10,11... | collective-permute-start | bytes 1597448 | tf_op jit(solution)/shard_map/ppermute | solution.py:516
  19.2 10.8 %collective-permute-start.5 = (f32[520,256]{1,0:T(8,128)S(1)}, f32[520,256]{1,0:T(8,128)S(1)}, u32[]{:S(2)}, u32[]{:S(2)}) collective-permute-start(f32[520,256]{1,0:T(8,128)S(1)} %collective-permute-done.refs_1_), channel_id=1, source_target_pairs={{0,1},{1,0},{2,3},{3,2},{4,5},{5,4},{6,7},{7,6},{8,9},{9,8},{10,11... | collective-permute-start | bytes 1597448 | tf_op jit(solution)/shard_map/ppermute | solution.py:516
  19.2 8.9 %collective-permute-start.2 = (f32[256,256]{1,0:T(8,128)S(1)}, f32[256,256]{1,0:T(8,128)}, u32[]{:S(2)}, u32[]{:S(2)}) collective-permute-start(f32[256,256]{1,0:T(8,128)S(1)} %slice.8), channel_id=1, source_target_pairs={{0,4},{2,6},{4,0},{6,2},{1,5},{3,7},{5,1},{7,3},{8,12},{10,14},{12... | collective-permute-start | bytes 786440 | tf_op jit(solution)/shard_map/ppermute | solution.py:513
  24.5 5.5 %collective-permute-start.8 = (f32[264,256]{1,0:T(8,128)S(1)}, f32[264,256]{1,0:T(8,128)}, u32[]{:S(2)}, u32[]{:S(2)}) collective-permute-start(f32[264,256]{1,0:T(8,128)S(1)} %collective-permute-done.3.refs_4_), channel_id=1, source_target_pairs={{0,1},{1,0},{2,3},{3,2},{4,5},{5,4},{6,7},{7,6},{8,9},{9,8},{10,11... | collective-permute-start | bytes 811016 | tf_op jit(solution)/shard_map/ppermute | solution.py:516
  28.1 1.9 collective-permute-start.7
  49.9 2.0 %copy-start.3 = (f32[4,520,512]{2,1,0:T(8,128)}, f32[4,520,512]{2,1,0:T(8,128)S(1)}, u32[]{:S(2)}) copy-start(f32[4,520,512]{2,1,0:T(8,128)S(1)} %get-tuple-element.40.bonds) | copy-start | bytes 12779524
  51.9 2.7 %collective-permute-start.9 = (f32[512,512]{1,0:T(8,128)S(1)}, f32[512,512]{1,0:T(8,128)S(1)}, u32[]{:S(2)}, u32[]{:S(2)}) collective-permute-start(f32[512,512]{1,0:T(8,128)S(1)} %get-tuple-element.41.mine.p_mine), channel_id=1, source_target_pairs={{0,1},{1,0},{2,3},{3,2},{4,5},{5,4},{6,7},{7,6},{8,9},{9,8},{10,11... | collective-permute-start | bytes 3145736 | tf_op jit(solution)/shard_map/ppermute | solution.py:516
  54.6 44.3 %copy-start.2 = (f32[1,512,128]{2,1,0:T(8,128)S(1)}, f32[1,512,128]{2,1,0:T(8,128)}, u32[]{:S(2)}) copy-start(f32[1,512,128]{2,1,0:T(8,128)} %param.7) | copy-start | bytes 786436
  85.8 13.1 %collective-permute-start.10 = (f32[384,256]{1,0:T(8,128)S(1)}, f32[384,256]{1,0:T(8,128)S(1)}, u32[]{:S(2)}, u32[]{:S(2)}) collective-permute-start(f32[384,256]{1,0:T(8,128)S(1)} %get-tuple-element.42), channel_id=1, source_target_pairs={{24,16},{25,17},{26,18},{27,19},{28,20},{29,21},{30,22},{31,23}} | collective-permute-start | bytes 1179656 | tf_op jit(solution)/shard_map/ppermute | solution.py:510
  98.9 3.5 %collective-permute-start.11 = (f32[384,256]{1,0:T(8,128)S(1)}, f32[384,256]{1,0:T(8,128)S(1)}, u32[]{:S(2)}, u32[]{:S(2)}) collective-permute-start(f32[384,256]{1,0:T(8,128)S(1)} %collective-permute-done.10.mine), channel_id=1, source_target_pairs={{0,1},{1,0},{2,3},{3,2},{4,5},{5,4},{6,7},{7,6},{8,9},{9,8},{10,11... | collective-permute-start | bytes 1179656 | tf_op jit(solution)/shard_map/ppermute | solution.py:516
  98.9 25.8 %collective-permute-start.14 = (f32[512,128]{1,0:T(8,128)S(1)}, f32[512,128]{1,0:T(8,128)S(1)}, u32[]{:S(2)}, u32[]{:S(2)}) collective-permute-start(f32[512,128]{1,0:T(8,128)S(1)} %bitcast.10), channel_id=1, source_target_pairs={{0,6},{2,4},{4,2},{6,0},{1,7},{3,5},{5,3},{7,1},{8,14},{10,12},{12... | collective-permute-start | bytes 786440 | tf_op jit(solution)/shard_map/ppermute | solution.py:513
  100.4 24.4 %collective-permute-start.13 = (f32[512,128]{1,0:T(8,128)S(1)}, f32[512,128]{1,0:T(8,128)S(1)}, u32[]{:S(2)}, u32[]{:S(2)}) collective-permute-start(f32[512,128]{1,0:T(8,128)S(1)} %bitcast.11), channel_id=1, source_target_pairs={{0,4},{2,6},{4,0},{6,2},{1,5},{3,7},{5,1},{7,3},{8,12},{10,14},{12... | collective-permute-start | bytes 786440 | tf_op jit(solution)/shard_map/ppermute | solution.py:513
  101.0 23.8 %collective-permute-start.12 = (f32[512,128]{1,0:T(8,128)S(1)}, f32[512,128]{1,0:T(8,128)S(1)}, u32[]{:S(2)}, u32[]{:S(2)}) collective-permute-start(f32[512,128]{1,0:T(8,128)S(1)} %bitcast.12), channel_id=1, source_target_pairs={{0,2},{2,0},{4,6},{6,4},{1,3},{3,1},{5,7},{7,5},{8,10},{10,8},{12,... | collective-permute-start | bytes 786440 | tf_op jit(solution)/shard_map/ppermute | solution.py:513
  122.7 21.2 %collective-permute-start.18 = (f32[384,256]{1,0:T(8,128)S(1)}, f32[384,256]{1,0:T(8,128)S(1)}, u32[]{:S(2)}, u32[]{:S(2)}) collective-permute-start(f32[384,256]{1,0:T(8,128)S(1)} %get-tuple-element.48), channel_id=1, source_target_pairs={{16,8},{17,9},{18,10},{19,11},{20,12},{21,13},{22,14},{23,15}} | collective-permute-start | bytes 1179656 | tf_op jit(solution)/shard_map/ppermute | solution.py:510
  124.0 20.0 %collective-permute-start.16 = (f32[384,256]{1,0:T(8,128)S(1)}, f32[384,256]{1,0:T(8,128)S(1)}, u32[]{:S(2)}, u32[]{:S(2)}) collective-permute-start(f32[384,256]{1,0:T(8,128)S(1)} %get-tuple-element.48), channel_id=1, source_target_pairs={{0,8},{1,9},{2,10},{3,11},{4,12},{5,13},{6,14},{7,15}} | collective-permute-start | bytes 1179656 | tf_op jit(solution)/shard_map/ppermute | solution.py:510
  133.1 9.8 %collective-permute-start.15 = (f32[512,128]{1,0:T(8,128)S(1)}, f32[512,128]{1,0:T(8,128)S(1)}, u32[]{:S(2)}, u32[]{:S(2)}) collective-permute-start(f32[512,128]{1,0:T(8,128)S(1)} %get-tuple-element.63.ri), channel_id=1, source_target_pairs={{24,16},{25,17},{26,18},{27,19},{28,20},{29,21},{30,22},{31,23}} | collective-permute-start | bytes 786440 | tf_op jit(solution)/shard_map/ppermute | solution.py:510
  143.9 2.6 %collective-permute-start.19 = (f32[384,256]{1,0:T(8,128)S(1)}, f32[384,256]{1,0:T(8,128)S(1)}, u32[]{:S(2)}, u32[]{:S(2)}) collective-permute-start(f32[384,256]{1,0:T(8,128)S(1)} %collective-permute-done.18.i_mine), channel_id=1, source_target_pairs={{0,1},{1,0},{2,3},{3,2},{4,5},{5,4},{6,7},{7,6},{8,9},{9,8},{10,11... | collective-permute-start | bytes 1179656 | tf_op jit(solution)/shard_map/ppermute | solution.py:516
  144.0 2.5 %collective-permute-start.17 = (f32[384,256]{1,0:T(8,128)S(1)}, f32[384,256]{1,0:T(8,128)S(1)}, u32[]{:S(2)}, u32[]{:S(2)}) collective-permute-start(f32[384,256]{1,0:T(8,128)S(1)} %collective-permute-done.16.o_mine), channel_id=1, source_target_pairs={{0,1},{1,0},{2,3},{3,2},{4,5},{5,4},{6,7},{7,6},{8,9},{9,8},{10,11... | collective-permute-start | bytes 1179656 | tf_op jit(solution)/shard_map/ppermute | solution.py:516
  144.5 7.4 %collective-permute-start.23 = (f32[512,128]{1,0:T(8,128)S(1)}, f32[512,128]{1,0:T(8,128)S(1)}, u32[]{:S(2)}, u32[]{:S(2)}) collective-permute-start(f32[512,128]{1,0:T(8,128)S(1)} %get-tuple-element.72), channel_id=1, source_target_pairs={{16,8},{17,9},{18,10},{19,11},{20,12},{21,13},{22,14},{23,15}} | collective-permute-start | bytes 786440 | tf_op jit(solution)/shard_map/ppermute | solution.py:510
  145.8 6.1 %collective-permute-start.22 = (f32[512,128]{1,0:T(8,128)S(1)}, f32[512,128]{1,0:T(8,128)S(1)}, u32[]{:S(2)}, u32[]{:S(2)}) collective-permute-start(f32[512,128]{1,0:T(8,128)S(1)} %get-tuple-element.72), channel_id=1, source_target_pairs={{0,8},{1,9},{2,10},{3,11},{4,12},{5,13},{6,14},{7,15}} | collective-permute-start | bytes 786440 | tf_op jit(solution)/shard_map/ppermute | solution.py:510
  147.4 10.2 %collective-permute-start.21 = (f32[512,128]{1,0:T(8,128)S(1)}, f32[512,128]{1,0:T(8,128)S(1)}, u32[]{:S(2)}, u32[]{:S(2)}) collective-permute-start(f32[512,128]{1,0:T(8,128)S(1)} %get-tuple-element.69.vo), channel_id=1, source_target_pairs={{16,24},{17,25},{18,26},{19,27},{20,28},{21,29},{22,30},{23,31}} | collective-permute-start | bytes 786440 | tf_op jit(solution)/shard_map/ppermute | solution.py:510
  148.8 45.9 %collective-permute-start.20 = (f32[512,512]{1,0:T(8,128)S(1)}, f32[512,512]{1,0:T(8,128)S(1)}, u32[]{:S(2)}, u32[]{:S(2)}) collective-permute-start(f32[512,512]{1,0:T(8,128)S(1)} %get-tuple-element.68.y), channel_id=1, source_target_pairs={{16,24},{17,25},{18,26},{19,27},{20,28},{21,29},{22,30},{23,31}} | collective-permute-start | bytes 3145736 | tf_op jit(solution)/shard_map/ppermute | solution.py:510
  155.0 2.7 %collective-permute-start.24 = (f32[512,128]{1,0:T(8,128)S(1)}, f32[512,128]{1,0:T(8,128)S(1)}, u32[]{:S(2)}, u32[]{:S(2)}) collective-permute-start(f32[512,128]{1,0:T(8,128)S(1)} %get-tuple-element.73.xo), channel_id=1, source_target_pairs={{8,0},{9,1},{10,2},{11,3},{12,4},{13,5},{14,6},{15,7}} | collective-permute-start | bytes 786440 | tf_op jit(solution)/shard_map/ppermute | solution.py:510
  155.7 2.0 %collective-permute-start.26 = (f32[512,128]{1,0:T(8,128)S(1)}, f32[512,128]{1,0:T(8,128)S(1)}, u32[]{:S(2)}, u32[]{:S(2)}) collective-permute-start(f32[512,128]{1,0:T(8,128)S(1)} %get-tuple-element.74.xi), channel_id=1, source_target_pairs={{8,24},{9,25},{10,26},{11,27},{12,28},{13,29},{14,30},{15,31}} | collective-permute-start | bytes 786440 | tf_op jit(solution)/shard_map/ppermute | solution.py:510
  156.4 38.3 %collective-permute-start.25 = (f32[512,128]{1,0:T(8,128)S(1)}, f32[512,128]{1,0:T(8,128)S(1)}, u32[]{:S(2)}, u32[]{:S(2)}) collective-permute-start(f32[512,128]{1,0:T(8,128)S(1)} %get-tuple-element.74.xi), channel_id=1, source_target_pairs={{8,16},{9,17},{10,18},{11,19},{12,20},{13,21},{14,22},{15,23}} | collective-permute-start | bytes 786440 | tf_op jit(solution)/shard_map/ppermute | solution.py:510

commit v3 on v2

--- a/solution.py
+++ b/solution.py
@@ -12,7 +12,7 @@
 MEMBERS = 4
 SPARE_BYTES = 16 * 1024 * 1024
 LEAF = 128
-PANEL = 32
+PANEL = 16
 GROUP = 8
 
 
@@ -24,8 +24,9 @@
 
 def dot_split(a, b):
     (ah, al), (bh, bl) = a, b
-    mul = functools.partial(jnp.dot, preferred_element_type=jnp.float32)
-    return mul(ah, bh) + (mul(ah, bl) + mul(al, bh))
+    left = jnp.concatenate([ah, ah, al], axis=1)
+    right = jnp.concatenate([bh, bl, bh], axis=0)
+    return jnp.dot(left, right, preferred_element_type=jnp.float32)
 
 
 def dot3(a, b):
@@ -55,19 +56,19 @@
         base = GROUP * k
         vs = [rows[k] for rows in sets]
         cols = [[col_of(v, base + p) for p in range(GROUP)] for v in vs]
+        inside = (lane >= base) & (lane < base + GROUP)
+        unit = jnp.where(lane == sub + base, 1.0, 0.0)
+        vs = [jnp.where(inside, unit, v) for v in vs]
         for p in range(GROUP):
             here = sub == p
-            unit = jnp.where(here, 1.0, 0.0)
             invs = [reciprocal(row_of(c[p], p)) for c in cols]
             for q in range(p + 1, GROUP):
                 for c, inv in zip(cols, invs):
                     entry = row_of(c[q], p) * inv
                     c[q] = jnp.where(here, entry, c[q] - c[p] * entry)
             for at, (c, inv) in enumerate(zip(cols, invs)):
-                v = jnp.where(lane == base + p, unit, vs[at])
-                scaled = row_of(v, p) * inv
-                vs[at] = jnp.where(here, scaled, v - c[p] * scaled)
-        inside = (lane >= base) & (lane < base + GROUP)
+                scaled = row_of(vs[at], p) * inv
+                vs[at] = jnp.where(here, scaled, vs[at] - c[p] * scaled)
         pivots = [[row_of(v, p) for p in range(GROUP)] for v in vs]
         for rows, v in zip(sets, vs):
             rows[k] = v
@@ -83,10 +84,7 @@
     panels = count // per
     for j in range(panels):
         panel = list(range(per * j, per * (j + 1)))
-        if j + 1 < panels:
-            eager = list(range(per * (j + 1), per * (j + 2)))
-        else:
-            eager = list(range(per * j))
+        eager = list(range(per * (j + 1), per * (j + 2))) if j + 1 < panels else []
         others = [i for i in range(count) if i not in panel and i not in eager]
         for k in panel:
             eliminate(k, [i for i in panel if i > k] + [i for i in panel if i < k] + eager)
@@ -527,8 +525,6 @@
     top, bottom = swap(by_x[:half], 2), swap(by_y[half:], 1)
     mine = [own, by_x, by_y, top, bottom]
     pieces = mine + [other_core(piece) for piece in mine]
-    source = after(sources[0], top, bottom)
-    rhs = [source, swap(source, 1), swap(source, 2), swap(source, 3)]
     settled = (group != 0) & (group < groups - 2)
     flags = jnp.stack(
         [
@@ -564,6 +560,7 @@
     into_o = send(mi_half, first)
     source = after(sources[0], mi_half)
     rhs = [source, swap(source, 1), swap(source, 2), swap(source, 3)]
+    into_o, *rhs = lax.optimization_barrier((into_o, *rhs))
     steps = []
     for t in range(middle - 1):
         new_half, si, y = call(

time: 203 us -> 209 us (1.030)
  waiting for transfers between devices: 81.4 us -> 86.2 us
    ppermute x7, waiting for transfers between devices: 18.1 us -> 29.6 us  [swap(): return lax.ppermute(x, 'member', [(m, m ^ bits) for m in range(MEMBERS)])]
    ppermute x11, waiting for transfers between devices: 58.9 us -> 50.6 us  [send(): return lax.ppermute(x, 'group', pairs)]
  transfers between devices with their start and end apart: 27 -> 27, of which waited for: 9 -> 12; matrix products, arithmetic and copies ran while one was open for 0% -> 0% of each run, Pallas kernels for 17% -> 6%
where the time goes in v3:
time: 209 us; the launch traced here: 205 us
  Pallas kernels  90.9 us (43%)
  waiting for transfers between devices  86.2 us (41%)
  starting transfers between devices  22.9 us (11%)
  local copies, waits for them, and re-layouts  4.68 us (2%)
    pallas_call x9, Pallas kernels, call(): pl.pallas_call(kernel, out_shape=[jax.ShapeDtypeStruct(s, jnp.float32) fo...  90.9 us
    ppermute x11, waiting for transfers between devices, send(): return lax.ppermute(x, 'group', pairs)  50.6 us
    ppermute x7, waiting for transfers between devices, swap(): return lax.ppermute(x, 'member', [(m, m ^ bits) for m in range(MEMBERS)])  29.6 us
    ppermute x11, starting transfers between devices, send(): return lax.ppermute(x, 'group', pairs)  11.9 us
    ppermute x7, starting transfers between devices, swap(): return lax.ppermute(x, 'member', [(m, m ^ bits) for m in range(MEMBERS)])  9.77 us
    ppermute x9, waiting for transfers between devices, other_core(): return lax.ppermute(x, 'col', [(0, 1), (1, 0)])  6.05 us
    unnamed x9, local copies, waits for them, and re-layouts  4.47 us
  transfers between devices with their start and end apart: 27, of which 12 were waited for; matrix products, arithmetic and copies ran while one was open for 0% of the time, Pallas kernels for 6%

profile of v3, /device:TPU:16, one launch (start us, length us, event | category | flops | bytes accessed | tf_op | source)
XLA Modules:
  0.0 205.1 jit_solution(11720121582761875147)
XLA Ops:
  3.2 1.6 collective-permute-start.1
  4.8 1.5 collective-permute-start
  6.3 10.8 %collective-permute-done.1.refs_2_ = f32[520,256]{1,0:T(8,128)S(1)} collective-permute-done((f32[520,256]{1,0:T(8,128)S(1)}, f32[520,256]{1,0:T(8,128)S(1)}, u32[]{:S(2)}, u32[]{:S(2)}) %collective-permute-start.1) | collective-permute-done | bytes 532512 | tf_op jit(solution)/shard_map/ppermute | solution.py:511
  17.1 1.6 collective-permute-start.3
  19.2 1.6 collective-permute-start.2
  20.8 3.7 %collective-permute-done.3.refs_4_ = f32[264,256]{1,0:T(8,128)S(1)} collective-permute-done((f32[264,256]{1,0:T(8,128)S(1)}, f32[264,256]{1,0:T(8,128)S(1)}, u32[]{:S(2)}, u32[]{:S(2)}) %collective-permute-start.3) | collective-permute-done | bytes 270368 | tf_op jit(solution)/shard_map/ppermute | solution.py:511
  24.5 3.6 %collective-permute-done.2.refs_3_ = f32[256,256]{1,0:T(8,128)} collective-permute-done((f32[256,256]{1,0:T(8,128)S(1)}, f32[256,256]{1,0:T(8,128)}, u32[]{:S(2)}, u32[]{:S(2)}) %collective-permute-start.2) | collective-permute-done | bytes 262176 | tf_op jit(solution)/shard_map/ppermute | solution.py:511
  28.2 1.8 collective-permute-done.7.refs_8_
  30.0 20.9 %shard_map.47 = (f32[4,520,512]{2,1,0:T(8,128)S(1)}, f32[512,512]{1,0:T(8,128)S(1)}) custom-call(s32[6]{0:T(128)S(1)} %stack.39.flags, f32[520,256]{1,0:T(8,128)S(1)} %shard_map.46.refs_0_, f32[520,256]{1,0:T(8,128)S(1)} %collective-permute-done.refs_1_, f32[520,256]{1,0:T(8,128)S(1)} %collective-permute-done.1.refs_2_, ...), custom_call_target="tpu_custom_call" | custom-call | flops 16106127360 | bytes 9568280 | tf_op jit(solution)/shard_map/pallas_call | solution.py:486
  50.9 2.0 copy-done.3
  53.1 2.5 %collective-permute-done.9.other.p_other = f32[512,512]{1,0:T(8,128)S(1)} collective-permute-done((f32[512,512]{1,0:T(8,128)S(1)}, f32[512,512]{1,0:T(8,128)S(1)}, u32[]{:S(2)}, u32[]{:S(2)}) %collective-permute-start.9) | collective-permute-done | bytes 1048608 | tf_op jit(solution)/shard_map/ppermute | solution.py:514
  55.6 31.5 %shard_map.48 = (f32[512,512]{1,0:T(8,128)S(1)}, f32[512,512]{1,0:T(8,128)S(1)}, f32[512,512]{1,0:T(8,128)S(1)}, f32[512,512]{1,0:T(8,128)S(1)}, f32[512,512]{1,...) custom-call(s32[6]{0:T(128)S(1)} %stack.39.flags, ...), custom_call_target="tpu_custom_call" | custom-call | flops 24159191040 | bytes 18284568 | tf_op jit(solution)/shard_map/pallas_call | solution.py:486
  87.1 1.3 collective-permute-start.10
  88.4 1.5 collective-permute-start.13
  90.5 1.4 collective-permute-start.11
  91.9 6.6 %collective-permute-done.13.by_xy = f32[512,128]{1,0:T(8,128)S(1)} collective-permute-done((f32[512,128]{1,0:T(8,128)S(1)}, f32[512,128]{1,0:T(8,128)S(1)}, u32[]{:S(2)}, u32[]{:S(2)}) %collective-permute-start.13) | collective-permute-done | bytes 262176 | tf_op jit(solution)/shard_map/ppermute | solution.py:511
  98.5 4.8 %collective-permute-done.12.by_y = f32[512,128]{1,0:T(8,128)S(1)} collective-permute-done((f32[512,128]{1,0:T(8,128)S(1)}, f32[512,128]{1,0:T(8,128)S(1)}, u32[]{:S(2)}, u32[]{:S(2)}) %collective-permute-start.12) | collective-permute-done | bytes 262176 | tf_op jit(solution)/shard_map/ppermute | solution.py:511
  103.4 1.7 collective-permute-done.14.other
  105.1 21.3 %shard_map.49 = (f32[384,256]{1,0:T(8,128)S(1)}, f32[512,512]{1,0:T(8,128)S(1)}, f32[512,512]{1,0:T(8,128)S(1)}) custom-call(s32[6]{0:T(128)S(1)} %stack.39.flags, f32[512,512]{1,0:T(8,128)S(1)} %get-tuple-element.50.goi, f32[512,512]{1,0:T(8,128)S(1)} %get-tuple-element.51.gio, f32[512,512]{1,0:T(8,128)S(1)} %get-tuple-element.52.mo, ...), custom_call_target="tpu_custom_call" | custom-call | flops 16106127360 | bytes 7471128 | tf_op jit(solution)/shard_map/pallas_call | solution.py:486
  126.4 1.3 collective-permute-start.18
  128.4 8.4 %shard_map.50 = (f32[512,128]{1,0:T(8,128)S(1)}, f32[512,512]{1,0:T(8,128)S(1)}, f32[512,512]{1,0:T(8,128)S(1)}, f32[512,128]{1,0:T(8,128)S(1)}, f32[512,128]{1,0:T(8,128)S(1)}) custom-call(s32[6]{0:T(128)S(1)} %stack.39.flags, f32[512,128]{1,0:T(8,128)S(1)} %bitcast.13, f32[512,128]{1,0:T(8,128)S(1)} %collective-permute-done.11.by_x, ...), custom_call_target="tpu_custom_call" | custom-call | flops 4831838208 | bytes 13369368 | tf_op jit(solution)/shard_map/pallas_call | solution.py:486
  136.8 1.3 collective-permute-start.15
  138.1 8.9 %collective-permute-done.15.ro_in = f32[512,128]{1,0:T(8,128)S(1)} collective-permute-done((f32[512,128]{1,0:T(8,128)S(1)}, f32[512,128]{1,0:T(8,128)S(1)}, u32[]{:S(2)}, u32[]{:S(2)}) %collective-permute-start.15) | collective-permute-done | bytes 262176 | tf_op jit(solution)/shard_map/ppermute | solution.py:508
  147.1 1.0 shard_map.51
  148.7 1.3 collective-permute-start.23
  151.7 1.3 collective-permute-start.21
  153.0 1.4 collective-permute-start.20
  154.4 1.7 collective-permute-done.23.ri_in
  156.1 2.5 %shard_map.53 = (f32[512,128]{1,0:T(8,128)S(1)}, f32[512,128]{1,0:T(8,128)S(1)}) custom-call(s32[6]{0:T(128)S(1)} %stack.39.flags, f32[512,512]{1,0:T(8,128)S(1)} %get-tuple-element.77.inv_i, f32[512,512]{1,0:T(8,128)S(1)} %get-tuple-element.80.y, f32[512,512]{1,0:T(8,128)S(1)} %get-tuple-element.81.left, f32[512,128]{1,0:T(8,128)S(1)} %get-tuple-element.72.ro, ...), custom_call_target="tpu_custom_call" | custom-call | flops 16106127360 | bytes 4718616 | tf_op jit(solution)/shard_map/pallas_call | solution.py:486
  159.9 1.3 collective-permute-start.25
  161.3 39.9 %collective-permute-done.25.in_b = f32[512,128]{1,0:T(8,128)S(1)} collective-permute-done((f32[512,128]{1,0:T(8,128)S(1)}, f32[512,128]{1,0:T(8,128)S(1)}, u32[]{:S(2)}, u32[]{:S(2)}) %collective-permute-start.25) | collective-permute-done | bytes 262176 | tf_op jit(solution)/shard_map/ppermute | solution.py:508
  201.2 3.7 %shard_map.54 = f32[512,128]{1,0:T(8,128)} custom-call(s32[6]{0:T(128)S(1)} %stack.39.flags, f32[512,128]{1,0:T(8,128)S(1)} %get-tuple-element.67.w, f32[512,512]{1,0:T(8,128)S(1)} %get-tuple-element.68.ao, f32[512,512]{1,0:T(8,128)S(1)} %get-tuple-element.69.ai, f32[512,512]{1,0:T(8,128)S(1)} %get-tuple-element.78.y, f32[512,128]{1,0:T(8,128)S(1)} %get-tuple-element.79.vo, ...), custom_call_target="tpu_custom_call" | custom-call | flops 1610612736 | bytes 6553624 | tf_op jit(solution)/shard_map/pallas_call | solution.py:486
  (44 shorter events, 9.0 us)
Async XLA Ops:
  0.9 1.0 copy-start
  1.9 0.7 copy-start.1
  3.2 13.9 %collective-permute-start.1 = (f32[520,256]{1,0:T(8,128)S(1)}, f32[520,256]{1,0:T(8,128)S(1)}, u32[]{:S(2)}, u32[]{:S(2)}) collective-permute-start(f32[520,256]{1,0:T(8,128)S(1)} %shard_map.46.refs_0_), channel_id=1, source_target_pairs={{0,4},{2,6},{4,0},{6,2},{1,5},{3,7},{5,1},{7,3},{8,12},{10,14},{12... | collective-permute-start | bytes 1597448 | tf_op jit(solution)/shard_map/ppermute | solution.py:511
  4.8 14.4 %collective-permute-start = (f32[520,256]{1,0:T(8,128)S(1)}, f32[520,256]{1,0:T(8,128)S(1)}, u32[]{:S(2)}, u32[]{:S(2)}) collective-permute-start(f32[520,256]{1,0:T(8,128)S(1)} %shard_map.46.refs_0_), channel_id=1, source_target_pairs={{0,2},{2,0},{4,6},{6,4},{1,3},{3,1},{5,7},{7,5},{8,10},{10,8},{12,... | collective-permute-start | bytes 1597448 | tf_op jit(solution)/shard_map/ppermute | solution.py:511
  17.1 7.4 %collective-permute-start.3 = (f32[264,256]{1,0:T(8,128)S(1)}, f32[264,256]{1,0:T(8,128)S(1)}, u32[]{:S(2)}, u32[]{:S(2)}) collective-permute-start(f32[264,256]{1,0:T(8,128)S(1)} %slice.9), channel_id=1, source_target_pairs={{0,2},{2,0},{4,6},{6,4},{1,3},{3,1},{5,7},{7,5},{8,10},{10,8},{12,... | collective-permute-start | bytes 811016 | tf_op jit(solution)/shard_map/ppermute | solution.py:511
  18.7 9.5 %collective-permute-start.4 = (f32[520,256]{1,0:T(8,128)S(1)}, f32[520,256]{1,0:T(8,128)S(1)}, u32[]{:S(2)}, u32[]{:S(2)}) collective-permute-start(f32[520,256]{1,0:T(8,128)S(1)} %shard_map.46.refs_0_), channel_id=1, source_target_pairs={{0,1},{1,0},{2,3},{3,2},{4,5},{5,4},{6,7},{7,6},{8,9},{9,8},{10,11... | collective-permute-start | bytes 1597448 | tf_op jit(solution)/shard_map/ppermute | solution.py:514
  18.7 11.3 %collective-permute-start.6 = (f32[520,256]{1,0:T(8,128)S(1)}, f32[520,256]{1,0:T(8,128)S(1)}, u32[]{:S(2)}, u32[]{:S(2)}) collective-permute-start(f32[520,256]{1,0:T(8,128)S(1)} %collective-permute-done.1.refs_2_), channel_id=1, source_target_pairs={{0,1},{1,0},{2,3},{3,2},{4,5},{5,4},{6,7},{7,6},{8,9},{9,8},{10,11... | collective-permute-start | bytes 1597448 | tf_op jit(solution)/shard_map/ppermute | solution.py:514
  19.2 10.8 %collective-permute-start.5 = (f32[520,256]{1,0:T(8,128)S(1)}, f32[520,256]{1,0:T(8,128)S(1)}, u32[]{:S(2)}, u32[]{:S(2)}) collective-permute-start(f32[520,256]{1,0:T(8,128)S(1)} %collective-permute-done.refs_1_), channel_id=1, source_target_pairs={{0,1},{1,0},{2,3},{3,2},{4,5},{5,4},{6,7},{7,6},{8,9},{9,8},{10,11... | collective-permute-start | bytes 1597448 | tf_op jit(solution)/shard_map/ppermute | solution.py:514
  19.2 8.9 %collective-permute-start.2 = (f32[256,256]{1,0:T(8,128)S(1)}, f32[256,256]{1,0:T(8,128)}, u32[]{:S(2)}, u32[]{:S(2)}) collective-permute-start(f32[256,256]{1,0:T(8,128)S(1)} %slice.8), channel_id=1, source_target_pairs={{0,4},{2,6},{4,0},{6,2},{1,5},{3,7},{5,1},{7,3},{8,12},{10,14},{12... | collective-permute-start | bytes 786440 | tf_op jit(solution)/shard_map/ppermute | solution.py:511
  24.5 5.5 %collective-permute-start.8 = (f32[264,256]{1,0:T(8,128)S(1)}, f32[264,256]{1,0:T(8,128)}, u32[]{:S(2)}, u32[]{:S(2)}) collective-permute-start(f32[264,256]{1,0:T(8,128)S(1)} %collective-permute-done.3.refs_4_), channel_id=1, source_target_pairs={{0,1},{1,0},{2,3},{3,2},{4,5},{5,4},{6,7},{7,6},{8,9},{9,8},{10,11... | collective-permute-start | bytes 811016 | tf_op jit(solution)/shard_map/ppermute | solution.py:514
  28.1 1.9 collective-permute-start.7
  50.9 2.0 copy-start.3
  52.9 2.7 %collective-permute-start.9 = (f32[512,512]{1,0:T(8,128)S(1)}, f32[512,512]{1,0:T(8,128)S(1)}, u32[]{:S(2)}, u32[]{:S(2)}) collective-permute-start(f32[512,512]{1,0:T(8,128)S(1)} %get-tuple-element.46.mine.p_mine), channel_id=1, source_target_pairs={{0,1},{1,0},{2,3},{3,2},{4,5},{5,4},{6,7},{7,6},{8,9},{9,8},{10,11... | collective-permute-start | bytes 3145736 | tf_op jit(solution)/shard_map/ppermute | solution.py:514
  55.6 32.8 %copy-start.2 = (f32[1,512,128]{2,1,0:T(8,128)S(1)}, f32[1,512,128]{2,1,0:T(8,128)}, u32[]{:S(2)}) copy-start(f32[1,512,128]{2,1,0:T(8,128)} %param.7) | copy-start | bytes 786436
  87.1 16.3 %collective-permute-start.10 = (f32[384,256]{1,0:T(8,128)S(1)}, f32[384,256]{1,0:T(8,128)S(1)}, u32[]{:S(2)}, u32[]{:S(2)}) collective-permute-start(f32[384,256]{1,0:T(8,128)S(1)} %get-tuple-element.47), channel_id=1, source_target_pairs={{24,16},{25,17},{26,18},{27,19},{28,20},{29,21},{30,22},{31,23}} | collective-permute-start | bytes 1179656 | tf_op jit(solution)/shard_map/ppermute | solution.py:508
  88.4 10.2 %collective-permute-start.13 = (f32[512,128]{1,0:T(8,128)S(1)}, f32[512,128]{1,0:T(8,128)S(1)}, u32[]{:S(2)}, u32[]{:S(2)}) collective-permute-start(f32[512,128]{1,0:T(8,128)S(1)} %bitcast.10), channel_id=1, source_target_pairs={{0,6},{2,4},{4,2},{6,0},{1,7},{3,5},{5,3},{7,1},{8,14},{10,12},{12... | collective-permute-start | bytes 786440 | tf_op jit(solution)/shard_map/ppermute | solution.py:511
  89.9 13.4 %collective-permute-start.12 = (f32[512,128]{1,0:T(8,128)S(1)}, f32[512,128]{1,0:T(8,128)S(1)}, u32[]{:S(2)}, u32[]{:S(2)}) collective-permute-start(f32[512,128]{1,0:T(8,128)S(1)} %bitcast.11), channel_id=1, source_target_pairs={{0,4},{2,6},{4,0},{6,2},{1,5},{3,7},{5,1},{7,3},{8,12},{10,14},{12... | collective-permute-start | bytes 786440 | tf_op jit(solution)/shard_map/ppermute | solution.py:511
  90.5 12.9 %collective-permute-start.11 = (f32[512,128]{1,0:T(8,128)S(1)}, f32[512,128]{1,0:T(8,128)S(1)}, u32[]{:S(2)}, u32[]{:S(2)}) collective-permute-start(f32[512,128]{1,0:T(8,128)S(1)} %bitcast.12), channel_id=1, source_target_pairs={{0,2},{2,0},{4,6},{6,4},{1,3},{3,1},{5,7},{7,5},{8,10},{10,8},{12,... | collective-permute-start | bytes 786440 | tf_op jit(solution)/shard_map/ppermute | solution.py:511
  103.4 1.7 collective-permute-start.14
  126.4 21.7 %collective-permute-start.18 = (f32[384,256]{1,0:T(8,128)S(1)}, f32[384,256]{1,0:T(8,128)S(1)}, u32[]{:S(2)}, u32[]{:S(2)}) collective-permute-start(f32[384,256]{1,0:T(8,128)S(1)} %get-tuple-element.55), channel_id=1, source_target_pairs={{16,8},{17,9},{18,10},{19,11},{20,12},{21,13},{22,14},{23,15}} | collective-permute-start | bytes 1179656 | tf_op jit(solution)/shard_map/ppermute | solution.py:508
  127.7 20.5 %collective-permute-start.16 = (f32[384,256]{1,0:T(8,128)S(1)}, f32[384,256]{1,0:T(8,128)S(1)}, u32[]{:S(2)}, u32[]{:S(2)}) collective-permute-start(f32[384,256]{1,0:T(8,128)S(1)} %get-tuple-element.55), channel_id=1, source_target_pairs={{0,8},{1,9},{2,10},{3,11},{4,12},{5,13},{6,14},{7,15}} | collective-permute-start | bytes 1179656 | tf_op jit(solution)/shard_map/ppermute | solution.py:508
  136.8 10.2 %collective-permute-start.15 = (f32[512,128]{1,0:T(8,128)S(1)}, f32[512,128]{1,0:T(8,128)S(1)}, u32[]{:S(2)}, u32[]{:S(2)}) collective-permute-start(f32[512,128]{1,0:T(8,128)S(1)} %get-tuple-element.73.ri), channel_id=1, source_target_pairs={{24,16},{25,17},{26,18},{27,19},{28,20},{29,21},{30,22},{31,23}} | collective-permute-start | bytes 786440 | tf_op jit(solution)/shard_map/ppermute | solution.py:508
  148.1 2.6 %collective-permute-start.19 = (f32[384,256]{1,0:T(8,128)S(1)}, f32[384,256]{1,0:T(8,128)S(1)}, u32[]{:S(2)}, u32[]{:S(2)}) collective-permute-start(f32[384,256]{1,0:T(8,128)S(1)} %collective-permute-done.18.i_mine), channel_id=1, source_target_pairs={{0,1},{1,0},{2,3},{3,2},{4,5},{5,4},{6,7},{7,6},{8,9},{9,8},{10,11... | collective-permute-start | bytes 1179656 | tf_op jit(solution)/shard_map/ppermute | solution.py:514
  148.2 2.5 %collective-permute-start.17 = (f32[384,256]{1,0:T(8,128)S(1)}, f32[384,256]{1,0:T(8,128)S(1)}, u32[]{:S(2)}, u32[]{:S(2)}) collective-permute-start(f32[384,256]{1,0:T(8,128)S(1)} %collective-permute-done.16.o_mine), channel_id=1, source_target_pairs={{0,1},{1,0},{2,3},{3,2},{4,5},{5,4},{6,7},{7,6},{8,9},{9,8},{10,11... | collective-permute-start | bytes 1179656 | tf_op jit(solution)/shard_map/ppermute | solution.py:514
  148.7 7.4 %collective-permute-start.23 = (f32[512,128]{1,0:T(8,128)S(1)}, f32[512,128]{1,0:T(8,128)S(1)}, u32[]{:S(2)}, u32[]{:S(2)}) collective-permute-start(f32[512,128]{1,0:T(8,128)S(1)} %get-tuple-element.82), channel_id=1, source_target_pairs={{16,8},{17,9},{18,10},{19,11},{20,12},{21,13},{22,14},{23,15}} | collective-permute-start | bytes 786440 | tf_op jit(solution)/shard_map/ppermute | solution.py:508
  150.0 6.1 %collective-permute-start.22 = (f32[512,128]{1,0:T(8,128)S(1)}, f32[512,128]{1,0:T(8,128)S(1)}, u32[]{:S(2)}, u32[]{:S(2)}) collective-permute-start(f32[512,128]{1,0:T(8,128)S(1)} %get-tuple-element.82), channel_id=1, source_target_pairs={{0,8},{1,9},{2,10},{3,11},{4,12},{5,13},{6,14},{7,15}} | collective-permute-start | bytes 786440 | tf_op jit(solution)/shard_map/ppermute | solution.py:508
  151.7 9.6 %collective-permute-start.21 = (f32[512,128]{1,0:T(8,128)S(1)}, f32[512,128]{1,0:T(8,128)S(1)}, u32[]{:S(2)}, u32[]{:S(2)}) collective-permute-start(f32[512,128]{1,0:T(8,128)S(1)} %get-tuple-element.79.vo), channel_id=1, source_target_pairs={{16,24},{17,25},{18,26},{19,27},{20,28},{21,29},{22,30},{23,31}} | collective-permute-start | bytes 786440 | tf_op jit(solution)/shard_map/ppermute | solution.py:508
  153.0 48.2 %collective-permute-start.20 = (f32[512,512]{1,0:T(8,128)S(1)}, f32[512,512]{1,0:T(8,128)S(1)}, u32[]{:S(2)}, u32[]{:S(2)}) collective-permute-start(f32[512,512]{1,0:T(8,128)S(1)} %get-tuple-element.78.y), channel_id=1, source_target_pairs={{16,24},{17,25},{18,26},{19,27},{20,28},{21,29},{22,30},{23,31}} | collective-permute-start | bytes 3145736 | tf_op jit(solution)/shard_map/ppermute | solution.py:508
  158.6 2.7 %collective-permute-start.24 = (f32[512,128]{1,0:T(8,128)S(1)}, f32[512,128]{1,0:T(8,128)S(1)}, u32[]{:S(2)}, u32[]{:S(2)}) collective-permute-start(f32[512,128]{1,0:T(8,128)S(1)} %get-tuple-element.83.xo), channel_id=1, source_target_pairs={{8,0},{9,1},{10,2},{11,3},{12,4},{13,5},{14,6},{15,7}} | collective-permute-start | bytes 786440 | tf_op jit(solution)/shard_map/ppermute | solution.py:508
  159.3 2.0 collective-permute-start.26
  159.9 41.2 %collective-permute-start.25 = (f32[512,128]{1,0:T(8,128)S(1)}, f32[512,128]{1,0:T(8,128)S(1)}, u32[]{:S(2)}, u32[]{:S(2)}) collective-permute-start(f32[512,128]{1,0:T(8,128)S(1)} %get-tuple-element.84.xi), channel_id=1, source_target_pairs={{8,16},{9,17},{10,18},{11,19},{12,20},{13,21},{14,22},{15,23}} | collective-permute-start | bytes 786440 | tf_op jit(solution)/shard_map/ppermute | solution.py:508

commit v4 on v3

--- a/solution.py
+++ b/solution.py
@@ -12,7 +12,7 @@
 MEMBERS = 4
 SPARE_BYTES = 16 * 1024 * 1024
 LEAF = 128
-PANEL = 16
+PANEL = 32
 GROUP = 8
 
 
@@ -84,7 +84,10 @@
     panels = count // per
     for j in range(panels):
         panel = list(range(per * j, per * (j + 1)))
-        eager = list(range(per * (j + 1), per * (j + 2))) if j + 1 < panels else []
+        if j + 1 < panels:
+            eager = list(range(per * (j + 1), per * (j + 2)))
+        else:
+            eager = list(range(per * j))
         others = [i for i in range(count) if i not in panel and i not in eager]
         for k in panel:
             eliminate(k, [i for i in panel if i > k] + [i for i in panel if i < k] + eager)
@@ -179,44 +182,56 @@
 
 
 def panel_kernel(pattern, coupling, mass, panel):
-    width, half = coupling.shape
-    tile_w = width // (width // LEAF)
-    first = lax.axis_index("col") * half
+    half = coupling.shape[1]
+    count = half // LEAF
+    first = lax.axis_index("col") == 0
     rows = lax.broadcasted_iota(jnp.int32, (LEAF, LEAF), 0)
     columns = lax.broadcasted_iota(jnp.int32, (LEAF, LEAF), 1)
-    across = half // tile_w
-    for r in range(width // tile_w):
-        for c in range(across):
-            at = (slice(tile_w * r, tile_w * (r + 1)), slice(tile_w * c, tile_w * (c + 1)))
-            unit = (rows + tile_w * r == columns + (first + tile_w * c)).astype(jnp.float32)
-            panel[at] = unit + pattern[across * r + c].astype(jnp.float32) * coupling[at]
-    panel[width:, :] = jnp.broadcast_to(mass[...], (GROUP, half))
+    unit = (rows == columns).astype(jnp.float32)
+
+    def tile(r, c):
+        on = pattern[count * r + c].astype(jnp.float32)
+        return on * coupling[LEAF * r : LEAF * (r + 1), LEAF * c : LEAF * (c + 1)]
+
+    for c in range(count):
+        at = slice(LEAF * c, LEAF * (c + 1))
+        for r in range(count):
+            block = jnp.where(first, tile(r, c), tile(count + r, c))
+            panel[LEAF * r : LEAF * (r + 1), at] = block + unit if r == c else block
+        for r in range(count // 2):
+            low = half + LEAF * r
+            above = tile(c, count // 2 + r).T
+            panel[low : low + LEAF, at] = jnp.where(first, tile(count + r, c), above)
+    panel[half + half // 2 :, :] = jnp.broadcast_to(mass[...], (GROUP, half))
 
 
 def place_bonds(flags, pieces, bonds):
-    half = bonds.shape[-1] // 2
-    me = flags[MEMBER]
+    width = bonds.shape[-1]
+    half = width // 2
+    low = half // 2
+    right = flags[RIGHT] == 1
     for source in range(2):
         core = flags[COL] if source == 0 else 1 - flags[COL]
-        columns = pl.ds(pl.multiple_of(core * half, half), half)
         own, by_x, by_y, top, bottom = pieces[5 * source : 5 * source + 5]
-        for rel, piece in enumerate((own, by_x, by_y)):
-            bonds[me ^ rel, :, columns] = piece[...]
-        bonds[me ^ 3, :half, columns] = top[...]
-        bonds[me ^ 3, half:, columns] = bottom[...]
+        crossed = jnp.concatenate([top[...], bottom[...]], axis=0)
+        same = pl.ds(pl.multiple_of(core * half, half), half)
+        below = pl.ds(pl.multiple_of(half + core * low, low), low)
+        for rel, piece in enumerate((own[...], by_x[...], by_y[...], crossed)):
+            member = flags[MEMBER] ^ rel
+            k = jnp.where(right, MEMBERS - 1 - member, member)
+            corner = piece[half : half + low, :]
+            bonds[k, same, same] = piece[:half, :]
+            bonds[k, below, :half] = corner
+            bonds[k, :half, below] = corner.T
+            k = jnp.where(right & (member > 0), MEMBERS - member, member)
+            bonds[k, width:, same] = piece[half + low :, :]
 
 
 def first_kernel(flags, *refs):
     pieces = refs[:10]
-    bonds, inverse, placed, work = refs[10:]
+    bonds, inverse, work = refs[10:]
     width = inverse.shape[0]
-    right = flags[RIGHT]
-    place_bonds(flags, pieces, placed)
-    for k in range(MEMBERS):
-        at = jnp.where(right == 1, MEMBERS - 1 - k, k)
-        bonds[k, :width, :] = placed[at, :width, :]
-        at = jnp.where((right == 1) & (k > 0), MEMBERS - k, k)
-        bonds[k, width:, :] = placed[at, width:, :]
+    place_bonds(flags, pieces, bonds)
     side = 2 * flags[COL]
     work[0] = plus_diagonal(
         bonds[side, :width, :] + bonds[side + 1, :width, :], bonds[side + 1, width : width + 1, :]
@@ -458,10 +473,11 @@
     (own,) = call(
         panel_kernel,
         [tile_pattern[0].reshape(-1), coupling[0], orbital_mass],
-        [(width + GROUP, half)],
+        [(half + half // 2 + GROUP, half)],
     )
     by_x, by_y = swap(own, 1), swap(own, 2)
-    top, bottom = swap(by_x[:half], 2), swap(by_y[half:], 1)
+    cut = half - half // 4
+    top, bottom = swap(by_x[:cut], 2), swap(by_y[cut:], 1)
     mine = [own, by_x, by_y, top, bottom]
     pieces = mine + [other_core(piece) for piece in mine]
     settled = flags[SETTLED] == 1
@@ -519,10 +535,11 @@
     (own,) = call(
         panel_kernel,
         [tile_pattern[0].reshape(-1), coupling[0], orbital_mass],
-        [(width + GROUP, half)],
+        [(half + half // 2 + GROUP, half)],
     )
     by_x, by_y = swap(own, 1), swap(own, 2)
-    top, bottom = swap(by_x[:half], 2), swap(by_y[half:], 1)
+    cut = half - half // 4
+    top, bottom = swap(by_x[:cut], 2), swap(by_y[cut:], 1)
     mine = [own, by_x, by_y, top, bottom]
     pieces = mine + [other_core(piece) for piece in mine]
     settled = (group != 0) & (group < groups - 2)
@@ -545,10 +562,12 @@
         first_kernel,
         [flags, *pieces],
         [(MEMBERS, width + GROUP, width), square],
-        [(MEMBERS, width + GROUP, width), room],
+        [room],
         20 * unit_flops,
     )
     p_other = other_core(p_mine)
+    source = after(sources[0], p_mine)
+    rhs = [source, swap(source, 1), swap(source, 2), swap(source, 3)]
     i2, y10, y12, y32, y3i, yo, yi, goi, gio, mo, mi, mi_half = call(
         reduce_kernel,
         [flags, bonds, p_mine, p_other],
@@ -558,9 +577,6 @@
     )
     first = [(groups - 1, groups - 2)]
     into_o = send(mi_half, first)
-    source = after(sources[0], mi_half)
-    rhs = [source, swap(source, 1), swap(source, 2), swap(source, 3)]
-    into_o, *rhs = lax.optimization_barrier((into_o, *rhs))
     steps = []
     for t in range(middle - 1):
         new_half, si, y = call(

time: 209 us -> 197 us (0.943)
  waiting for transfers between devices: 86.2 us -> 76.7 us
  Pallas kernels: 90.9 us -> 88.8 us
    ppermute x7, waiting for transfers between devices: 29.6 us -> 13.8 us  [swap(): return lax.ppermute(x, 'member', [(m, m ^ bits) for m in range(MEMBERS)])]
    ppermute x11, waiting for transfers between devices: 50.6 us -> 59 us  [send(): return lax.ppermute(x, 'group', pairs)]
    ppermute x9, waiting for transfers between devices: 6.05 us -> 3.9 us  [other_core(): return lax.ppermute(x, 'col', [(0, 1), (1, 0)])]
    pallas_call x9, Pallas kernels: 90.9 us -> 88.8 us  [call(): pl.pallas_call(kernel, out_shape=[jax.ShapeDtypeStruct(s, jnp.float32) fo...]
  transfers between devices with their start and end apart: 27 -> 27, of which waited for: 12 -> 9; matrix products, arithmetic and copies ran while one was open for 0% -> 0% of each run, Pallas kernels for 6% -> 17%
where the time goes in v4:
time: 197 us; the launch traced here: 193 us
  Pallas kernels  88.8 us (45%)
  waiting for transfers between devices  76.7 us (39%)
  starting transfers between devices  22.8 us (12%)
  local copies, waits for them, and re-layouts  4.67 us (2%)
    pallas_call x9, Pallas kernels, call(): pl.pallas_call(kernel, out_shape=[jax.ShapeDtypeStruct(s, jnp.float32) fo...  88.8 us
    ppermute x11, waiting for transfers between devices, send(): return lax.ppermute(x, 'group', pairs)  59 us
    ppermute x7, waiting for transfers between devices, swap(): return lax.ppermute(x, 'member', [(m, m ^ bits) for m in range(MEMBERS)])  13.8 us
    ppermute x11, starting transfers between devices, send(): return lax.ppermute(x, 'group', pairs)  11.9 us
    ppermute x7, starting transfers between devices, swap(): return lax.ppermute(x, 'member', [(m, m ^ bits) for m in range(MEMBERS)])  9.71 us
    unnamed x9, local copies, waits for them, and re-layouts  4.47 us
  transfers between devices with their start and end apart: 27, of which 9 were waited for; matrix products, arithmetic and copies ran while one was open for 0% of the time, Pallas kernels for 17%

profile of v4, /device:TPU:16, one launch (start us, length us, event | category | flops | bytes accessed | tf_op | source)
XLA Modules:
  0.0 193.4 jit_solution(17113526219123081580)
XLA Ops:
  0.9 1.0 copy-done
  3.2 1.6 collective-permute-start.1
  4.8 1.5 collective-permute-start
  6.3 8.0 %collective-permute-done.1.refs_2_ = f32[392,256]{1,0:T(8,128)S(1)} collective-permute-done((f32[392,256]{1,0:T(8,128)S(1)}, f32[392,256]{1,0:T(8,128)S(1)}, u32[]{:S(2)}, u32[]{:S(2)}) %collective-permute-start.1) | collective-permute-done | bytes 401440 | tf_op jit(solution)/shard_map/ppermute | solution.py:527
  14.3 1.6 collective-permute-start.3
  16.4 1.6 collective-permute-start.2
  18.0 2.3 %collective-permute-done.3.refs_4_ = f32[200,256]{1,0:T(8,128)S(1)} collective-permute-done((f32[200,256]{1,0:T(8,128)S(1)}, f32[200,256]{1,0:T(8,128)S(1)}, u32[]{:S(2)}, u32[]{:S(2)}) %collective-permute-start.3) | collective-permute-done | bytes 204832 | tf_op jit(solution)/shard_map/ppermute | solution.py:527
  20.3 3.5 %collective-permute-done.2.refs_3_ = f32[192,256]{1,0:T(8,128)S(1)} collective-permute-done((f32[192,256]{1,0:T(8,128)S(1)}, f32[192,256]{1,0:T(8,128)S(1)}, u32[]{:S(2)}, u32[]{:S(2)}) %collective-permute-start.2) | collective-permute-done | bytes 196640 | tf_op jit(solution)/shard_map/ppermute | solution.py:527
  23.9 1.4 collective-permute-done.7.refs_8_
  25.3 19.1 %shard_map.47 = (f32[4,520,512]{2,1,0:T(8,128)S(1)}, f32[512,512]{1,0:T(8,128)S(1)}) custom-call(s32[6]{0:T(128)S(1)} %stack.39.flags, f32[392,256]{1,0:T(8,128)S(1)} %shard_map.46.refs_0_, f32[392,256]{1,0:T(8,128)S(1)} %collective-permute-done.refs_1_, f32[392,256]{1,0:T(8,128)S(1)} %collective-permute-done.1.refs_2_, ...), custom_call_target="tpu_custom_call" | custom-call | flops 16106127360 | bytes 8519704 | tf_op jit(solution)/shard_map/pallas_call | solution.py:502
  44.4 2.0 %copy-done.3 = f32[4,520,512]{2,1,0:T(8,128)} copy-done((f32[4,520,512]{2,1,0:T(8,128)}, f32[4,520,512]{2,1,0:T(8,128)S(1)}, u32[]{:S(2)}) %copy-start.3) | copy-done | bytes 4259864
  46.5 2.5 %collective-permute-done.9.other.p_other = f32[512,512]{1,0:T(8,128)S(1)} collective-permute-done((f32[512,512]{1,0:T(8,128)S(1)}, f32[512,512]{1,0:T(8,128)S(1)}, u32[]{:S(2)}, u32[]{:S(2)}) %collective-permute-start.9) | collective-permute-done | bytes 1048608 | tf_op jit(solution)/shard_map/ppermute | solution.py:530
  49.1 31.4 %shard_map.48 = (f32[512,512]{1,0:T(8,128)S(1)}, f32[512,512]{1,0:T(8,128)S(1)}, f32[512,512]{1,0:T(8,128)S(1)}, f32[512,512]{1,0:T(8,128)S(1)}, f32[512,512]{1,...) custom-call(s32[6]{0:T(128)S(1)} %stack.39.flags, ...), custom_call_target="tpu_custom_call" | custom-call | flops 24159191040 | bytes 18284568 | tf_op jit(solution)/shard_map/pallas_call | solution.py:502
  80.5 1.3 collective-permute-start.10
  81.8 11.7 %collective-permute-done.10.mine = f32[384,256]{1,0:T(8,128)S(1)} collective-permute-done((f32[384,256]{1,0:T(8,128)S(1)}, f32[384,256]{1,0:T(8,128)S(1)}, u32[]{:S(2)}, u32[]{:S(2)}) %collective-permute-start.10) | collective-permute-done | bytes 393248 | tf_op jit(solution)/shard_map/ppermute | solution.py:524
  93.5 1.5 collective-permute-start.14
  95.7 1.4 collective-permute-start.12
  97.0 20.3 %shard_map.49 = (f32[384,256]{1,0:T(8,128)S(1)}, f32[512,512]{1,0:T(8,128)S(1)}, f32[512,512]{1,0:T(8,128)S(1)}) custom-call(s32[6]{0:T(128)S(1)} %stack.39.flags, f32[512,512]{1,0:T(8,128)S(1)} %get-tuple-element.43.goi, f32[512,512]{1,0:T(8,128)S(1)} %get-tuple-element.44.gio, f32[512,512]{1,0:T(8,128)S(1)} %get-tuple-element.45.mo, ...), custom_call_target="tpu_custom_call" | custom-call | flops 16106127360 | bytes 7471128 | tf_op jit(solution)/shard_map/pallas_call | solution.py:502
  117.4 1.3 collective-permute-start.18
  119.4 8.4 %shard_map.50 = (f32[512,128]{1,0:T(8,128)S(1)}, f32[512,512]{1,0:T(8,128)S(1)}, f32[512,512]{1,0:T(8,128)S(1)}, f32[512,128]{1,0:T(8,128)S(1)}, f32[512,128]{1,0:T(8,128)S(1)}) custom-call(s32[6]{0:T(128)S(1)} %stack.39.flags, f32[512,128]{1,0:T(8,128)S(1)} %bitcast.13, f32[512,128]{1,0:T(8,128)S(1)} %collective-permute-done.12.by_x, ...), custom_call_target="tpu_custom_call" | custom-call | flops 4831838208 | bytes 13369368 | tf_op jit(solution)/shard_map/pallas_call | solution.py:502
  127.8 1.3 collective-permute-start.15
  129.1 8.5 %collective-permute-done.15.ro_in = f32[512,128]{1,0:T(8,128)S(1)} collective-permute-done((f32[512,128]{1,0:T(8,128)S(1)}, f32[512,128]{1,0:T(8,128)S(1)}, u32[]{:S(2)}, u32[]{:S(2)}) %collective-permute-start.15) | collective-permute-done | bytes 262176 | tf_op jit(solution)/shard_map/ppermute | solution.py:524
  137.6 1.0 shard_map.51
  139.2 1.3 collective-permute-start.23
  141.2 1.0 shard_map.52
  142.2 1.3 collective-permute-start.21
  143.5 1.4 collective-permute-start.20
  144.9 1.7 collective-permute-done.23.ri_in
  146.6 3.1 %shard_map.53 = (f32[512,128]{1,0:T(8,128)S(1)}, f32[512,128]{1,0:T(8,128)S(1)}) custom-call(s32[6]{0:T(128)S(1)} %stack.39.flags, f32[512,512]{1,0:T(8,128)S(1)} %get-tuple-element.67.inv_i, f32[512,512]{1,0:T(8,128)S(1)} %get-tuple-element.70.y, f32[512,512]{1,0:T(8,128)S(1)} %get-tuple-element.71.left, f32[512,128]{1,0:T(8,128)S(1)} %get-tuple-element.62.ro, ...), custom_call_target="tpu_custom_call" | custom-call | flops 16106127360 | bytes 4718616 | tf_op jit(solution)/shard_map/pallas_call | solution.py:502
  151.1 1.3 collective-permute-start.25
  152.4 37.0 %collective-permute-done.25.in_b = f32[512,128]{1,0:T(8,128)S(1)} collective-permute-done((f32[512,128]{1,0:T(8,128)S(1)}, f32[512,128]{1,0:T(8,128)S(1)}, u32[]{:S(2)}, u32[]{:S(2)}) %collective-permute-start.25) | collective-permute-done | bytes 262176 | tf_op jit(solution)/shard_map/ppermute | solution.py:524
  189.5 3.7 %shard_map.54 = f32[512,128]{1,0:T(8,128)} custom-call(s32[6]{0:T(128)S(1)} %stack.39.flags, f32[512,128]{1,0:T(8,128)S(1)} %get-tuple-element.57.w, f32[512,512]{1,0:T(8,128)S(1)} %get-tuple-element.58.ao, f32[512,512]{1,0:T(8,128)S(1)} %get-tuple-element.59.ai, f32[512,512]{1,0:T(8,128)S(1)} %get-tuple-element.68.y, f32[512,128]{1,0:T(8,128)S(1)} %get-tuple-element.69.vo, ...), custom_call_target="tpu_custom_call" | custom-call | flops 1610612736 | bytes 6553624 | tf_op jit(solution)/shard_map/pallas_call | solution.py:502
  (44 shorter events, 6.9 us)
Async XLA Ops:
  0.9 1.0 copy-start
  1.9 0.7 copy-start.1
  3.2 11.1 %collective-permute-start.1 = (f32[392,256]{1,0:T(8,128)S(1)}, f32[392,256]{1,0:T(8,128)S(1)}, u32[]{:S(2)}, u32[]{:S(2)}) collective-permute-start(f32[392,256]{1,0:T(8,128)S(1)} %shard_map.46.refs_0_), channel_id=1, source_target_pairs={{0,4},{2,6},{4,0},{6,2},{1,5},{3,7},{5,1},{7,3},{8,12},{10,14},{12... | collective-permute-start | bytes 1204232 | tf_op jit(solution)/shard_map/ppermute | solution.py:527
  4.8 11.6 %collective-permute-start = (f32[392,256]{1,0:T(8,128)S(1)}, f32[392,256]{1,0:T(8,128)S(1)}, u32[]{:S(2)}, u32[]{:S(2)}) collective-permute-start(f32[392,256]{1,0:T(8,128)S(1)} %shard_map.46.refs_0_), channel_id=1, source_target_pairs={{0,2},{2,0},{4,6},{6,4},{1,3},{3,1},{5,7},{7,5},{8,10},{10,8},{12,... | collective-permute-start | bytes 1204232 | tf_op jit(solution)/shard_map/ppermute | solution.py:527
  14.3 6.0 %collective-permute-start.3 = (f32[200,256]{1,0:T(8,128)S(1)}, f32[200,256]{1,0:T(8,128)S(1)}, u32[]{:S(2)}, u32[]{:S(2)}) collective-permute-start(f32[200,256]{1,0:T(8,128)S(1)} %slice.9), channel_id=1, source_target_pairs={{0,2},{2,0},{4,6},{6,4},{1,3},{3,1},{5,7},{7,5},{8,10},{10,8},{12,... | collective-permute-start | bytes 614408 | tf_op jit(solution)/shard_map/ppermute | solution.py:527
  15.9 8.0 %collective-permute-start.4 = (f32[392,256]{1,0:T(8,128)S(1)}, f32[392,256]{1,0:T(8,128)S(1)}, u32[]{:S(2)}, u32[]{:S(2)}) collective-permute-start(f32[392,256]{1,0:T(8,128)S(1)} %shard_map.46.refs_0_), channel_id=1, source_target_pairs={{0,1},{1,0},{2,3},{3,2},{4,5},{5,4},{6,7},{7,6},{8,9},{9,8},{10,11... | collective-permute-start | bytes 1204232 | tf_op jit(solution)/shard_map/ppermute | solution.py:530
  15.9 9.4 %collective-permute-start.6 = (f32[392,256]{1,0:T(8,128)S(1)}, f32[392,256]{1,0:T(8,128)S(1)}, u32[]{:S(2)}, u32[]{:S(2)}) collective-permute-start(f32[392,256]{1,0:T(8,128)S(1)} %collective-permute-done.1.refs_2_), channel_id=1, source_target_pairs={{0,1},{1,0},{2,3},{3,2},{4,5},{5,4},{6,7},{7,6},{8,9},{9,8},{10,11... | collective-permute-start | bytes 1204232 | tf_op jit(solution)/shard_map/ppermute | solution.py:530
  16.4 8.8 %collective-permute-start.5 = (f32[392,256]{1,0:T(8,128)S(1)}, f32[392,256]{1,0:T(8,128)S(1)}, u32[]{:S(2)}, u32[]{:S(2)}) collective-permute-start(f32[392,256]{1,0:T(8,128)S(1)} %collective-permute-done.refs_1_), channel_id=1, source_target_pairs={{0,1},{1,0},{2,3},{3,2},{4,5},{5,4},{6,7},{7,6},{8,9},{9,8},{10,11... | collective-permute-start | bytes 1204232 | tf_op jit(solution)/shard_map/ppermute | solution.py:530
  16.4 7.4 %collective-permute-start.2 = (f32[192,256]{1,0:T(8,128)S(1)}, f32[192,256]{1,0:T(8,128)S(1)}, u32[]{:S(2)}, u32[]{:S(2)}) collective-permute-start(f32[192,256]{1,0:T(8,128)S(1)} %slice.8), channel_id=1, source_target_pairs={{0,4},{2,6},{4,0},{6,2},{1,5},{3,7},{5,1},{7,3},{8,12},{10,14},{12... | collective-permute-start | bytes 589832 | tf_op jit(solution)/shard_map/ppermute | solution.py:527
  20.3 4.9 %collective-permute-start.8 = (f32[200,256]{1,0:T(8,128)S(1)}, f32[200,256]{1,0:T(8,128)S(1)}, u32[]{:S(2)}, u32[]{:S(2)}) collective-permute-start(f32[200,256]{1,0:T(8,128)S(1)} %collective-permute-done.3.refs_4_), channel_id=1, source_target_pairs={{0,1},{1,0},{2,3},{3,2},{4,5},{5,4},{6,7},{7,6},{8,9},{9,8},{10,11... | collective-permute-start | bytes 614408 | tf_op jit(solution)/shard_map/ppermute | solution.py:530
  23.8 1.4 collective-permute-start.7
  44.4 2.0 %copy-start.3 = (f32[4,520,512]{2,1,0:T(8,128)}, f32[4,520,512]{2,1,0:T(8,128)S(1)}, u32[]{:S(2)}) copy-start(f32[4,520,512]{2,1,0:T(8,128)S(1)} %get-tuple-element.42.bonds) | copy-start | bytes 12779524
  46.4 2.7 %collective-permute-start.9 = (f32[512,512]{1,0:T(8,128)S(1)}, f32[512,512]{1,0:T(8,128)S(1)}, u32[]{:S(2)}, u32[]{:S(2)}) collective-permute-start(f32[512,512]{1,0:T(8,128)S(1)} %get-tuple-element.40.mine.p_mine), channel_id=1, source_target_pairs={{0,1},{1,0},{2,3},{3,2},{4,5},{5,4},{6,7},{7,6},{8,9},{9,8},{10,11... | collective-permute-start | bytes 3145736 | tf_op jit(solution)/shard_map/ppermute | solution.py:530
  49.1 44.5 %copy-start.2 = (f32[1,512,128]{2,1,0:T(8,128)S(1)}, f32[1,512,128]{2,1,0:T(8,128)}, u32[]{:S(2)}) copy-start(f32[1,512,128]{2,1,0:T(8,128)} %param.7) | copy-start | bytes 786436
  80.5 13.0 %collective-permute-start.10 = (f32[384,256]{1,0:T(8,128)S(1)}, f32[384,256]{1,0:T(8,128)S(1)}, u32[]{:S(2)}, u32[]{:S(2)}) collective-permute-start(f32[384,256]{1,0:T(8,128)S(1)} %get-tuple-element.47), channel_id=1, source_target_pairs={{24,16},{25,17},{26,18},{27,19},{28,20},{29,21},{30,22},{31,23}} | collective-permute-start | bytes 1179656 | tf_op jit(solution)/shard_map/ppermute | solution.py:524
  93.5 3.5 %collective-permute-start.11 = (f32[384,256]{1,0:T(8,128)S(1)}, f32[384,256]{1,0:T(8,128)S(1)}, u32[]{:S(2)}, u32[]{:S(2)}) collective-permute-start(f32[384,256]{1,0:T(8,128)S(1)} %collective-permute-done.10.mine), channel_id=1, source_target_pairs={{0,1},{1,0},{2,3},{3,2},{4,5},{5,4},{6,7},{7,6},{8,9},{9,8},{10,11... | collective-permute-start | bytes 1179656 | tf_op jit(solution)/shard_map/ppermute | solution.py:530
  93.5 25.8 %collective-permute-start.14 = (f32[512,128]{1,0:T(8,128)S(1)}, f32[512,128]{1,0:T(8,128)S(1)}, u32[]{:S(2)}, u32[]{:S(2)}) collective-permute-start(f32[512,128]{1,0:T(8,128)S(1)} %bitcast.10), channel_id=1, source_target_pairs={{0,6},{2,4},{4,2},{6,0},{1,7},{3,5},{5,3},{7,1},{8,14},{10,12},{12... | collective-permute-start | bytes 786440 | tf_op jit(solution)/shard_map/ppermute | solution.py:527
  95.0 24.3 %collective-permute-start.13 = (f32[512,128]{1,0:T(8,128)S(1)}, f32[512,128]{1,0:T(8,128)S(1)}, u32[]{:S(2)}, u32[]{:S(2)}) collective-permute-start(f32[512,128]{1,0:T(8,128)S(1)} %bitcast.11), channel_id=1, source_target_pairs={{0,4},{2,6},{4,0},{6,2},{1,5},{3,7},{5,1},{7,3},{8,12},{10,14},{12... | collective-permute-start | bytes 786440 | tf_op jit(solution)/shard_map/ppermute | solution.py:527
  95.7 23.7 %collective-permute-start.12 = (f32[512,128]{1,0:T(8,128)S(1)}, f32[512,128]{1,0:T(8,128)S(1)}, u32[]{:S(2)}, u32[]{:S(2)}) collective-permute-start(f32[512,128]{1,0:T(8,128)S(1)} %bitcast.12), channel_id=1, source_target_pairs={{0,2},{2,0},{4,6},{6,4},{1,3},{3,1},{5,7},{7,5},{8,10},{10,8},{12,... | collective-permute-start | bytes 786440 | tf_op jit(solution)/shard_map/ppermute | solution.py:527
  117.4 21.3 %collective-permute-start.18 = (f32[384,256]{1,0:T(8,128)S(1)}, f32[384,256]{1,0:T(8,128)S(1)}, u32[]{:S(2)}, u32[]{:S(2)}) collective-permute-start(f32[384,256]{1,0:T(8,128)S(1)} %get-tuple-element.48), channel_id=1, source_target_pairs={{16,8},{17,9},{18,10},{19,11},{20,12},{21,13},{22,14},{23,15}} | collective-permute-start | bytes 1179656 | tf_op jit(solution)/shard_map/ppermute | solution.py:524
  118.7 20.1 %collective-permute-start.16 = (f32[384,256]{1,0:T(8,128)S(1)}, f32[384,256]{1,0:T(8,128)S(1)}, u32[]{:S(2)}, u32[]{:S(2)}) collective-permute-start(f32[384,256]{1,0:T(8,128)S(1)} %get-tuple-element.48), channel_id=1, source_target_pairs={{0,8},{1,9},{2,10},{3,11},{4,12},{5,13},{6,14},{7,15}} | collective-permute-start | bytes 1179656 | tf_op jit(solution)/shard_map/ppermute | solution.py:524
  127.8 9.8 %collective-permute-start.15 = (f32[512,128]{1,0:T(8,128)S(1)}, f32[512,128]{1,0:T(8,128)S(1)}, u32[]{:S(2)}, u32[]{:S(2)}) collective-permute-start(f32[512,128]{1,0:T(8,128)S(1)} %get-tuple-element.63.ri), channel_id=1, source_target_pairs={{24,16},{25,17},{26,18},{27,19},{28,20},{29,21},{30,22},{31,23}} | collective-permute-start | bytes 786440 | tf_op jit(solution)/shard_map/ppermute | solution.py:524
  138.6 2.6 %collective-permute-start.19 = (f32[384,256]{1,0:T(8,128)S(1)}, f32[384,256]{1,0:T(8,128)S(1)}, u32[]{:S(2)}, u32[]{:S(2)}) collective-permute-start(f32[384,256]{1,0:T(8,128)S(1)} %collective-permute-done.18.i_mine), channel_id=1, source_target_pairs={{0,1},{1,0},{2,3},{3,2},{4,5},{5,4},{6,7},{7,6},{8,9},{9,8},{10,11... | collective-permute-start | bytes 1179656 | tf_op jit(solution)/shard_map/ppermute | solution.py:530
  138.7 2.5 %collective-permute-start.17 = (f32[384,256]{1,0:T(8,128)S(1)}, f32[384,256]{1,0:T(8,128)S(1)}, u32[]{:S(2)}, u32[]{:S(2)}) collective-permute-start(f32[384,256]{1,0:T(8,128)S(1)} %collective-permute-done.16.o_mine), channel_id=1, source_target_pairs={{0,1},{1,0},{2,3},{3,2},{4,5},{5,4},{6,7},{7,6},{8,9},{9,8},{10,11... | collective-permute-start | bytes 1179656 | tf_op jit(solution)/shard_map/ppermute | solution.py:530
  139.2 7.4 %collective-permute-start.23 = (f32[512,128]{1,0:T(8,128)S(1)}, f32[512,128]{1,0:T(8,128)S(1)}, u32[]{:S(2)}, u32[]{:S(2)}) collective-permute-start(f32[512,128]{1,0:T(8,128)S(1)} %get-tuple-element.72), channel_id=1, source_target_pairs={{16,8},{17,9},{18,10},{19,11},{20,12},{21,13},{22,14},{23,15}} | collective-permute-start | bytes 786440 | tf_op jit(solution)/shard_map/ppermute | solution.py:524
  140.5 6.1 %collective-permute-start.22 = (f32[512,128]{1,0:T(8,128)S(1)}, f32[512,128]{1,0:T(8,128)S(1)}, u32[]{:S(2)}, u32[]{:S(2)}) collective-permute-start(f32[512,128]{1,0:T(8,128)S(1)} %get-tuple-element.72), channel_id=1, source_target_pairs={{0,8},{1,9},{2,10},{3,11},{4,12},{5,13},{6,14},{7,15}} | collective-permute-start | bytes 786440 | tf_op jit(solution)/shard_map/ppermute | solution.py:524
  142.2 10.2 %collective-permute-start.21 = (f32[512,128]{1,0:T(8,128)S(1)}, f32[512,128]{1,0:T(8,128)S(1)}, u32[]{:S(2)}, u32[]{:S(2)}) collective-permute-start(f32[512,128]{1,0:T(8,128)S(1)} %get-tuple-element.69.vo), channel_id=1, source_target_pairs={{16,24},{17,25},{18,26},{19,27},{20,28},{21,29},{22,30},{23,31}} | collective-permute-start | bytes 786440 | tf_op jit(solution)/shard_map/ppermute | solution.py:524
  143.5 45.9 %collective-permute-start.20 = (f32[512,512]{1,0:T(8,128)S(1)}, f32[512,512]{1,0:T(8,128)S(1)}, u32[]{:S(2)}, u32[]{:S(2)}) collective-permute-start(f32[512,512]{1,0:T(8,128)S(1)} %get-tuple-element.68.y), channel_id=1, source_target_pairs={{16,24},{17,25},{18,26},{19,27},{20,28},{21,29},{22,30},{23,31}} | collective-permute-start | bytes 3145736 | tf_op jit(solution)/shard_map/ppermute | solution.py:524
  149.7 2.7 %collective-permute-start.24 = (f32[512,128]{1,0:T(8,128)S(1)}, f32[512,128]{1,0:T(8,128)S(1)}, u32[]{:S(2)}, u32[]{:S(2)}) collective-permute-start(f32[512,128]{1,0:T(8,128)S(1)} %get-tuple-element.73.xo), channel_id=1, source_target_pairs={{8,0},{9,1},{10,2},{11,3},{12,4},{13,5},{14,6},{15,7}} | collective-permute-start | bytes 786440 | tf_op jit(solution)/shard_map/ppermute | solution.py:524
  150.4 2.0 %collective-permute-start.26 = (f32[512,128]{1,0:T(8,128)S(1)}, f32[512,128]{1,0:T(8,128)S(1)}, u32[]{:S(2)}, u32[]{:S(2)}) collective-permute-start(f32[512,128]{1,0:T(8,128)S(1)} %get-tuple-element.74.xi), channel_id=1, source_target_pairs={{8,24},{9,25},{10,26},{11,27},{12,28},{13,29},{14,30},{15,31}} | collective-permute-start | bytes 786440 | tf_op jit(solution)/shard_map/ppermute | solution.py:524
  151.1 38.4 %collective-permute-start.25 = (f32[512,128]{1,0:T(8,128)S(1)}, f32[512,128]{1,0:T(8,128)S(1)}, u32[]{:S(2)}, u32[]{:S(2)}) collective-permute-start(f32[512,128]{1,0:T(8,128)S(1)} %get-tuple-element.74.xi), channel_id=1, source_target_pairs={{8,16},{9,17},{10,18},{11,19},{12,20},{13,21},{14,22},{15,23}} | collective-permute-start | bytes 786440 | tf_op jit(solution)/shard_map/ppermute | solution.py:524

commit v5 on v4

--- a/solution.py
+++ b/solution.py
@@ -576,6 +576,7 @@
         30 * unit_flops,
     )
     first = [(groups - 1, groups - 2)]
+    mi_half, *rhs = lax.optimization_barrier((mi_half, *rhs))
     into_o = send(mi_half, first)
     steps = []
     for t in range(middle - 1):

time: 197 us -> 196 us (level)
  transfers between devices with their start and end apart: 27 -> 27, of which waited for: 9 -> 9; matrix products, arithmetic and copies ran while one was open for 0% -> 0% of each run, Pallas kernels for 17% -> 23%
where the time goes in v5:
time: 196 us; the launch traced here: 192 us
  Pallas kernels  88.7 us (45%)
  waiting for transfers between devices  75.8 us (39%)
  starting transfers between devices  22.8 us (12%)
  local copies, waits for them, and re-layouts  4.67 us (2%)
    pallas_call x9, Pallas kernels, call(): pl.pallas_call(kernel, out_shape=[jax.ShapeDtypeStruct(s, jnp.float32) fo...  88.7 us
    ppermute x11, waiting for transfers between devices, send(): return lax.ppermute(x, 'group', pairs)  58.9 us
    ppermute x7, waiting for transfers between devices, swap(): return lax.ppermute(x, 'member', [(m, m ^ bits) for m in range(MEMBERS)])  13.8 us
    ppermute x11, starting transfers between devices, send(): return lax.ppermute(x, 'group', pairs)  11.9 us
    ppermute x7, starting transfers between devices, swap(): return lax.ppermute(x, 'member', [(m, m ^ bits) for m in range(MEMBERS)])  9.72 us
    unnamed x9, local copies, waits for them, and re-layouts  4.47 us
  transfers between devices with their start and end apart: 27, of which 9 were waited for; matrix products, arithmetic and copies ran while one was open for 0% of the time, Pallas kernels for 23%

profile of v5, /device:TPU:16, one launch (start us, length us, event | category | flops | bytes accessed | tf_op | source)
XLA Modules:
  0.0 192.4 jit_solution(5935154787913640436)
XLA Ops:
  0.9 1.0 copy-done
  3.2 1.6 collective-permute-start.1
  4.8 1.5 collective-permute-start
  6.3 8.0 %collective-permute-done.1.refs_2_ = f32[392,256]{1,0:T(8,128)S(1)} collective-permute-done((f32[392,256]{1,0:T(8,128)S(1)}, f32[392,256]{1,0:T(8,128)S(1)}, u32[]{:S(2)}, u32[]{:S(2)}) %collective-permute-start.1) | collective-permute-done | bytes 401440 | tf_op jit(solution)/shard_map/ppermute | solution.py:527
  14.3 1.6 collective-permute-start.3
  16.4 1.6 collective-permute-start.2
  18.0 2.3 %collective-permute-done.3.refs_4_ = f32[200,256]{1,0:T(8,128)S(1)} collective-permute-done((f32[200,256]{1,0:T(8,128)S(1)}, f32[200,256]{1,0:T(8,128)S(1)}, u32[]{:S(2)}, u32[]{:S(2)}) %collective-permute-start.3) | collective-permute-done | bytes 204832 | tf_op jit(solution)/shard_map/ppermute | solution.py:527
  20.3 3.5 %collective-permute-done.2.refs_3_ = f32[192,256]{1,0:T(8,128)S(1)} collective-permute-done((f32[192,256]{1,0:T(8,128)S(1)}, f32[192,256]{1,0:T(8,128)S(1)}, u32[]{:S(2)}, u32[]{:S(2)}) %collective-permute-start.2) | collective-permute-done | bytes 196640 | tf_op jit(solution)/shard_map/ppermute | solution.py:527
  23.9 1.4 collective-permute-done.7.refs_8_
  25.3 19.1 %shard_map.47 = (f32[4,520,512]{2,1,0:T(8,128)S(1)}, f32[512,512]{1,0:T(8,128)S(1)}) custom-call(s32[6]{0:T(128)S(1)} %stack.39.flags, f32[392,256]{1,0:T(8,128)S(1)} %shard_map.46.refs_0_, f32[392,256]{1,0:T(8,128)S(1)} %collective-permute-done.refs_1_, f32[392,256]{1,0:T(8,128)S(1)} %collective-permute-done.1.refs_2_, ...), custom_call_target="tpu_custom_call" | custom-call | flops 16106127360 | bytes 8519704 | tf_op jit(solution)/shard_map/pallas_call | solution.py:502
  44.4 2.0 %copy-done.3 = f32[4,520,512]{2,1,0:T(8,128)} copy-done((f32[4,520,512]{2,1,0:T(8,128)}, f32[4,520,512]{2,1,0:T(8,128)S(1)}, u32[]{:S(2)}) %copy-start.3) | copy-done | bytes 4259864
  46.5 1.5 collective-permute-start.12
  48.7 1.4 collective-permute-start.10
  50.0 31.4 %shard_map.48 = (f32[512,512]{1,0:T(8,128)S(1)}, f32[512,512]{1,0:T(8,128)S(1)}, f32[512,512]{1,0:T(8,128)S(1)}, f32[512,512]{1,0:T(8,128)S(1)}, f32[512,512]{1,...) custom-call(s32[6]{0:T(128)S(1)} %stack.39.flags, ...), custom_call_target="tpu_custom_call" | custom-call | flops 24159191040 | bytes 18284568 | tf_op jit(solution)/shard_map/pallas_call | solution.py:502
  81.5 1.3 collective-permute-start.13
  82.8 11.1 %collective-permute-done.13.mine = f32[384,256]{1,0:T(8,128)S(1)} collective-permute-done((f32[384,256]{1,0:T(8,128)S(1)}, f32[384,256]{1,0:T(8,128)S(1)}, u32[]{:S(2)}, u32[]{:S(2)}) %collective-permute-start.13) | collective-permute-done | bytes 393248 | tf_op jit(solution)/shard_map/ppermute | solution.py:524
  93.9 1.7 collective-permute-done.14.other
  95.6 20.3 %shard_map.49 = (f32[384,256]{1,0:T(8,128)S(1)}, f32[512,512]{1,0:T(8,128)S(1)}, f32[512,512]{1,0:T(8,128)S(1)}) custom-call(s32[6]{0:T(128)S(1)} %stack.39.flags, f32[512,512]{1,0:T(8,128)S(1)} %get-tuple-element.50.goi, f32[512,512]{1,0:T(8,128)S(1)} %get-tuple-element.51.gio, f32[512,512]{1,0:T(8,128)S(1)} %get-tuple-element.52.mo, ...), custom_call_target="tpu_custom_call" | custom-call | flops 16106127360 | bytes 7471128 | tf_op jit(solution)/shard_map/pallas_call | solution.py:502
  115.9 1.3 collective-permute-start.18
  118.0 8.4 %shard_map.50 = (f32[512,128]{1,0:T(8,128)S(1)}, f32[512,512]{1,0:T(8,128)S(1)}, f32[512,512]{1,0:T(8,128)S(1)}, f32[512,128]{1,0:T(8,128)S(1)}, f32[512,128]{1,0:T(8,128)S(1)}) custom-call(s32[6]{0:T(128)S(1)} %stack.39.flags, f32[512,128]{1,0:T(8,128)S(1)} %bitcast.13, f32[512,128]{1,0:T(8,128)S(1)} %collective-permute-done.10.by_x, ...), custom_call_target="tpu_custom_call" | custom-call | flops 4831838208 | bytes 13369368 | tf_op jit(solution)/shard_map/pallas_call | solution.py:502
  126.4 1.3 collective-permute-start.15
  127.7 8.9 %collective-permute-done.15.ro_in = f32[512,128]{1,0:T(8,128)S(1)} collective-permute-done((f32[512,128]{1,0:T(8,128)S(1)}, f32[512,128]{1,0:T(8,128)S(1)}, u32[]{:S(2)}, u32[]{:S(2)}) %collective-permute-start.15) | collective-permute-done | bytes 262176 | tf_op jit(solution)/shard_map/ppermute | solution.py:524
  136.6 1.0 shard_map.51
  138.3 1.3 collective-permute-start.23
  140.3 1.0 shard_map.52
  141.2 1.3 collective-permute-start.21
  142.5 1.4 collective-permute-start.20
  143.9 1.7 collective-permute-done.23.ri_in
  145.6 3.1 %shard_map.53 = (f32[512,128]{1,0:T(8,128)S(1)}, f32[512,128]{1,0:T(8,128)S(1)}) custom-call(s32[6]{0:T(128)S(1)} %stack.39.flags, f32[512,512]{1,0:T(8,128)S(1)} %get-tuple-element.77.inv_i, f32[512,512]{1,0:T(8,128)S(1)} %get-tuple-element.80.y, f32[512,512]{1,0:T(8,128)S(1)} %get-tuple-element.81.left, f32[512,128]{1,0:T(8,128)S(1)} %get-tuple-element.72.ro, ...), custom_call_target="tpu_custom_call" | custom-call | flops 16106127360 | bytes 4718616 | tf_op jit(solution)/shard_map/pallas_call | solution.py:502
  150.1 1.3 collective-permute-start.25
  151.5 37.0 %collective-permute-done.25.in_b = f32[512,128]{1,0:T(8,128)S(1)} collective-permute-done((f32[512,128]{1,0:T(8,128)S(1)}, f32[512,128]{1,0:T(8,128)S(1)}, u32[]{:S(2)}, u32[]{:S(2)}) %collective-permute-start.25) | collective-permute-done | bytes 262176 | tf_op jit(solution)/shard_map/ppermute | solution.py:524
  188.5 3.7 %shard_map.54 = f32[512,128]{1,0:T(8,128)} custom-call(s32[6]{0:T(128)S(1)} %stack.39.flags, f32[512,128]{1,0:T(8,128)S(1)} %get-tuple-element.67.w, f32[512,512]{1,0:T(8,128)S(1)} %get-tuple-element.68.ao, f32[512,512]{1,0:T(8,128)S(1)} %get-tuple-element.69.ai, f32[512,512]{1,0:T(8,128)S(1)} %get-tuple-element.78.y, f32[512,128]{1,0:T(8,128)S(1)} %get-tuple-element.79.vo, ...), custom_call_target="tpu_custom_call" | custom-call | flops 1610612736 | bytes 6553624 | tf_op jit(solution)/shard_map/pallas_call | solution.py:502
  (44 shorter events, 6.9 us)
Async XLA Ops:
  0.9 1.0 copy-start
  1.9 0.7 copy-start.1
  3.2 11.1 %collective-permute-start.1 = (f32[392,256]{1,0:T(8,128)S(1)}, f32[392,256]{1,0:T(8,128)S(1)}, u32[]{:S(2)}, u32[]{:S(2)}) collective-permute-start(f32[392,256]{1,0:T(8,128)S(1)} %shard_map.46.refs_0_), channel_id=1, source_target_pairs={{0,4},{2,6},{4,0},{6,2},{1,5},{3,7},{5,1},{7,3},{8,12},{10,14},{12... | collective-permute-start | bytes 1204232 | tf_op jit(solution)/shard_map/ppermute | solution.py:527
  4.8 11.6 %collective-permute-start = (f32[392,256]{1,0:T(8,128)S(1)}, f32[392,256]{1,0:T(8,128)S(1)}, u32[]{:S(2)}, u32[]{:S(2)}) collective-permute-start(f32[392,256]{1,0:T(8,128)S(1)} %shard_map.46.refs_0_), channel_id=1, source_target_pairs={{0,2},{2,0},{4,6},{6,4},{1,3},{3,1},{5,7},{7,5},{8,10},{10,8},{12,... | collective-permute-start | bytes 1204232 | tf_op jit(solution)/shard_map/ppermute | solution.py:527
  14.3 6.0 %collective-permute-start.3 = (f32[200,256]{1,0:T(8,128)S(1)}, f32[200,256]{1,0:T(8,128)S(1)}, u32[]{:S(2)}, u32[]{:S(2)}) collective-permute-start(f32[200,256]{1,0:T(8,128)S(1)} %slice.9), channel_id=1, source_target_pairs={{0,2},{2,0},{4,6},{6,4},{1,3},{3,1},{5,7},{7,5},{8,10},{10,8},{12,... | collective-permute-start | bytes 614408 | tf_op jit(solution)/shard_map/ppermute | solution.py:527
  15.9 8.0 %collective-permute-start.4 = (f32[392,256]{1,0:T(8,128)S(1)}, f32[392,256]{1,0:T(8,128)S(1)}, u32[]{:S(2)}, u32[]{:S(2)}) collective-permute-start(f32[392,256]{1,0:T(8,128)S(1)} %shard_map.46.refs_0_), channel_id=1, source_target_pairs={{0,1},{1,0},{2,3},{3,2},{4,5},{5,4},{6,7},{7,6},{8,9},{9,8},{10,11... | collective-permute-start | bytes 1204232 | tf_op jit(solution)/shard_map/ppermute | solution.py:530
  15.9 9.4 %collective-permute-start.6 = (f32[392,256]{1,0:T(8,128)S(1)}, f32[392,256]{1,0:T(8,128)S(1)}, u32[]{:S(2)}, u32[]{:S(2)}) collective-permute-start(f32[392,256]{1,0:T(8,128)S(1)} %collective-permute-done.1.refs_2_), channel_id=1, source_target_pairs={{0,1},{1,0},{2,3},{3,2},{4,5},{5,4},{6,7},{7,6},{8,9},{9,8},{10,11... | collective-permute-start | bytes 1204232 | tf_op jit(solution)/shard_map/ppermute | solution.py:530
  16.4 8.8 %collective-permute-start.5 = (f32[392,256]{1,0:T(8,128)S(1)}, f32[392,256]{1,0:T(8,128)S(1)}, u32[]{:S(2)}, u32[]{:S(2)}) collective-permute-start(f32[392,256]{1,0:T(8,128)S(1)} %collective-permute-done.refs_1_), channel_id=1, source_target_pairs={{0,1},{1,0},{2,3},{3,2},{4,5},{5,4},{6,7},{7,6},{8,9},{9,8},{10,11... | collective-permute-start | bytes 1204232 | tf_op jit(solution)/shard_map/ppermute | solution.py:530
  16.4 7.4 %collective-permute-start.2 = (f32[192,256]{1,0:T(8,128)S(1)}, f32[192,256]{1,0:T(8,128)S(1)}, u32[]{:S(2)}, u32[]{:S(2)}) collective-permute-start(f32[192,256]{1,0:T(8,128)S(1)} %slice.8), channel_id=1, source_target_pairs={{0,4},{2,6},{4,0},{6,2},{1,5},{3,7},{5,1},{7,3},{8,12},{10,14},{12... | collective-permute-start | bytes 589832 | tf_op jit(solution)/shard_map/ppermute | solution.py:527
  20.3 4.9 %collective-permute-start.8 = (f32[200,256]{1,0:T(8,128)S(1)}, f32[200,256]{1,0:T(8,128)S(1)}, u32[]{:S(2)}, u32[]{:S(2)}) collective-permute-start(f32[200,256]{1,0:T(8,128)S(1)} %collective-permute-done.3.refs_4_), channel_id=1, source_target_pairs={{0,1},{1,0},{2,3},{3,2},{4,5},{5,4},{6,7},{7,6},{8,9},{9,8},{10,11... | collective-permute-start | bytes 614408 | tf_op jit(solution)/shard_map/ppermute | solution.py:530
  23.8 1.4 collective-permute-start.7
  23.9 22.6 %copy-start.2 = (f32[1,512,128]{2,1,0:T(8,128)S(1)}, f32[1,512,128]{2,1,0:T(8,128)}, u32[]{:S(2)}) copy-start(f32[1,512,128]{2,1,0:T(8,128)} %param.7) | copy-start | bytes 786436
  44.4 2.0 %copy-start.3 = (f32[4,520,512]{2,1,0:T(8,128)}, f32[4,520,512]{2,1,0:T(8,128)S(1)}, u32[]{:S(2)}) copy-start(f32[4,520,512]{2,1,0:T(8,128)S(1)} %get-tuple-element.45.bonds) | copy-start | bytes 12779524
  46.4 3.6 %collective-permute-start.9 = (f32[512,512]{1,0:T(8,128)S(1)}, f32[512,512]{1,0:T(8,128)S(1)}, u32[]{:S(2)}, u32[]{:S(2)}) collective-permute-start(f32[512,512]{1,0:T(8,128)S(1)} %get-tuple-element.46.mine.p_mine), channel_id=1, source_target_pairs={{0,1},{1,0},{2,3},{3,2},{4,5},{5,4},{6,7},{7,6},{8,9},{9,8},{10,11... | collective-permute-start | bytes 3145736 | tf_op jit(solution)/shard_map/ppermute | solution.py:530
  46.5 34.9 %collective-permute-start.12 = (f32[512,128]{1,0:T(8,128)S(1)}, f32[512,128]{1,0:T(8,128)S(1)}, u32[]{:S(2)}, u32[]{:S(2)}) collective-permute-start(f32[512,128]{1,0:T(8,128)S(1)} %bitcast.10), channel_id=1, source_target_pairs={{0,6},{2,4},{4,2},{6,0},{1,7},{3,5},{5,3},{7,1},{8,14},{10,12},{12... | collective-permute-start | bytes 786440 | tf_op jit(solution)/shard_map/ppermute | solution.py:527
  48.0 33.4 %collective-permute-start.11 = (f32[512,128]{1,0:T(8,128)S(1)}, f32[512,128]{1,0:T(8,128)S(1)}, u32[]{:S(2)}, u32[]{:S(2)}) collective-permute-start(f32[512,128]{1,0:T(8,128)S(1)} %bitcast.11), channel_id=1, source_target_pairs={{0,4},{2,6},{4,0},{6,2},{1,5},{3,7},{5,1},{7,3},{8,12},{10,14},{12... | collective-permute-start | bytes 786440 | tf_op jit(solution)/shard_map/ppermute | solution.py:527
  48.7 32.8 %collective-permute-start.10 = (f32[512,128]{1,0:T(8,128)S(1)}, f32[512,128]{1,0:T(8,128)S(1)}, u32[]{:S(2)}, u32[]{:S(2)}) collective-permute-start(f32[512,128]{1,0:T(8,128)S(1)} %bitcast.12), channel_id=1, source_target_pairs={{0,2},{2,0},{4,6},{6,4},{1,3},{3,1},{5,7},{7,5},{8,10},{10,8},{12,... | collective-permute-start | bytes 786440 | tf_op jit(solution)/shard_map/ppermute | solution.py:527
  81.5 12.4 %collective-permute-start.13 = (f32[384,256]{1,0:T(8,128)S(1)}, f32[384,256]{1,0:T(8,128)S(1)}, u32[]{:S(2)}, u32[]{:S(2)}) collective-permute-start(f32[384,256]{1,0:T(8,128)S(1)} %get-tuple-element.54), channel_id=1, source_target_pairs={{24,16},{25,17},{26,18},{27,19},{28,20},{29,21},{30,22},{31,23}} | collective-permute-start | bytes 1179656 | tf_op jit(solution)/shard_map/ppermute | solution.py:524
  93.9 1.7 collective-permute-start.14
  115.9 21.7 %collective-permute-start.18 = (f32[384,256]{1,0:T(8,128)S(1)}, f32[384,256]{1,0:T(8,128)S(1)}, u32[]{:S(2)}, u32[]{:S(2)}) collective-permute-start(f32[384,256]{1,0:T(8,128)S(1)} %get-tuple-element.55), channel_id=1, source_target_pairs={{16,8},{17,9},{18,10},{19,11},{20,12},{21,13},{22,14},{23,15}} | collective-permute-start | bytes 1179656 | tf_op jit(solution)/shard_map/ppermute | solution.py:524
  117.3 20.5 %collective-permute-start.16 = (f32[384,256]{1,0:T(8,128)S(1)}, f32[384,256]{1,0:T(8,128)S(1)}, u32[]{:S(2)}, u32[]{:S(2)}) collective-permute-start(f32[384,256]{1,0:T(8,128)S(1)} %get-tuple-element.55), channel_id=1, source_target_pairs={{0,8},{1,9},{2,10},{3,11},{4,12},{5,13},{6,14},{7,15}} | collective-permute-start | bytes 1179656 | tf_op jit(solution)/shard_map/ppermute | solution.py:524
  126.4 10.2 %collective-permute-start.15 = (f32[512,128]{1,0:T(8,128)S(1)}, f32[512,128]{1,0:T(8,128)S(1)}, u32[]{:S(2)}, u32[]{:S(2)}) collective-permute-start(f32[512,128]{1,0:T(8,128)S(1)} %get-tuple-element.73.ri), channel_id=1, source_target_pairs={{24,16},{25,17},{26,18},{27,19},{28,20},{29,21},{30,22},{31,23}} | collective-permute-start | bytes 786440 | tf_op jit(solution)/shard_map/ppermute | solution.py:524
  137.7 2.6 %collective-permute-start.19 = (f32[384,256]{1,0:T(8,128)S(1)}, f32[384,256]{1,0:T(8,128)S(1)}, u32[]{:S(2)}, u32[]{:S(2)}) collective-permute-start(f32[384,256]{1,0:T(8,128)S(1)} %collective-permute-done.18.i_mine), channel_id=1, source_target_pairs={{0,1},{1,0},{2,3},{3,2},{4,5},{5,4},{6,7},{7,6},{8,9},{9,8},{10,11... | collective-permute-start | bytes 1179656 | tf_op jit(solution)/shard_map/ppermute | solution.py:530
  137.8 2.5 %collective-permute-start.17 = (f32[384,256]{1,0:T(8,128)S(1)}, f32[384,256]{1,0:T(8,128)S(1)}, u32[]{:S(2)}, u32[]{:S(2)}) collective-permute-start(f32[384,256]{1,0:T(8,128)S(1)} %collective-permute-done.16.o_mine), channel_id=1, source_target_pairs={{0,1},{1,0},{2,3},{3,2},{4,5},{5,4},{6,7},{7,6},{8,9},{9,8},{10,11... | collective-permute-start | bytes 1179656 | tf_op jit(solution)/shard_map/ppermute | solution.py:530
  138.3 7.4 %collective-permute-start.23 = (f32[512,128]{1,0:T(8,128)S(1)}, f32[512,128]{1,0:T(8,128)S(1)}, u32[]{:S(2)}, u32[]{:S(2)}) collective-permute-start(f32[512,128]{1,0:T(8,128)S(1)} %get-tuple-element.82), channel_id=1, source_target_pairs={{16,8},{17,9},{18,10},{19,11},{20,12},{21,13},{22,14},{23,15}} | collective-permute-start | bytes 786440 | tf_op jit(solution)/shard_map/ppermute | solution.py:524
  139.6 6.1 %collective-permute-start.22 = (f32[512,128]{1,0:T(8,128)S(1)}, f32[512,128]{1,0:T(8,128)S(1)}, u32[]{:S(2)}, u32[]{:S(2)}) collective-permute-start(f32[512,128]{1,0:T(8,128)S(1)} %get-tuple-element.82), channel_id=1, source_target_pairs={{0,8},{1,9},{2,10},{3,11},{4,12},{5,13},{6,14},{7,15}} | collective-permute-start | bytes 786440 | tf_op jit(solution)/shard_map/ppermute | solution.py:524
  141.2 10.2 %collective-permute-start.21 = (f32[512,128]{1,0:T(8,128)S(1)}, f32[512,128]{1,0:T(8,128)S(1)}, u32[]{:S(2)}, u32[]{:S(2)}) collective-permute-start(f32[512,128]{1,0:T(8,128)S(1)} %get-tuple-element.79.vo), channel_id=1, source_target_pairs={{16,24},{17,25},{18,26},{19,27},{20,28},{21,29},{22,30},{23,31}} | collective-permute-start | bytes 786440 | tf_op jit(solution)/shard_map/ppermute | solution.py:524
  142.5 46.0 %collective-permute-start.20 = (f32[512,512]{1,0:T(8,128)S(1)}, f32[512,512]{1,0:T(8,128)S(1)}, u32[]{:S(2)}, u32[]{:S(2)}) collective-permute-start(f32[512,512]{1,0:T(8,128)S(1)} %get-tuple-element.78.y), channel_id=1, source_target_pairs={{16,24},{17,25},{18,26},{19,27},{20,28},{21,29},{22,30},{23,31}} | collective-permute-start | bytes 3145736 | tf_op jit(solution)/shard_map/ppermute | solution.py:524
  148.8 2.7 %collective-permute-start.24 = (f32[512,128]{1,0:T(8,128)S(1)}, f32[512,128]{1,0:T(8,128)S(1)}, u32[]{:S(2)}, u32[]{:S(2)}) collective-permute-start(f32[512,128]{1,0:T(8,128)S(1)} %get-tuple-element.83.xo), channel_id=1, source_target_pairs={{8,0},{9,1},{10,2},{11,3},{12,4},{13,5},{14,6},{15,7}} | collective-permute-start | bytes 786440 | tf_op jit(solution)/shard_map/ppermute | solution.py:524
  149.4 2.0 %collective-permute-start.26 = (f32[512,128]{1,0:T(8,128)S(1)}, f32[512,128]{1,0:T(8,128)S(1)}, u32[]{:S(2)}, u32[]{:S(2)}) collective-permute-start(f32[512,128]{1,0:T(8,128)S(1)} %get-tuple-element.84.xi), channel_id=1, source_target_pairs={{8,24},{9,25},{10,26},{11,27},{12,28},{13,29},{14,30},{15,31}} | collective-permute-start | bytes 786440 | tf_op jit(solution)/shard_map/ppermute | solution.py:524
  150.1 38.4 %collective-permute-start.25 = (f32[512,128]{1,0:T(8,128)S(1)}, f32[512,128]{1,0:T(8,128)S(1)}, u32[]{:S(2)}, u32[]{:S(2)}) collective-permute-start(f32[512,128]{1,0:T(8,128)S(1)} %get-tuple-element.84.xi), channel_id=1, source_target_pairs={{8,16},{9,17},{10,18},{11,19},{12,20},{13,21},{14,22},{15,23}} | collective-permute-start | bytes 786440 | tf_op jit(solution)/shard_map/ppermute | solution.py:524
